TPU v7x, 32 devices: a whole 2x2x4 slice. The times are simulated.
32 devices in a mesh: blk: 8 (over z, y), grp: 4 (over x, core).
Axes of the slice: x: 2, y: 2, z: 4, core: 2. Of those that a mesh axis runs over, the one named last changes fastest.
Arguments:
- inputs: bfloat16 [4, 1024, 1024], P('grp', 'blk'), may hold values from -6 to 6
- skipped: bfloat16 [4, 1024, 1024], P('grp', 'blk'), may hold values from -6 to 6
- w_skip: bfloat16 [2048, 1024], P('grp'), may hold values from -0.125 to 0.125
- w_mod: bfloat16 [1024, 2048], P('grp'), may hold values from -0.1875 to 0.1875
- w_qkv: bfloat16 [1024, 3072], P('grp'), may hold values from -0.1875 to 0.1875
- w_out: bfloat16 [1024, 1024], P('grp'), may hold values from -12 to 12
- ff_gain: bfloat16 [1024], P('grp'), may hold values from 0.099609375 to 1.8984375
- w_up: bfloat16 [1024, 4096], P('grp'), may hold values from -0.1875 to 0.1875
- w_down: bfloat16 [4096, 1024], P('grp'), may hold values from -0.09375 to 0.09375
- cotangent: bfloat16 [4, 1024, 1024], P('grp', 'blk'), may hold values from -6 to 6
- lengths: int32 [4, 8], P('grp'), may hold values from 1 to 960, 1024 in all within a row
- flow_steps: int32 [4, 8], P('grp'), may hold values from 0 to 31
Outputs:
- output: bfloat16 [4, 1024, 1024], P('grp', 'blk')
- grad_inputs: float32 [4, 1024, 1024], P('grp', 'blk')
- grad_skipped: float32 [4, 1024, 1024], P('grp', 'blk')
- grad_w_skip: float32 [2048, 1024], P('grp')
- grad_w_mod: float32 [1024, 2048], P('grp')
- grad_w_qkv: float32 [1024, 3072], P('grp')
- grad_w_out: float32 [1024, 1024], P('grp')
- grad_ff_gain: float32 [1024], P('grp')
- grad_w_up: float32 [1024, 4096], P('grp')
- grad_w_down: float32 [4096, 1024], P('grp')
Inputs may be any that keep to these rules, and one draw needn't show every extreme that they name: Each row's lengths sum to 1024; the longest utterance of a row has exactly 960 frames.
All inputs are finite; a program needn't handle non-finite values.
Results may differ from a plain program's by a relative error of at most 0.018.
Values may be sent and summed in bfloat16 or wider, within the bound.
A program may use at most 192 MiB of HBM per device.

v0:
```python
import math

import jax
import jax.numpy as jnp
from jax import lax
from jax.sharding import PartitionSpec as P

HEADS = 16
HEAD_DIM = 64
STEPS = 32


EPSILON = 1e-06
NEGATIVE = -1e30
HIGHEST = lax.Precision.HIGHEST


def from_behind(block, axis, distance):
    devices = range(lax.axis_size(axis))
    route = [((i - distance) % len(devices), i) for i in devices]
    return lax.ppermute(block, axis, route)


def layout(lengths_row, frames):
    end_frame = jnp.cumsum(lengths_row)
    start_frame = end_frame - lengths_row
    segment = jnp.sum((frames[:, None] >= end_frame[None, :]).astype(jnp.int32), axis=1)
    chosen = segment[:, None] == jnp.arange(lengths_row.shape[0], dtype=jnp.int32)[None, :]
    position = frames - jnp.sum(jnp.where(chosen, start_frame[None, :], 0), axis=1)
    return (segment, position)


def flow_condition(steps_row, model_width):
    half_width = model_width // 2
    rate_table = jnp.exp(
        -math.log(10000.0) * jnp.arange(half_width, dtype=jnp.float32) / half_width
    )
    angles = 1000.0 * (steps_row.astype(jnp.float32) / STEPS)[:, None] * rate_table[None, :]
    return jax.nn.silu(jnp.concatenate([jnp.sin(angles), jnp.cos(angles)], axis=1))


def rotation_tables(position, head_width):
    half_width = head_width // 2
    rate_table = jnp.exp(
        -math.log(10000.0) * jnp.arange(half_width, dtype=jnp.float32) / half_width
    )
    angles = position.astype(jnp.float32)[:, None] * rate_table[None, :]
    return (jnp.cos(angles)[:, None, :], jnp.sin(angles)[:, None, :], half_width)


def rotate(head_block, position):
    cosine_part, sine_part, half_width = rotation_tables(position, head_block.shape[-1])
    first_half = head_block[..., :half_width]
    second_half = head_block[..., half_width:]
    return jnp.concatenate(
        [
            first_half * cosine_part - second_half * sine_part,
            second_half * cosine_part + first_half * sine_part,
        ],
        axis=-1,
    )


def rotate_back(head_block, position):
    cosine_part, sine_part, half_width = rotation_tables(position, head_block.shape[-1])
    first_half = head_block[..., :half_width]
    second_half = head_block[..., half_width:]
    return jnp.concatenate(
        [
            first_half * cosine_part + second_half * sine_part,
            second_half * cosine_part - first_half * sine_part,
        ],
        axis=-1,
    )


def normalize(hidden):
    centred = hidden - jnp.mean(hidden, axis=-1, keepdims=True)
    scaled = lax.rsqrt(jnp.mean(centred * centred, axis=-1, keepdims=True) + EPSILON)
    return (centred * scaled, scaled)


def norm_back(grad_normal, normal, scaled):
    centred_grad = grad_normal - jnp.mean(grad_normal, axis=-1, keepdims=True)
    return scaled * (centred_grad - normal * jnp.mean(grad_normal * normal, axis=-1, keepdims=True))


def exact_gelu(values_in):
    return jax.nn.gelu(values_in, approximate=False)


def contract_rows(left_side, right_side):
    return lax.dot_general(
        left_side, right_side, (((0,), (0,)), ((), ())), preferred_element_type=jnp.float32
    )


def heads_of(flat_block):
    return flat_block.reshape(flat_block.shape[0], HEADS, HEAD_DIM)


def per_device(
    inputs,
    skipped,
    w_skip,
    w_mod,
    w_qkv,
    w_out,
    ff_gain,
    w_up,
    w_down,
    cotangent,
    lengths,
    flow_steps,
):
    w_skip, w_mod, w_qkv, w_out, ff_gain, w_up, w_down = (
        lax.all_gather(w_skip, "grp", axis=0, tiled=True),
        lax.all_gather(w_mod, "grp", axis=0, tiled=True),
        lax.all_gather(w_qkv, "grp", axis=0, tiled=True),
        lax.all_gather(w_out, "grp", axis=0, tiled=True),
        lax.all_gather(ff_gain, "grp", axis=0, tiled=True),
        lax.all_gather(w_up, "grp", axis=0, tiled=True),
        lax.all_gather(w_down, "grp", axis=0, tiled=True),
    )
    frame_count = inputs.shape[1]
    model_width = inputs.shape[2]
    cycle_size = lax.axis_size("blk")
    device_rank = lax.axis_index("blk")
    score_scale = HEAD_DIM ** (-0.5)
    local_frames = jnp.arange(frame_count, dtype=jnp.int32)
    lengths_row = lengths[0]
    own_segment, own_position = layout(lengths_row, device_rank * frame_count + local_frames)

    def segment_of(source):
        return layout(lengths_row, source * frame_count + local_frames)[0]

    def scored(query_block, key_block, query_segment, key_segment):
        raw_scores = (
            jnp.einsum(
                "qhd,khd->hqk",
                heads_of(query_block),
                heads_of(key_block),
                preferred_element_type=jnp.float32,
            )
            * score_scale
        )
        allowed = (query_segment[:, None] == key_segment[None, :])[None]
        return (raw_scores, allowed)

    joined = jnp.concatenate([inputs[0], skipped[0]], axis=1)
    hidden = jnp.dot(joined, w_skip, preferred_element_type=jnp.float32)
    condition = flow_condition(flow_steps[0], model_width).astype(jnp.bfloat16)
    modulation = jnp.dot(condition, w_mod, preferred_element_type=jnp.float32)
    picker = (
        own_segment[:, None] == jnp.arange(lengths_row.shape[0], dtype=jnp.int32)[None, :]
    ).astype(jnp.float32)
    per_frame = jnp.dot(picker, modulation, precision=HIGHEST)
    scale_one = 1.0 + per_frame[:, :model_width]
    normal_one, spread_one = normalize(hidden)
    attn_in = (normal_one * scale_one + per_frame[:, model_width:]).astype(jnp.bfloat16)
    project = jnp.dot(attn_in, w_qkv, preferred_element_type=jnp.float32).reshape(
        frame_count, 3, HEADS, HEAD_DIM
    )
    queries = (
        rotate(project[:, 0], own_position).astype(jnp.bfloat16).reshape(frame_count, model_width)
    )
    keys_own = (
        rotate(project[:, 1], own_position).astype(jnp.bfloat16).reshape(frame_count, model_width)
    )
    values_own = project[:, 2].astype(jnp.bfloat16).reshape(frame_count, model_width)

    def forward_turn(turn_index, carried):
        key_now, value_now, running_top, running_total, running_sum = carried
        source = (device_rank - turn_index) % cycle_size
        raw_scores, allowed = scored(queries, key_now, own_segment, segment_of(source))
        raw_scores = jnp.where(allowed, raw_scores, NEGATIVE)
        new_top = jnp.maximum(running_top, jnp.max(raw_scores, axis=2, keepdims=True))
        weights = jnp.where(allowed, jnp.exp(raw_scores - new_top), 0.0)
        shrink = jnp.exp(running_top - new_top)
        running_total = running_total * shrink + jnp.sum(weights, axis=2, keepdims=True)
        running_sum = running_sum * shrink + jnp.einsum(
            "hqk,khd->hqd",
            weights.astype(jnp.bfloat16),
            heads_of(value_now),
            preferred_element_type=jnp.float32,
        )
        key_now, value_now = from_behind((key_now, value_now), "blk", 1)
        return (key_now, value_now, new_top, running_total, running_sum)

    initial = (
        keys_own,
        values_own,
        jnp.full((HEADS, frame_count, 1), NEGATIVE, jnp.float32),
        jnp.zeros((HEADS, frame_count, 1), jnp.float32),
        jnp.zeros((HEADS, frame_count, HEAD_DIM), jnp.float32),
    )
    finished = lax.fori_loop(0, cycle_size, forward_turn, initial)
    running_top, running_total, running_sum = (finished[2], finished[3], finished[4])
    attended = jnp.transpose(running_sum / running_total, (1, 0, 2)).reshape(
        frame_count, model_width
    )
    log_total = (running_top + jnp.log(running_total))[:, :, 0]
    attended_low = attended.astype(jnp.bfloat16)
    hidden_two = hidden + jnp.dot(attended_low, w_out, preferred_element_type=jnp.float32)
    normal_two, spread_two = normalize(hidden_two)
    gain_vector = ff_gain.astype(jnp.float32)
    ff_in = (normal_two * gain_vector).astype(jnp.bfloat16)
    widened = jnp.dot(ff_in, w_up, preferred_element_type=jnp.float32)
    activated, gelu_back = jax.vjp(exact_gelu, widened)
    activated_low = activated.astype(jnp.bfloat16)
    output = (
        hidden_two + jnp.dot(activated_low, w_down, preferred_element_type=jnp.float32)
    ).astype(jnp.bfloat16)
    upstream = cotangent[0]
    grad_down = contract_rows(activated_low, upstream)
    grad_activated = jnp.dot(upstream, w_down.T, preferred_element_type=jnp.float32)
    grad_widened = gelu_back(grad_activated)[0].astype(jnp.bfloat16)
    grad_up = contract_rows(ff_in, grad_widened)
    grad_ff_in = jnp.dot(grad_widened, w_up.T, preferred_element_type=jnp.float32)
    grad_gain = jnp.sum(grad_ff_in * normal_two, axis=0)
    grad_hidden_two = upstream.astype(jnp.float32) + norm_back(
        grad_ff_in * gain_vector, normal_two, spread_two
    )
    grad_two_low = grad_hidden_two.astype(jnp.bfloat16)
    grad_out = contract_rows(attended_low, grad_two_low)
    grad_attended = jnp.dot(grad_two_low, w_out.T, preferred_element_type=jnp.float32).astype(
        jnp.bfloat16
    )
    delta = jnp.transpose(jnp.sum(heads_of(grad_attended.astype(jnp.float32) * attended), axis=2))
    zero_grad = jnp.zeros((frame_count, model_width), jnp.float32)

    def pair_terms(
        query_block,
        upstream_block,
        key_block,
        value_block,
        total_block,
        delta_block,
        query_segment,
        key_segment,
    ):
        raw_scores, allowed = scored(query_block, key_block, query_segment, key_segment)
        prob_block = jnp.where(allowed, jnp.exp(raw_scores - total_block[:, :, None]), 0.0)
        value_term = jnp.einsum(
            "hqk,qhd->khd",
            prob_block.astype(jnp.bfloat16),
            heads_of(upstream_block),
            preferred_element_type=jnp.float32,
        ).reshape(frame_count, model_width)
        prob_grad = jnp.einsum(
            "qhd,khd->hqk",
            heads_of(upstream_block),
            heads_of(value_block),
            preferred_element_type=jnp.float32,
        )
        score_grad = (prob_block * (prob_grad - delta_block[:, :, None])).astype(jnp.bfloat16)
        query_term = (
            jnp.einsum(
                "hqk,khd->qhd", score_grad, heads_of(key_block), preferred_element_type=jnp.float32
            ).reshape(frame_count, model_width)
            * score_scale
        )
        key_term = (
            jnp.einsum(
                "hqk,qhd->khd",
                score_grad,
                heads_of(query_block),
                preferred_element_type=jnp.float32,
            ).reshape(frame_count, model_width)
            * score_scale
        )
        return (query_term, key_term, value_term)

    def keys_turn(turn_index, carried):
        key_now, value_now, key_grad, value_grad, query_grad = carried
        source = (device_rank - turn_index) % cycle_size
        query_term, key_term, value_term = pair_terms(
            queries,
            grad_attended,
            key_now,
            value_now,
            log_total,
            delta,
            own_segment,
            segment_of(source),
        )
        key_now, value_now = from_behind((key_now, value_now), "blk", 1)
        key_grad, value_grad = (
            from_behind((key_grad + key_term).astype(jnp.bfloat16), "blk", 1).astype(jnp.float32),
            from_behind((value_grad + value_term).astype(jnp.bfloat16), "blk", 1).astype(
                jnp.float32
            ),
        )
        return (key_now, value_now, key_grad, value_grad, query_grad + query_term)

    done = lax.fori_loop(
        0, cycle_size, keys_turn, (keys_own, values_own, zero_grad, zero_grad, zero_grad)
    )
    key_grad, value_grad, query_grad = (done[2], done[3], done[4])
    grad_project = jnp.concatenate(
        [
            rotate_back(heads_of(query_grad), own_position).reshape(frame_count, model_width),
            rotate_back(heads_of(key_grad), own_position).reshape(frame_count, model_width),
            value_grad,
        ],
        axis=1,
    ).astype(jnp.bfloat16)
    grad_qkv = contract_rows(attn_in, grad_project)
    grad_attn_in = jnp.dot(grad_project, w_qkv.T, preferred_element_type=jnp.float32)
    mod_terms = jnp.concatenate([grad_attn_in * normal_one, grad_attn_in], axis=1)
    grad_modulation = jnp.dot(picker.T, mod_terms, precision=HIGHEST)
    grad_mod = jnp.dot(condition.astype(jnp.float32).T, grad_modulation, precision=HIGHEST)
    grad_hidden = grad_hidden_two + norm_back(grad_attn_in * scale_one, normal_one, spread_one)
    grad_hidden_low = grad_hidden.astype(jnp.bfloat16)
    grad_skip_weight = contract_rows(joined, grad_hidden_low)
    grad_joined = jnp.dot(grad_hidden_low, w_skip.T, preferred_element_type=jnp.float32)
    shards = (
        lax.psum_scatter(
            grad_skip_weight.astype(jnp.bfloat16), "grp", scatter_dimension=0, tiled=True
        ).astype(jnp.float32),
        lax.psum_scatter(
            grad_mod.astype(jnp.bfloat16), "grp", scatter_dimension=0, tiled=True
        ).astype(jnp.float32),
        lax.psum_scatter(
            grad_qkv.astype(jnp.bfloat16), "grp", scatter_dimension=0, tiled=True
        ).astype(jnp.float32),
        lax.psum_scatter(
            grad_out.astype(jnp.bfloat16), "grp", scatter_dimension=0, tiled=True
        ).astype(jnp.float32),
        lax.psum_scatter(
            grad_gain.astype(jnp.bfloat16), "grp", scatter_dimension=0, tiled=True
        ).astype(jnp.float32),
        lax.psum_scatter(
            grad_up.astype(jnp.bfloat16), "grp", scatter_dimension=0, tiled=True
        ).astype(jnp.float32),
        lax.psum_scatter(
            grad_down.astype(jnp.bfloat16), "grp", scatter_dimension=0, tiled=True
        ).astype(jnp.float32),
    )
    totals = lax.psum(
        (shards[0], shards[1], shards[2], shards[3], shards[4], shards[5], shards[6]), "blk"
    )
    return (
        output[None],
        grad_joined[:, :model_width][None],
        grad_joined[:, model_width:][None],
        totals[0],
        totals[1],
        totals[2],
        totals[3],
        totals[4],
        totals[5],
        totals[6],
    )


def solution(mesh):
    placed = (
        P("grp", "blk", None),
        P("grp", "blk", None),
        P("grp", None),
        P("grp", None),
        P("grp", None),
        P("grp", None),
        P("grp"),
        P("grp", None),
        P("grp", None),
        P("grp", "blk", None),
        P("grp", None),
        P("grp", None),
    )
    return jax.shard_map(
        per_device,
        mesh=mesh,
        in_specs=placed,
        out_specs=(
            P("grp", "blk", None),
            P("grp", "blk", None),
            P("grp", "blk", None),
            P("grp", None),
            P("grp", None),
            P("grp", None),
            P("grp", None),
            P("grp"),
            P("grp", None),
            P("grp", None),
        ),
        check_vma=False,
    )
```

profile of v0, /device:TPU:0, one launch (start us, length us, event | category | flops | bytes accessed | tf_op | source)
XLA Modules:
  0.0 1476.5 jit_solution(8510525605521068427)
XLA Ops:
  11.9 6.0 all-gather
  18.2 28.6 %all-gather.8.cloned.1.call-done = bf16[2048,1024]{1,0:T(8,128)(2,1)} async-done(((bf16[512,1024]{1,0:T(8,128)(2,1)}), bf16[2048,1024]{1,0:T(8,128)(2,1)}) %all-gather.8.cloned.1.call-update) | async-done | bytes 4194320 | tf_op jit(solution)/shard_map/all_gather | solution.py:117
  46.8 3.0 fusion.61
  50.0 32.9 %all-gather.10.cloned.1.call-done = bf16[1024,2048]{1,0:T(8,128)(2,1)} async-done(((bf16[256,2048]{1,0:T(8,128)(2,1)}), bf16[1024,2048]{1,0:T(8,128)(2,1)}) %all-gather.10.cloned.1.call-update) | async-done | bytes 4194320 | tf_op jit(solution)/shard_map/all_gather | solution.py:118
  82.9 2.8 fusion.57
  87.5 43.4 %all-gather.12.cloned.1.call-done = bf16[1024,3072]{1,0:T(8,128)(2,1)} async-done(((bf16[256,3072]{1,0:T(8,128)(2,1)}), bf16[1024,3072]{1,0:T(8,128)(2,1)}) %all-gather.12.cloned.1.call-update) | async-done | bytes 6291472 | tf_op jit(solution)/shard_map/all_gather | solution.py:119
  130.8 5.4 fusion.63
  139.7 119.8 %while.48 = (s32[]{:T(128)}, bf16[128,1024]{0,1:T(8,128)(2,1)}, bf16[128,1024]{0,1:T(8,128)(2,1)}, f32[16,128,1]{1,0,2:T(8,128)S(1)}, f32[16,128,1]{1,0,2:T(8,12...) while((s32[]{:T(128)}, bf16[128,1024]{0,1:T(8,128)(2,1)}, ...), condition=%wide.region_10.11_spmd.clone, body=%wide.region_6.10_spmd.clone.sunk | while | flops 69893136 | bytes 8326034 | solution.py:197
  145.9 6.9 collective-permute-done
  152.8 5.0 collective-permute-done.1
  162.0 8.8 collective-permute-done
  170.8 4.0 collective-permute-done.1
  177.8 10.0 collective-permute-done
  187.8 3.1 collective-permute-done.1
  194.0 9.4 collective-permute-done
  203.3 2.8 collective-permute-done.1
  209.1 8.4 collective-permute-done
  217.6 2.8 collective-permute-done.1
  223.4 7.5 collective-permute-done
  230.9 2.8 collective-permute-done.1
  236.7 7.1 collective-permute-done
  243.8 2.8 collective-permute-done.1
  249.7 7.1 collective-permute-done
  256.8 2.8 collective-permute-done.1
  260.6 2.1 fusion.62
  263.0 9.1 multiply_convert_fusion
  272.1 2.2 all-gather.18.cloned.1.call-done
  274.4 10.0 add_convert_fusion
  284.4 3.0 multiply_reduce_fusion
  287.8 2.0 convolution_convert_fusion.5
  289.8 3.2 convert_multiply_fusion
  296.3 215.7 %while.49 = (s32[]{:T(128)}, bf16[128,1024]{0,1:T(8,128)(2,1)}, bf16[128,1024]{0,1:T(8,128)(2,1)S(1)}, f32[128,1024]{0,1:T(8,128)S(1)}, f32[128,1024]{0,1:T(8,12...) while((s32[]{:T(128)}, bf16[128,1024]{0,1:T(8,128)(2,1)}, ...), condition=%wide.region_18.19_spmd.clone, body=%wide.region_16.18_spmd.clone.sunk | while | flops 171199504 | bytes 19188728 | solution.py:296
  307.1 13.3 collective-permute-done.4
  321.4 4.0 collective-permute-done.5
  332.5 2.4 collective-permute-start.5
  335.4 15.2 %collective-permute-done.4 = bf16[128,1024]{0,1:T(8,128)(2,1)} collective-permute-done((bf16[128,1024]{0,1:T(8,128)(2,1)}, bf16[128,1024]{0,1:T(8,128)(2,1)}, u32[]{:S(2)}, u32[]{:S(2)}) %collective-permute-start.4) | collective-permute-done | bytes 262176 | tf_op jit(solution)/shard_map/while/body/eval_jaxpr/ppermute | solution.py:21
  351.6 3.0 collective-permute-done.5
  360.1 2.3 collective-permute-start.5
  362.9 17.0 %collective-permute-done.4 = bf16[128,1024]{0,1:T(8,128)(2,1)} collective-permute-done((bf16[128,1024]{0,1:T(8,128)(2,1)}, bf16[128,1024]{0,1:T(8,128)(2,1)}, u32[]{:S(2)}, u32[]{:S(2)}) %collective-permute-start.4) | collective-permute-done | bytes 262176 | tf_op jit(solution)/shard_map/while/body/eval_jaxpr/ppermute | solution.py:21
  380.9 2.1 collective-permute-done.5
  389.5 18.2 %collective-permute-done.4 = bf16[128,1024]{0,1:T(8,128)(2,1)} collective-permute-done((bf16[128,1024]{0,1:T(8,128)(2,1)}, bf16[128,1024]{0,1:T(8,128)(2,1)}, u32[]{:S(2)}, u32[]{:S(2)}) %collective-permute-start.4) | collective-permute-done | bytes 262176 | tf_op jit(solution)/shard_map/while/body/eval_jaxpr/ppermute | solution.py:21
  408.7 1.8 collective-permute-done.5
  416.5 17.7 %collective-permute-done.4 = bf16[128,1024]{0,1:T(8,128)(2,1)} collective-permute-done((bf16[128,1024]{0,1:T(8,128)(2,1)}, bf16[128,1024]{0,1:T(8,128)(2,1)}, u32[]{:S(2)}, u32[]{:S(2)}) %collective-permute-start.4) | collective-permute-done | bytes 262176 | tf_op jit(solution)/shard_map/while/body/eval_jaxpr/ppermute | solution.py:21
  435.2 1.8 collective-permute-done.5
  443.0 16.8 %collective-permute-done.4 = bf16[128,1024]{0,1:T(8,128)(2,1)} collective-permute-done((bf16[128,1024]{0,1:T(8,128)(2,1)}, bf16[128,1024]{0,1:T(8,128)(2,1)}, u32[]{:S(2)}, u32[]{:S(2)}) %collective-permute-start.4) | collective-permute-done | bytes 262176 | tf_op jit(solution)/shard_map/while/body/eval_jaxpr/ppermute | solution.py:21
  460.8 1.8 collective-permute-done.5
  468.6 15.9 %collective-permute-done.4 = bf16[128,1024]{0,1:T(8,128)(2,1)} collective-permute-done((bf16[128,1024]{0,1:T(8,128)(2,1)}, bf16[128,1024]{0,1:T(8,128)(2,1)}, u32[]{:S(2)}, u32[]{:S(2)}) %collective-permute-start.4) | collective-permute-done | bytes 262176 | tf_op jit(solution)/shard_map/while/body/eval_jaxpr/ppermute | solution.py:21
  485.5 1.8 collective-permute-done.5
  493.3 14.8 %collective-permute-done.4 = bf16[128,1024]{0,1:T(8,128)(2,1)} collective-permute-done((bf16[128,1024]{0,1:T(8,128)(2,1)}, bf16[128,1024]{0,1:T(8,128)(2,1)}, u32[]{:S(2)}, u32[]{:S(2)}) %collective-permute-start.4) | collective-permute-done | bytes 262176 | tf_op jit(solution)/shard_map/while/body/eval_jaxpr/ppermute | solution.py:21
  509.1 1.8 collective-permute-done.5
  513.3 5.2 fusion.58
  519.3 5.0 convolution_convert_fusion.3
  525.3 3.3 convolution_convert_fusion.4
  529.7 4.5 convolution_convert_fusion.2
  535.4 5.9 convolution_convert_fusion.1
  542.6 5.6 convolution_convert_fusion
  550.1 6.2 all-reduce
  556.4 3.7 fusion.64
  561.2 5.3 fusion.29
  566.5 46.6 %reduce-scatter.7.cloned.1.call-done = bf16[512,1024]{1,0:T(8,128)(2,1)} async-done(((bf16[2048,1024]{1,0:T(8,128)(2,1)}), bf16[512,1024]{1,0:T(8,128)(2,1)}) %reduce-scatter.7.cloned.1.call-update) | async-done | bytes 1048592 | tf_op jit(solution)/shard_map/reduce_scatter | solution.py:318
  613.1 61.0 %reduce-scatter.11.cloned.1.call-done = bf16[256,3072]{1,0:T(8,128)(2,1)} async-done(((bf16[1024,3072]{1,0:T(8,128)(2,1)}), bf16[256,3072]{1,0:T(8,128)(2,1)}) %reduce-scatter.11.cloned.1.call-update) | async-done | bytes 1572880 | tf_op jit(solution)/shard_map/reduce_scatter | solution.py:324
  674.1 74.3 %reduce-scatter.15.cloned.1.call-done = bf16[256,4096]{1,0:T(8,128)(2,1)} async-done(((bf16[1024,4096]{1,0:T(8,128)(2,1)}), bf16[256,4096]{1,0:T(8,128)(2,1)}) %reduce-scatter.15.cloned.1.call-update) | async-done | bytes 2097168 | tf_op jit(solution)/shard_map/reduce_scatter | solution.py:333
  748.4 74.4 %reduce-scatter.17.cloned.1.call-done = bf16[1024,1024]{1,0:T(8,128)(2,1)} async-done(((bf16[4096,1024]{1,0:T(8,128)(2,1)}), bf16[1024,1024]{1,0:T(8,128)(2,1)}) %reduce-scatter.17.cloned.1.call-update) | async-done | bytes 2097168 | tf_op jit(solution)/shard_map/reduce_scatter | solution.py:336
  822.8 646.4 %all-reduce.3 = (f32[512,1024]{1,0:T(8,128)}, f32[256,2048]{1,0:T(8,128)}, f32[256,3072]{1,0:T(8,128)}, f32[256,1024]{1,0:T(8,128)}, f32[256]{0:T(256)}, /*index=5*/f32[256,4096]{1,0:T(8,128)}, f32[1024,1024]{1,0:T(8,128)}) all-reduce(bf16[512,1024]{1,0:T(8,128)(2,1)} %reduce-scatter.7.cloned.1.call-don, ...), channel_id=1, replica_groups=mesh['blk'=8,'grp'=4] {'blk'}, use_global_device_ids=true, to_apply=%region_22.23 | all-reduce | flops 4194560 | bytes 25167872 | tf_op jit(solution)/shard_map/psum | solution.py:340
  (402 shorter events, 115.1 us)
Async XLA Ops:
  7.2 39.6 %all-gather.8.cloned.1.call-start = ((), (), s32[]{:S(2)}) async-start(), calls=%async_computation.6 | async-start | bytes 5242880 | tf_op jit(solution)/shard_map/all_gather | solution.py:117
  7.9 74.9 %all-gather.10.cloned.1.call-start = ((), (), s32[]{:S(2)}) async-start(), calls=%async_computation.7 | async-start | bytes 5242880 | tf_op jit(solution)/shard_map/all_gather | solution.py:118
  8.7 122.2 %all-gather.12.cloned.1.call-start = ((), (), s32[]{:S(2)}) async-start(), calls=%async_computation.8 | async-start | bytes 7864320 | tf_op jit(solution)/shard_map/all_gather | solution.py:119
  9.4 251.2 %all-gather.14.cloned.1.call-start = ((), (), s32[]{:S(2)}) async-start(), calls=%async_computation.9 | async-start | bytes 2621440 | tf_op jit(solution)/shard_map/all_gather | solution.py:120
  10.0 36.8 %copy-start.14 = (bf16[1,128,1024]{2,1,0:T(8,128)(2,1)S(1)}, bf16[1,128,1024]{2,1,0:T(8,128)(2,1)}, u32[]{:S(2)}) copy-start(bf16[1,128,1024]{2,1,0:T(8,128)(2,1)} %param.17) | copy-start | bytes 786436
  10.0 36.8 %copy-start.16 = (bf16[1,128,1024]{2,1,0:T(8,128)(2,1)S(1)}, bf16[1,128,1024]{2,1,0:T(8,128)(2,1)}, u32[]{:S(2)}) copy-start(bf16[1,128,1024]{2,1,0:T(8,128)(2,1)} %param.16) | copy-start | bytes 786436
  10.0 253.0 %all-gather.16.cloned.1.call-start = ((), (), s32[]{:S(2)}) async-start(), calls=%async_computation.10 | async-start | bytes 10485760 | tf_op jit(solution)/shard_map/all_gather | solution.py:122
  10.6 263.8 %all-gather.18.cloned.1.call-start = ((), (), s32[]{:S(2)}) async-start(), calls=%async_computation.11 | async-start | bytes 10485760 | tf_op jit(solution)/shard_map/all_gather | solution.py:123
  11.2 555.3 %reduce-scatter.13.cloned.1.call-start = ((), (), s32[]{:S(2)}) async-start(), calls=%async_computation.15 | async-start | bytes 2621440 | tf_op jit(solution)/shard_map/reduce_scatter | solution.py:327
  49.8 210.9 %copy-start = (f32[128,1024]{1,0:T(8,128)}, f32[128,1024]{1,0:T(8,128)S(1)}, u32[]{:S(2)}) copy-start(f32[128,1024]{1,0:T(8,128)S(1)} %get-tuple-element.836) | copy-start | bytes 1572868
  87.5 48.8 %copy-start.12 = (bf16[128,1024]{1,0:T(8,128)(2,1)}, bf16[128,1024]{1,0:T(8,128)(2,1)S(1)}, u32[]{:S(2)}) copy-start(bf16[128,1024]{1,0:T(8,128)(2,1)S(1)} %fusion.34) | copy-start | bytes 786436
  140.9 11.9 collective-permute-start
  143.4 14.4 collective-permute-start.1
  158.7 12.0 collective-permute-start
  159.7 15.1 %collective-permute-start.1 = (bf16[128,1024]{0,1:T(8,128)(2,1)S(1)}, bf16[128,1024]{0,1:T(8,128)(2,1)}, u32[]{:S(2)}, u32[]{:S(2)}) collective-permute-start(bf16[128,1024]{0,1:T(8,128)(2,1)S(1)} %copy.53), channel_id=1, source_target_pairs={{28,0},{0,4},{4,8},{8,12},{12,16},{16,20},{20,24},{24,28},{29,1},{... | collective-permute-start | bytes 786440 | tf_op jit(solution)/shard_map/while/body/eval_jaxpr/ppermute | solution.py:21
  175.8 12.0 collective-permute-start
  176.7 14.2 collective-permute-start.1
  191.9 11.4 collective-permute-start
  192.8 13.3 collective-permute-start.1
  207.1 10.5 collective-permute-start
  208.0 12.3 collective-permute-start.1
  221.3 9.6 collective-permute-start
  222.3 11.4 collective-permute-start.1
  234.7 9.2 collective-permute-start
  235.6 11.0 collective-permute-start.1
  247.6 9.2 collective-permute-start
  248.5 11.0 collective-permute-start.1
  296.2 270.3 %reduce-scatter.9.cloned.1.call-start = ((), (), s32[]{:S(2)}) async-start(), calls=%async_computation.13 | async-start | bytes 5242880 | tf_op jit(solution)/shard_map/reduce_scatter | solution.py:321
  297.2 29.1 %collective-permute-start.2 = (bf16[128,1024]{0,1:T(8,128)(2,1)S(1)}, bf16[128,1024]{0,1:T(8,128)(2,1)}, u32[]{:S(2)}, u32[]{:S(2)}) collective-permute-start(bf16[128,1024]{0,1:T(8,128)(2,1)S(1)} %copy.70), channel_id=1, source_target_pairs={{28,0},{0,4},{4,8},{8,12},{12,16},{16,20},{20,24},{24,28},{29,1},{... | collective-permute-start | bytes 786440 | tf_op jit(solution)/shard_map/while/body/eval_jaxpr/ppermute | solution.py:21
  298.7 27.6 %collective-permute-start.3 = (bf16[128,1024]{0,1:T(8,128)(2,1)S(1)}, bf16[128,1024]{0,1:T(8,128)(2,1)S(1)}, u32[]{:S(2)}, u32[]{:S(2)}) collective-permute-start(bf16[128,1024]{0,1:T(8,128)(2,1)S(1)} %copy.71), channel_id=1, source_target_pairs={{28,0},{0,4},{4,8},{8,12},{12,16},{16,20},{20,24},{24,28},{29,1},{... | collective-permute-start | bytes 786440 | tf_op jit(solution)/shard_map/while/body/eval_jaxpr/ppermute | solution.py:21
  302.6 17.8 %collective-permute-start.4 = (bf16[128,1024]{0,1:T(8,128)(2,1)}, bf16[128,1024]{0,1:T(8,128)(2,1)}, u32[]{:S(2)}, u32[]{:S(2)}) collective-permute-start(bf16[128,1024]{0,1:T(8,128)(2,1)} %fusion.139), channel_id=1, source_target_pairs={{28,0},{0,4},{4,8},{8,12},{12,16},{16,20},{20,24},{24,28},{29,1},{... | collective-permute-start | bytes 786440 | tf_op jit(solution)/shard_map/while/body/eval_jaxpr/ppermute | solution.py:21
  305.1 20.3 %collective-permute-start.5 = (bf16[128,1024]{0,1:T(8,128)(2,1)}, bf16[128,1024]{0,1:T(8,128)(2,1)}, u32[]{:S(2)}, u32[]{:S(2)}) collective-permute-start(bf16[128,1024]{0,1:T(8,128)(2,1)} %fusion.141), channel_id=1, source_target_pairs={{28,0},{0,4},{4,8},{8,12},{12,16},{16,20},{20,24},{24,28},{29,1},{... | collective-permute-start | bytes 786440 | tf_op jit(solution)/shard_map/while/body/eval_jaxpr/ppermute | solution.py:21
  327.3 28.3 %collective-permute-start.2 = (bf16[128,1024]{0,1:T(8,128)(2,1)S(1)}, bf16[128,1024]{0,1:T(8,128)(2,1)}, u32[]{:S(2)}, u32[]{:S(2)}) collective-permute-start(bf16[128,1024]{0,1:T(8,128)(2,1)S(1)} %copy.70), channel_id=1, source_target_pairs={{28,0},{0,4},{4,8},{8,12},{12,16},{16,20},{20,24},{24,28},{29,1},{... | collective-permute-start | bytes 786440 | tf_op jit(solution)/shard_map/while/body/eval_jaxpr/ppermute | solution.py:21
  327.4 28.3 %collective-permute-start.3 = (bf16[128,1024]{0,1:T(8,128)(2,1)S(1)}, bf16[128,1024]{0,1:T(8,128)(2,1)S(1)}, u32[]{:S(2)}, u32[]{:S(2)}) collective-permute-start(bf16[128,1024]{0,1:T(8,128)(2,1)S(1)} %copy.71), channel_id=1, source_target_pairs={{28,0},{0,4},{4,8},{8,12},{12,16},{16,20},{20,24},{24,28},{29,1},{... | collective-permute-start | bytes 786440 | tf_op jit(solution)/shard_map/while/body/eval_jaxpr/ppermute | solution.py:21
  330.9 19.8 %collective-permute-start.4 = (bf16[128,1024]{0,1:T(8,128)(2,1)}, bf16[128,1024]{0,1:T(8,128)(2,1)}, u32[]{:S(2)}, u32[]{:S(2)}) collective-permute-start(bf16[128,1024]{0,1:T(8,128)(2,1)} %fusion.139), channel_id=1, source_target_pairs={{28,0},{0,4},{4,8},{8,12},{12,16},{16,20},{20,24},{24,28},{29,1},{... | collective-permute-start | bytes 786440 | tf_op jit(solution)/shard_map/while/body/eval_jaxpr/ppermute | solution.py:21
  332.5 22.2 %collective-permute-start.5 = (bf16[128,1024]{0,1:T(8,128)(2,1)}, bf16[128,1024]{0,1:T(8,128)(2,1)}, u32[]{:S(2)}, u32[]{:S(2)}) collective-permute-start(bf16[128,1024]{0,1:T(8,128)(2,1)} %fusion.141), channel_id=1, source_target_pairs={{28,0},{0,4},{4,8},{8,12},{12,16},{16,20},{20,24},{24,28},{29,1},{... | collective-permute-start | bytes 786440 | tf_op jit(solution)/shard_map/while/body/eval_jaxpr/ppermute | solution.py:21
  356.6 27.4 %collective-permute-start.2 = (bf16[128,1024]{0,1:T(8,128)(2,1)S(1)}, bf16[128,1024]{0,1:T(8,128)(2,1)}, u32[]{:S(2)}, u32[]{:S(2)}) collective-permute-start(bf16[128,1024]{0,1:T(8,128)(2,1)S(1)} %copy.70), channel_id=1, source_target_pairs={{28,0},{0,4},{4,8},{8,12},{12,16},{16,20},{20,24},{24,28},{29,1},{... | collective-permute-start | bytes 786440 | tf_op jit(solution)/shard_map/while/body/eval_jaxpr/ppermute | solution.py:21
  356.7 27.4 %collective-permute-start.3 = (bf16[128,1024]{0,1:T(8,128)(2,1)S(1)}, bf16[128,1024]{0,1:T(8,128)(2,1)S(1)}, u32[]{:S(2)}, u32[]{:S(2)}) collective-permute-start(bf16[128,1024]{0,1:T(8,128)(2,1)S(1)} %copy.71), channel_id=1, source_target_pairs={{28,0},{0,4},{4,8},{8,12},{12,16},{16,20},{20,24},{24,28},{29,1},{... | collective-permute-start | bytes 786440 | tf_op jit(solution)/shard_map/while/body/eval_jaxpr/ppermute | solution.py:21
  359.1 20.9 %collective-permute-start.4 = (bf16[128,1024]{0,1:T(8,128)(2,1)}, bf16[128,1024]{0,1:T(8,128)(2,1)}, u32[]{:S(2)}, u32[]{:S(2)}) collective-permute-start(bf16[128,1024]{0,1:T(8,128)(2,1)} %fusion.139), channel_id=1, source_target_pairs={{28,0},{0,4},{4,8},{8,12},{12,16},{16,20},{20,24},{24,28},{29,1},{... | collective-permute-start | bytes 786440 | tf_op jit(solution)/shard_map/while/body/eval_jaxpr/ppermute | solution.py:21
  360.1 22.9 %collective-permute-start.5 = (bf16[128,1024]{0,1:T(8,128)(2,1)}, bf16[128,1024]{0,1:T(8,128)(2,1)}, u32[]{:S(2)}, u32[]{:S(2)}) collective-permute-start(bf16[128,1024]{0,1:T(8,128)(2,1)} %fusion.141), channel_id=1, source_target_pairs={{28,0},{0,4},{4,8},{8,12},{12,16},{16,20},{20,24},{24,28},{29,1},{... | collective-permute-start | bytes 786440 | tf_op jit(solution)/shard_map/while/body/eval_jaxpr/ppermute | solution.py:21
  385.0 26.5 %collective-permute-start.2 = (bf16[128,1024]{0,1:T(8,128)(2,1)S(1)}, bf16[128,1024]{0,1:T(8,128)(2,1)}, u32[]{:S(2)}, u32[]{:S(2)}) collective-permute-start(bf16[128,1024]{0,1:T(8,128)(2,1)S(1)} %copy.70), channel_id=1, source_target_pairs={{28,0},{0,4},{4,8},{8,12},{12,16},{16,20},{20,24},{24,28},{29,1},{... | collective-permute-start | bytes 786440 | tf_op jit(solution)/shard_map/while/body/eval_jaxpr/ppermute | solution.py:21
  385.0 26.4 %collective-permute-start.3 = (bf16[128,1024]{0,1:T(8,128)(2,1)S(1)}, bf16[128,1024]{0,1:T(8,128)(2,1)S(1)}, u32[]{:S(2)}, u32[]{:S(2)}) collective-permute-start(bf16[128,1024]{0,1:T(8,128)(2,1)S(1)} %copy.71), channel_id=1, source_target_pairs={{28,0},{0,4},{4,8},{8,12},{12,16},{16,20},{20,24},{24,28},{29,1},{... | collective-permute-start | bytes 786440 | tf_op jit(solution)/shard_map/while/body/eval_jaxpr/ppermute | solution.py:21
  387.4 20.2 %collective-permute-start.4 = (bf16[128,1024]{0,1:T(8,128)(2,1)}, bf16[128,1024]{0,1:T(8,128)(2,1)}, u32[]{:S(2)}, u32[]{:S(2)}) collective-permute-start(bf16[128,1024]{0,1:T(8,128)(2,1)} %fusion.139), channel_id=1, source_target_pairs={{28,0},{0,4},{4,8},{8,12},{12,16},{16,20},{20,24},{24,28},{29,1},{... | collective-permute-start | bytes 786440 | tf_op jit(solution)/shard_map/while/body/eval_jaxpr/ppermute | solution.py:21
  388.5 22.0 %collective-permute-start.5 = (bf16[128,1024]{0,1:T(8,128)(2,1)}, bf16[128,1024]{0,1:T(8,128)(2,1)}, u32[]{:S(2)}, u32[]{:S(2)}) collective-permute-start(bf16[128,1024]{0,1:T(8,128)(2,1)} %fusion.141), channel_id=1, source_target_pairs={{28,0},{0,4},{4,8},{8,12},{12,16},{16,20},{20,24},{24,28},{29,1},{... | collective-permute-start | bytes 786440 | tf_op jit(solution)/shard_map/while/body/eval_jaxpr/ppermute | solution.py:21
  412.4 25.5 %collective-permute-start.2 = (bf16[128,1024]{0,1:T(8,128)(2,1)S(1)}, bf16[128,1024]{0,1:T(8,128)(2,1)}, u32[]{:S(2)}, u32[]{:S(2)}) collective-permute-start(bf16[128,1024]{0,1:T(8,128)(2,1)S(1)} %copy.70), channel_id=1, source_target_pairs={{28,0},{0,4},{4,8},{8,12},{12,16},{16,20},{20,24},{24,28},{29,1},{... | collective-permute-start | bytes 786440 | tf_op jit(solution)/shard_map/while/body/eval_jaxpr/ppermute | solution.py:21
  412.5 25.5 %collective-permute-start.3 = (bf16[128,1024]{0,1:T(8,128)(2,1)S(1)}, bf16[128,1024]{0,1:T(8,128)(2,1)S(1)}, u32[]{:S(2)}, u32[]{:S(2)}) collective-permute-start(bf16[128,1024]{0,1:T(8,128)(2,1)S(1)} %copy.71), channel_id=1, source_target_pairs={{28,0},{0,4},{4,8},{8,12},{12,16},{16,20},{20,24},{24,28},{29,1},{... | collective-permute-start | bytes 786440 | tf_op jit(solution)/shard_map/while/body/eval_jaxpr/ppermute | solution.py:21
  414.9 19.3 %collective-permute-start.4 = (bf16[128,1024]{0,1:T(8,128)(2,1)}, bf16[128,1024]{0,1:T(8,128)(2,1)}, u32[]{:S(2)}, u32[]{:S(2)}) collective-permute-start(bf16[128,1024]{0,1:T(8,128)(2,1)} %fusion.139), channel_id=1, source_target_pairs={{28,0},{0,4},{4,8},{8,12},{12,16},{16,20},{20,24},{24,28},{29,1},{... | collective-permute-start | bytes 786440 | tf_op jit(solution)/shard_map/while/body/eval_jaxpr/ppermute | solution.py:21
  415.9 21.1 %collective-permute-start.5 = (bf16[128,1024]{0,1:T(8,128)(2,1)}, bf16[128,1024]{0,1:T(8,128)(2,1)}, u32[]{:S(2)}, u32[]{:S(2)}) collective-permute-start(bf16[128,1024]{0,1:T(8,128)(2,1)} %fusion.141), channel_id=1, source_target_pairs={{28,0},{0,4},{4,8},{8,12},{12,16},{16,20},{20,24},{24,28},{29,1},{... | collective-permute-start | bytes 786440 | tf_op jit(solution)/shard_map/while/body/eval_jaxpr/ppermute | solution.py:21
  439.0 24.6 %collective-permute-start.2 = (bf16[128,1024]{0,1:T(8,128)(2,1)S(1)}, bf16[128,1024]{0,1:T(8,128)(2,1)}, u32[]{:S(2)}, u32[]{:S(2)}) collective-permute-start(bf16[128,1024]{0,1:T(8,128)(2,1)S(1)} %copy.70), channel_id=1, source_target_pairs={{28,0},{0,4},{4,8},{8,12},{12,16},{16,20},{20,24},{24,28},{29,1},{... | collective-permute-start | bytes 786440 | tf_op jit(solution)/shard_map/while/body/eval_jaxpr/ppermute | solution.py:21
  439.0 24.6 %collective-permute-start.3 = (bf16[128,1024]{0,1:T(8,128)(2,1)S(1)}, bf16[128,1024]{0,1:T(8,128)(2,1)S(1)}, u32[]{:S(2)}, u32[]{:S(2)}) collective-permute-start(bf16[128,1024]{0,1:T(8,128)(2,1)S(1)} %copy.71), channel_id=1, source_target_pairs={{28,0},{0,4},{4,8},{8,12},{12,16},{16,20},{20,24},{24,28},{29,1},{... | collective-permute-start | bytes 786440 | tf_op jit(solution)/shard_map/while/body/eval_jaxpr/ppermute | solution.py:21
  441.4 18.4 %collective-permute-start.4 = (bf16[128,1024]{0,1:T(8,128)(2,1)}, bf16[128,1024]{0,1:T(8,128)(2,1)}, u32[]{:S(2)}, u32[]{:S(2)}) collective-permute-start(bf16[128,1024]{0,1:T(8,128)(2,1)} %fusion.139), channel_id=1, source_target_pairs={{28,0},{0,4},{4,8},{8,12},{12,16},{16,20},{20,24},{24,28},{29,1},{... | collective-permute-start | bytes 786440 | tf_op jit(solution)/shard_map/while/body/eval_jaxpr/ppermute | solution.py:21
  442.4 20.2 %collective-permute-start.5 = (bf16[128,1024]{0,1:T(8,128)(2,1)}, bf16[128,1024]{0,1:T(8,128)(2,1)}, u32[]{:S(2)}, u32[]{:S(2)}) collective-permute-start(bf16[128,1024]{0,1:T(8,128)(2,1)} %fusion.141), channel_id=1, source_target_pairs={{28,0},{0,4},{4,8},{8,12},{12,16},{16,20},{20,24},{24,28},{29,1},{... | collective-permute-start | bytes 786440 | tf_op jit(solution)/shard_map/while/body/eval_jaxpr/ppermute | solution.py:21
  464.6 23.7 %collective-permute-start.2 = (bf16[128,1024]{0,1:T(8,128)(2,1)S(1)}, bf16[128,1024]{0,1:T(8,128)(2,1)}, u32[]{:S(2)}, u32[]{:S(2)}) collective-permute-start(bf16[128,1024]{0,1:T(8,128)(2,1)S(1)} %copy.70), channel_id=1, source_target_pairs={{28,0},{0,4},{4,8},{8,12},{12,16},{16,20},{20,24},{24,28},{29,1},{... | collective-permute-start | bytes 786440 | tf_op jit(solution)/shard_map/while/body/eval_jaxpr/ppermute | solution.py:21
  464.6 23.7 %collective-permute-start.3 = (bf16[128,1024]{0,1:T(8,128)(2,1)S(1)}, bf16[128,1024]{0,1:T(8,128)(2,1)S(1)}, u32[]{:S(2)}, u32[]{:S(2)}) collective-permute-start(bf16[128,1024]{0,1:T(8,128)(2,1)S(1)} %copy.71), channel_id=1, source_target_pairs={{28,0},{0,4},{4,8},{8,12},{12,16},{16,20},{20,24},{24,28},{29,1},{... | collective-permute-start | bytes 786440 | tf_op jit(solution)/shard_map/while/body/eval_jaxpr/ppermute | solution.py:21
  467.0 17.5 %collective-permute-start.4 = (bf16[128,1024]{0,1:T(8,128)(2,1)}, bf16[128,1024]{0,1:T(8,128)(2,1)}, u32[]{:S(2)}, u32[]{:S(2)}) collective-permute-start(bf16[128,1024]{0,1:T(8,128)(2,1)} %fusion.139), channel_id=1, source_target_pairs={{28,0},{0,4},{4,8},{8,12},{12,16},{16,20},{20,24},{24,28},{29,1},{... | collective-permute-start | bytes 786440 | tf_op jit(solution)/shard_map/while/body/eval_jaxpr/ppermute | solution.py:21
  468.0 19.2 %collective-permute-start.5 = (bf16[128,1024]{0,1:T(8,128)(2,1)}, bf16[128,1024]{0,1:T(8,128)(2,1)}, u32[]{:S(2)}, u32[]{:S(2)}) collective-permute-start(bf16[128,1024]{0,1:T(8,128)(2,1)} %fusion.141), channel_id=1, source_target_pairs={{28,0},{0,4},{4,8},{8,12},{12,16},{16,20},{20,24},{24,28},{29,1},{... | collective-permute-start | bytes 786440 | tf_op jit(solution)/shard_map/while/body/eval_jaxpr/ppermute | solution.py:21
  489.3 22.7 %collective-permute-start.2 = (bf16[128,1024]{0,1:T(8,128)(2,1)S(1)}, bf16[128,1024]{0,1:T(8,128)(2,1)}, u32[]{:S(2)}, u32[]{:S(2)}) collective-permute-start(bf16[128,1024]{0,1:T(8,128)(2,1)S(1)} %copy.70), channel_id=1, source_target_pairs={{28,0},{0,4},{4,8},{8,12},{12,16},{16,20},{20,24},{24,28},{29,1},{... | collective-permute-start | bytes 786440 | tf_op jit(solution)/shard_map/while/body/eval_jaxpr/ppermute | solution.py:21
  489.3 22.7 %collective-permute-start.3 = (bf16[128,1024]{0,1:T(8,128)(2,1)S(1)}, bf16[128,1024]{0,1:T(8,128)(2,1)S(1)}, u32[]{:S(2)}, u32[]{:S(2)}) collective-permute-start(bf16[128,1024]{0,1:T(8,128)(2,1)S(1)} %copy.71), channel_id=1, source_target_pairs={{28,0},{0,4},{4,8},{8,12},{12,16},{16,20},{20,24},{24,28},{29,1},{... | collective-permute-start | bytes 786440 | tf_op jit(solution)/shard_map/while/body/eval_jaxpr/ppermute | solution.py:21
  491.7 16.4 %collective-permute-start.4 = (bf16[128,1024]{0,1:T(8,128)(2,1)}, bf16[128,1024]{0,1:T(8,128)(2,1)}, u32[]{:S(2)}, u32[]{:S(2)}) collective-permute-start(bf16[128,1024]{0,1:T(8,128)(2,1)} %fusion.139), channel_id=1, source_target_pairs={{28,0},{0,4},{4,8},{8,12},{12,16},{16,20},{20,24},{24,28},{29,1},{... | collective-permute-start | bytes 786440 | tf_op jit(solution)/shard_map/while/body/eval_jaxpr/ppermute | solution.py:21
  492.7 18.2 %collective-permute-start.5 = (bf16[128,1024]{0,1:T(8,128)(2,1)}, bf16[128,1024]{0,1:T(8,128)(2,1)}, u32[]{:S(2)}, u32[]{:S(2)}) collective-permute-start(bf16[128,1024]{0,1:T(8,128)(2,1)} %fusion.141), channel_id=1, source_target_pairs={{28,0},{0,4},{4,8},{8,12},{12,16},{16,20},{20,24},{24,28},{29,1},{... | collective-permute-start | bytes 786440 | tf_op jit(solution)/shard_map/while/body/eval_jaxpr/ppermute | solution.py:21
  524.3 88.8 %reduce-scatter.7.cloned.1.call-start = ((), (), s32[]{:S(2)}) async-start(), calls=%async_computation.12 | async-start | bytes 5242880 | tf_op jit(solution)/shard_map/reduce_scatter | solution.py:318
  528.6 145.5 %reduce-scatter.11.cloned.1.call-start = ((), (), s32[]{:S(2)}) async-start(), calls=%async_computation.14 | async-start | bytes 7864320 | tf_op jit(solution)/shard_map/reduce_scatter | solution.py:324
  534.2 214.2 %reduce-scatter.15.cloned.1.call-start = ((), (), s32[]{:S(2)}) async-start(), calls=%async_computation.16 | async-start | bytes 10485760 | tf_op jit(solution)/shard_map/reduce_scatter | solution.py:333
  541.4 281.4 %reduce-scatter.17.cloned.1.call-start = ((), (), s32[]{:S(2)}) async-start(), calls=%async_computation.17 | async-start | bytes 10485760 | tf_op jit(solution)/shard_map/reduce_scatter | solution.py:336
  (21 other events, 59.7 us)
Sparse Core Ops, SparseCore 0:
  9.6 37.1 all-gather.7
  48.3 34.4 all-gather.9
  84.4 46.3 all-gather.11
  132.3 22.5 all-gather.13
  156.3 58.3 all-gather.15
  216.1 58.2 all-gather.17
  296.3 31.4 reduce-scatter.12
  524.4 41.0 reduce-scatter.8
  568.6 44.4 reduce-scatter.6
  615.7 58.3 reduce-scatter.10
  676.7 71.7 reduce-scatter.14
  751.1 71.6 reduce-scatter.16
where the time goes:
time: 1480 us
  blocking collectives  659 us (45%)
  waiting for transfers between devices  606 us (41%)
  matrix products  102 us (7%)
  other arithmetic  38 us (3%)
  local copies, waits for them, and re-layouts  37.2 us (3%)
  starting transfers between devices  18.1 us (1%)
  between operations  15.8 us (1%)
    psum x1, blocking collectives, per_device(): lax.psum((shards[0], shards[1], shards[2], shards[3], shards[4], shards[5...  646 us
    ppermute x48, waiting for transfers between devices, from_behind(): return lax.ppermute(block, axis, route)  238 us
    reduce_scatter x1, waiting for transfers between devices, per_device(): lax.psum_scatter(grad_down.astype(jnp.bfloat16), 'grp', scatter_dimension...  74.4 us
    reduce_scatter x1, waiting for transfers between devices, per_device(): lax.psum_scatter(grad_up.astype(jnp.bfloat16), 'grp', scatter_dimension=0...  74.3 us
    reduce_scatter x1, waiting for transfers between devices, per_device(): lax.psum_scatter(grad_qkv.astype(jnp.bfloat16), 'grp', scatter_dimension=...  61 us
    reduce_scatter x1, waiting for transfers between devices, per_device(): lax.psum_scatter(grad_skip_weight.astype(jnp.bfloat16), 'grp', scatter_di...  46.6 us
    all_gather x1, waiting for transfers between devices, per_device(): lax.all_gather(w_qkv, 'grp', axis=0, tiled=True)  43.4 us
    all_gather x1, waiting for transfers between devices, per_device(): lax.all_gather(w_mod, 'grp', axis=0, tiled=True)  32.9 us
  transfers between devices with their start and end apart: 60, of which 40 were waited for; matrix products, arithmetic and copies ran while one was open for 10% of the time, Pallas kernels for 0%

commit v1 on v0

--- a/solution.py
+++ b/solution.py
@@ -354,6 +354,261 @@
     )
 
 
+def rows_dot(left_side, right_side):
+    return jnp.dot(left_side, right_side, preferred_element_type=jnp.float32)
+
+
+def dot_columns(left_side, right_side):
+    return lax.dot_general(
+        left_side, right_side, (((1,), (1,)), ((), ())), preferred_element_type=jnp.float32
+    )
+
+
+def summed_rows(partial, axis="grp"):
+    return lax.psum_scatter(
+        partial.astype(jnp.bfloat16), axis, scatter_dimension=0, tiled=True
+    ).astype(jnp.float32)
+
+
+def gathered(block, axis="grp"):
+    return lax.all_gather(block, axis, axis=0, tiled=True)
+
+
+def per_device_shards(
+    inputs,
+    skipped,
+    w_skip,
+    w_mod,
+    w_qkv,
+    w_out,
+    ff_gain,
+    w_up,
+    w_down,
+    cotangent,
+    lengths,
+    flow_steps,
+):
+    frame_count = inputs.shape[1]
+    model_width = inputs.shape[2]
+    rows = lax.axis_size("grp")
+    blocks = lax.axis_size("blk")
+    group_rank = lax.axis_index("grp")
+    block_rank = lax.axis_index("blk")
+    tokens = rows * frame_count
+    heads_here = HEADS // rows
+    columns_here = model_width // rows
+    pairs_per_row = blocks // rows
+    pair_heads = heads_here // pairs_per_row
+    pair_columns = pair_heads * HEAD_DIM
+    score_scale = HEAD_DIM ** (-0.5)
+    utterances = lengths.shape[1]
+
+    lengths_all = gathered(lengths)
+    steps_all = gathered(flow_steps)
+    gain_vector = gathered(ff_gain).astype(jnp.float32)
+    w_qkv_here = lax.all_to_all(
+        w_qkv.reshape(columns_here, 3, rows, columns_here), "grp", 2, 0, tiled=True
+    ).reshape(model_width, 3 * columns_here)
+    w_up_here = lax.all_to_all(
+        w_up.reshape(columns_here, rows, -1), "grp", 1, 0, tiled=True
+    ).reshape(model_width, -1)
+    upstream = cotangent[0]
+    upstream_all = gathered(upstream)
+
+    frames = block_rank * frame_count + jnp.arange(frame_count, dtype=jnp.int32)
+    lengths_row = lengths[0]
+    own_segment, own_position = layout(lengths_row, frames)
+    all_position = jax.vmap(lambda row: layout(row, frames)[1])(lengths_all).reshape(tokens)
+
+    joined = jnp.concatenate([inputs[0], skipped[0]], axis=1)
+    joined_here = lax.all_to_all(
+        joined.reshape(frame_count, rows, -1), "grp", 1, 0, tiled=True
+    ).reshape(tokens, -1)
+    hidden = summed_rows(rows_dot(joined_here, w_skip))
+
+    condition = flow_condition(steps_all.reshape(-1), model_width).astype(jnp.bfloat16)
+    condition_here = lax.dynamic_slice_in_dim(
+        condition, group_rank * columns_here, columns_here, axis=1
+    )
+    modulation = lax.psum_scatter(
+        rows_dot(condition_here, w_mod), "grp", scatter_dimension=0, tiled=True
+    )
+    picker = (
+        own_segment[:, None] == jnp.arange(utterances, dtype=jnp.int32)[None, :]
+    ).astype(jnp.float32)
+    per_frame = jnp.dot(picker, modulation, precision=HIGHEST)
+    scale_one = 1.0 + per_frame[:, :model_width]
+    normal_one, spread_one = normalize(hidden)
+    attn_in = gathered(
+        (normal_one * scale_one + per_frame[:, model_width:]).astype(jnp.bfloat16)
+    )
+
+    def rotated(block, position, turn):
+        return turn(heads_of_block(block), position).reshape(block.shape)
+
+    def heads_of_block(block):
+        return block.reshape(block.shape[0], -1, HEAD_DIM)
+
+    project = rows_dot(attn_in, w_qkv_here)
+    sent = jnp.concatenate(
+        [
+            rotated(project[:, :columns_here], all_position, rotate),
+            rotated(project[:, columns_here : 2 * columns_here], all_position, rotate),
+            project[:, 2 * columns_here :],
+        ],
+        axis=1,
+    ).astype(jnp.bfloat16)
+
+    def to_pairs(block, kinds):
+        block = block.reshape(rows, frame_count, kinds, pairs_per_row, pair_columns)
+        block = jnp.transpose(block, (0, 3, 1, 2, 4)).reshape(
+            blocks, frame_count, kinds * pair_columns
+        )
+        return lax.all_to_all(block, "blk", 0, 0, tiled=True).reshape(
+            blocks * frame_count, kinds * pair_columns
+        )
+
+    def from_pairs(block, kinds):
+        block = lax.all_to_all(
+            block.reshape(blocks, frame_count, kinds * pair_columns), "blk", 0, 0, tiled=True
+        ).reshape(rows, pairs_per_row, frame_count, kinds, pair_columns)
+        return jnp.transpose(block, (0, 2, 3, 1, 4)).reshape(
+            tokens, kinds * pairs_per_row * pair_columns
+        )
+
+    paired = to_pairs(sent, 3)
+    queries, keys, values = (
+        heads_of_block(paired[:, :pair_columns]),
+        heads_of_block(paired[:, pair_columns : 2 * pair_columns]),
+        heads_of_block(paired[:, 2 * pair_columns :]),
+    )
+    pair_lengths = lax.dynamic_index_in_dim(
+        lengths_all, block_rank // pairs_per_row, axis=0, keepdims=False
+    )
+    row_segment, row_position = layout(
+        pair_lengths, jnp.arange(blocks * frame_count, dtype=jnp.int32)
+    )
+    allowed = (row_segment[:, None] == row_segment[None, :])[None]
+    raw_scores = (
+        jnp.einsum("qhd,khd->hqk", queries, keys, preferred_element_type=jnp.float32)
+        * score_scale
+    )
+    raw_scores = jnp.where(allowed, raw_scores, NEGATIVE)
+    top = jnp.max(raw_scores, axis=2, keepdims=True)
+    weights = jnp.exp(raw_scores - top)
+    total = jnp.sum(weights, axis=2, keepdims=True)
+    probabilities = weights / total
+    prob_low = probabilities.astype(jnp.bfloat16)
+    attended_pair = jnp.einsum(
+        "hqk,khd->qhd", prob_low, values, preferred_element_type=jnp.float32
+    )
+    attended_here = from_pairs(
+        attended_pair.astype(jnp.bfloat16).reshape(-1, pair_columns), 1
+    )
+
+    hidden_two = hidden + summed_rows(rows_dot(attended_here, w_out))
+    normal_two, spread_two = normalize(hidden_two)
+    ff_in = gathered((normal_two * gain_vector).astype(jnp.bfloat16))
+    widened = rows_dot(ff_in, w_up_here)
+    activated, gelu_back = jax.vjp(exact_gelu, widened)
+    activated_low = activated.astype(jnp.bfloat16)
+    output = (hidden_two + summed_rows(rows_dot(activated_low, w_down))).astype(jnp.bfloat16)
+    grad_down = contract_rows(activated_low, upstream_all)
+    grad_widened = gelu_back(dot_columns(upstream_all, w_down))[0].astype(jnp.bfloat16)
+    grad_up = contract_rows(ff_in, grad_widened)
+    grad_ff_in = summed_rows(dot_columns(grad_widened, w_up_here))
+    grad_gain = jnp.sum(grad_ff_in * normal_two, axis=0)
+    grad_hidden_two = upstream.astype(jnp.float32) + norm_back(
+        grad_ff_in * gain_vector, normal_two, spread_two
+    )
+
+    def over_blocks(grad):
+        shard = lax.psum_scatter(
+            grad.astype(jnp.bfloat16), "blk", scatter_dimension=0, tiled=True
+        )
+        return gathered(shard, "blk").astype(jnp.float32)
+
+    def over_blocks_columns(grad, kinds):
+        wide = grad.shape[1] // kinds
+        grad = grad.reshape(rows, blocks, columns_here // blocks, grad.shape[1])
+        grad = jnp.transpose(grad, (1, 0, 2, 3)).astype(jnp.bfloat16)
+        shard = lax.psum_scatter(grad, "blk", scatter_dimension=0, tiled=True)[0]
+        shard = lax.all_to_all(
+            shard.reshape(rows, columns_here // blocks, kinds, 1, wide), "grp", 0, 3, tiled=True
+        )
+        return gathered(shard.reshape(columns_here // blocks, -1), "blk").astype(jnp.float32)
+
+    total_down = over_blocks(grad_down)
+    total_up = over_blocks_columns(grad_up, 1)
+
+    grad_two_low = gathered(grad_hidden_two.astype(jnp.bfloat16))
+    total_out = over_blocks(contract_rows(attended_here, grad_two_low))
+    grad_attended = heads_of_block(
+        to_pairs(dot_columns(grad_two_low, w_out).astype(jnp.bfloat16), 1)
+    )
+    delta = jnp.transpose(jnp.sum(grad_attended.astype(jnp.float32) * attended_pair, axis=2))
+    value_grad = jnp.einsum(
+        "hqk,qhd->khd", prob_low, grad_attended, preferred_element_type=jnp.float32
+    )
+    prob_grad = jnp.einsum(
+        "qhd,khd->hqk", grad_attended, values, preferred_element_type=jnp.float32
+    )
+    score_grad = (probabilities * (prob_grad - delta[:, :, None])).astype(jnp.bfloat16)
+    query_grad = (
+        jnp.einsum("hqk,khd->qhd", score_grad, keys, preferred_element_type=jnp.float32)
+        * score_scale
+    )
+    key_grad = (
+        jnp.einsum("hqk,qhd->khd", score_grad, queries, preferred_element_type=jnp.float32)
+        * score_scale
+    )
+    grad_paired = jnp.concatenate(
+        [
+            rotate_back(query_grad, row_position).reshape(-1, pair_columns),
+            rotate_back(key_grad, row_position).reshape(-1, pair_columns),
+            value_grad.reshape(-1, pair_columns),
+        ],
+        axis=1,
+    ).astype(jnp.bfloat16)
+    grad_project = from_pairs(grad_paired, 3)
+    total_qkv = over_blocks_columns(contract_rows(attn_in, grad_project), 3)
+    grad_attn_in = summed_rows(dot_columns(grad_project, w_qkv_here))
+
+    mod_terms = jnp.concatenate([grad_attn_in * normal_one, grad_attn_in], axis=1)
+    grad_modulation = gathered(lax.psum(jnp.dot(picker.T, mod_terms, precision=HIGHEST), "blk"))
+    grad_mod = jnp.dot(
+        condition_here.astype(jnp.float32).T, grad_modulation, precision=HIGHEST
+    )
+
+    grad_hidden = grad_hidden_two + norm_back(grad_attn_in * scale_one, normal_one, spread_one)
+    grad_hidden_low = gathered(grad_hidden.astype(jnp.bfloat16))
+    total_skip = over_blocks(contract_rows(joined_here, grad_hidden_low))
+    grad_joined = lax.all_to_all(
+        dot_columns(grad_hidden_low, w_skip)
+        .astype(jnp.bfloat16)
+        .reshape(rows, frame_count, 1, -1),
+        "grp",
+        0,
+        2,
+        tiled=True,
+    ).reshape(frame_count, -1).astype(jnp.float32)
+    total_gain = lax.psum_scatter(
+        lax.psum(grad_gain, "blk"), "grp", scatter_dimension=0, tiled=True
+    )
+    return (
+        output[None],
+        grad_joined[:, :model_width][None],
+        grad_joined[:, model_width:][None],
+        total_skip,
+        grad_mod,
+        total_qkv,
+        total_out,
+        total_gain,
+        total_up,
+        total_down,
+    )
+
+
 def solution(mesh):
     placed = (
         P("grp", "blk", None),
@@ -369,8 +624,12 @@
         P("grp", None),
         P("grp", None),
     )
+    rows, blocks = mesh.shape["grp"], mesh.shape["blk"]
+    body = per_device
+    if blocks % rows == 0 and HEADS % blocks == 0:
+        body = per_device_shards
     return jax.shard_map(
-        per_device,
+        body,
         mesh=mesh,
         in_specs=placed,
         out_specs=(

time: 1480 us -> 1110 us (0.75)
  blocking collectives: 659 us -> 155 us
  waiting for transfers between devices: 606 us -> 697 us
  local copies, waits for them, and re-layouts: 37.2 us -> 76.9 us
  matrix products: 102 us -> 79.8 us
    psum x1, blocking collectives: 646 us -> 20 us  [per_device_shards(): lax.psum(grad_gain, 'blk')]
    ppermute x48 -> x0, waiting for transfers between devices: 238 us -> none  [from_behind(): return lax.ppermute(block, axis, route)]
    unnamed x12 -> x21, waiting for transfers between devices: 3.74 us -> 147 us
    all_gather x6 -> x9, waiting for transfers between devices: 107 us -> 179 us  [gathered(): return lax.all_gather(block, axis, axis=0, tiled=True)]
    all_gather x1 -> x5, blocking collectives: 5.98 us -> 76.1 us  [gathered(): return lax.all_gather(block, axis, axis=0, tiled=True)]
    all_to_all x0 -> x6, waiting for transfers between devices: none -> 59.7 us  [the longest x1 34.1 us: per_device_shards(): lax.all_to_all(w_up.reshape(columns_here, rows, -1), 'grp', 1, 0, tiled=T...]
    all_to_all x0 -> x4, blocking collectives: none -> 52.8 us  [the longest x2 36.5 us: from_pairs(): lax.all_to_all(block.reshape(blocks, frame_count, kinds * pair_columns),...]
    psum x0 -> x1, waiting for transfers between devices: none -> 38.5 us  [per_device_shards(): lax.psum(jnp.dot(picker.T, mod_terms, precision=HIGHEST), 'blk')]
  transfers between devices with their start and end apart: 60 -> 26, of which waited for: 40 -> 20; matrix products, arithmetic and copies ran while one was open for 10% -> 9% of each run, Pallas kernels for 0% -> 0%
where the time goes in v1:
time: 1110 us; the launch traced here: 1100 us
  waiting for transfers between devices  697 us (63%)
  blocking collectives  155 us (14%)
  matrix products  79.8 us (7%)
  local copies, waits for them, and re-layouts  76.9 us (7%)
  other arithmetic  49.6 us (4%)
  starting transfers between devices  29.4 us (3%)
  between operations  15.9 us (1%)
    all_gather x9, waiting for transfers between devices, gathered(): return lax.all_gather(block, axis, axis=0, tiled=True)  179 us
    unnamed x21, waiting for transfers between devices  147 us
    reduce_scatter x3, waiting for transfers between devices, over_blocks(): lax.psum_scatter(grad.astype(jnp.bfloat16), 'blk', scatter_dimension=0, t...  141 us
    reduce_scatter x5, waiting for transfers between devices, summed_rows(): lax.psum_scatter(partial.astype(jnp.bfloat16), axis, scatter_dimension=0,...  115 us
    all_gather x5, blocking collectives, gathered(): return lax.all_gather(block, axis, axis=0, tiled=True)  76.1 us
    psum x1, waiting for transfers between devices, per_device_shards(): lax.psum(jnp.dot(picker.T, mod_terms, precision=HIGHEST), 'blk')  38.5 us
    all_to_all x2, blocking collectives, from_pairs(): lax.all_to_all(block.reshape(blocks, frame_count, kinds * pair_columns),...  36.5 us
    all_to_all x1, waiting for transfers between devices, per_device_shards(): lax.all_to_all(w_up.reshape(columns_here, rows, -1), 'grp', 1, 0, tiled=T...  34.1 us
  transfers between devices with their start and end apart: 26, of which 20 were waited for; matrix products, arithmetic and copies ran while one was open for 9% of the time, Pallas kernels for 0%

profile of v1, /device:TPU:0, one launch (start us, length us, event | category | flops | bytes accessed | tf_op | source)
XLA Modules:
  0.0 1103.2 jit_solution(12231450477230405164)
XLA Ops:
  10.5 4.2 all-to-all-start
  14.7 9.7 all-gather.1
  27.4 3.1 convolution_convert_fusion.8
  30.9 17.4 %reduce-scatter.18.cloned.1.call-done = f32[8,2048]{1,0:T(8,128)} async-done(((f32[32,2048]{1,0:T(8,128)}), f32[8,2048]{1,0:T(8,128)}) %reduce-scatter.18.cloned.1.call-update) | async-done | bytes 65552 | tf_op jit(solution)/shard_map/reduce_scatter | solution.py:433
  49.7 26.7 %reduce-scatter.16.cloned.1.call-done = bf16[128,1024]{1,0:T(8,128)(2,1)} async-done(((bf16[512,1024]{1,0:T(8,128)(2,1)}), bf16[128,1024]{1,0:T(8,128)(2,1)}) %reduce-scatter.16.cloned.1.call-update) | async-done | bytes 262160 | tf_op jit(solution)/shard_map/reduce_scatter | solution.py:368
  80.7 2.6 copy.152
  83.3 2.7 copy.153
  85.9 4.4 all-to-all-start.1
  90.3 23.5 %all-gather.2 = s32[4,1,8]{2,1,0:T(1,128)S(1)} all-gather(s32[1,1,8]{2,1,0:T(1,128)S(1)} %bitcast.270), channel_id=1, replica_groups=mesh['blk'=8,'grp'=4] {'grp'}, dimensions={0}, use_global_device_ids=true | all-gather | bytes 160 | tf_op jit(solution)/shard_map/all_gather | solution.py:374
  114.8 2.6 copy.154
  118.9 2.7 fusion.73
  134.5 2.7 convert_element_type.183
  137.2 3.0 copy.159
  140.2 5.5 all-to-all-start.2
  147.9 18.6 %all-to-all-done.2 = bf16[8,128,384]{1,2,0:T(8,128)(2,1)} async-done(((bf16[8,128,384]{1,2,0:T(8,128)(2,1)}), bf16[8,128,384]{1,2,0:T(8,128)(2,1)}, u32[]{:S(2)}, u32[]{:S(2)}) %all-to-all-start.2) | async-done | bytes 786464 | tf_op jit(solution)/shard_map/all_to_all | solution.py:467
  174.4 8.0 fusion.70
  182.4 4.6 fusion.5
  190.2 12.9 %all_to_all.104 = bf16[8,128,128]{2,1,0:T(8,128)(2,1)S(1)} all-to-all(bf16[8,128,128]{2,1,0:T(8,128)(2,1)} %copy.165), channel_id=1, replica_groups=mesh['blk'=8,'grp'=4] {'blk'}, dimensions={0} | all-to-all | bytes 524288 | tf_op jit(solution)/shard_map/all_to_all | solution.py:472
  206.6 5.1 all-gather.3
  211.7 18.0 %reduce-scatter.20.cloned.1.call-done = bf16[128,1024]{1,0:T(8,128)(2,1)} async-done(((bf16[512,1024]{1,0:T(8,128)(2,1)}), bf16[128,1024]{1,0:T(8,128)(2,1)}) %reduce-scatter.20.cloned.1.call-update) | async-done | bytes 262160 | tf_op jit(solution)/shard_map/reduce_scatter | solution.py:368
  233.8 4.1 copy.167
  237.9 4.5 all-to-all-start.4
  243.3 34.1 %all-to-all-done.4 = bf16[256,4,1024]{0,2,1:T(8,128)(2,1)} async-done(((bf16[256,4,1024]{0,2,1:T(8,128)(2,1)}), bf16[256,4,1024]{0,2,1:T(8,128)(2,1)}, u32[]{:S(2)}, u32[]{:S(2)}) %all-to-all-start.4) | async-done | bytes 2097184 | tf_op jit(solution)/shard_map/all_to_all | solution.py:412
  277.4 3.9 copy.168
  281.3 8.5 multiply_convert_fusion.1
  289.9 4.5 add_convert_fusion
  297.7 25.0 %reduce-scatter.24.cloned.1.call-done = bf16[128,1024]{1,0:T(8,128)(2,1)} async-done(((bf16[512,1024]{1,0:T(8,128)(2,1)}), bf16[128,1024]{1,0:T(8,128)(2,1)}) %reduce-scatter.24.cloned.1.call-update) | async-done | bytes 262160 | tf_op jit(solution)/shard_map/reduce_scatter | solution.py:368
  326.8 16.9 %all-gather.18.cloned.1.call-done = bf16[512,1024]{1,0:T(8,128)(2,1)} async-done(((bf16[128,1024]{1,0:T(8,128)(2,1)}), bf16[512,1024]{1,0:T(8,128)(2,1)}) %all-gather.18.cloned.1.call-update) | async-done | bytes 1048592 | tf_op jit(solution)/shard_map/all_gather | solution.py:374
  349.7 5.5 all-to-all-start.5
  357.7 7.0 all-to-all-done.5
  369.5 4.9 multiply_convert_fusion
  380.0 23.6 %all_to_all.105 = bf16[8,128,384]{1,2,0:T(8,128)(2,1)} all-to-all(bf16[8,128,384]{1,2,0:T(8,128)(2,1)S(1)} %pad_maximum_fusion.1), channel_id=1, replica_groups=mesh['blk'=8,'grp'=4] {'blk'}, dimensions={0} | all-to-all | bytes 1572864 | tf_op jit(solution)/shard_map/all_to_all | solution.py:472
  403.6 3.0 copy.178
  406.7 3.1 reshape.408
  409.8 3.6 convolution_convert_fusion.3
  413.5 3.4 convolution_convert_fusion.5
  417.0 19.5 %reduce-scatter.26.cloned.1.call-done = bf16[128,1024]{1,0:T(8,128)(2,1)} async-done(((bf16[512,1024]{1,0:T(8,128)(2,1)}), bf16[128,1024]{1,0:T(8,128)(2,1)}) %reduce-scatter.26.cloned.1.call-update) | async-done | bytes 262160 | tf_op jit(solution)/shard_map/reduce_scatter | solution.py:368
  438.5 26.1 %reduce-scatter.22.cloned.1.call-done = bf16[128,1024]{1,0:T(8,128)(2,1)} async-done(((bf16[512,1024]{1,0:T(8,128)(2,1)}), bf16[128,1024]{1,0:T(8,128)(2,1)}) %reduce-scatter.22.cloned.1.call-update) | async-done | bytes 262160 | tf_op jit(solution)/shard_map/reduce_scatter | solution.py:368
  467.2 4.2 convolution_convert_fusion
  473.9 4.4 convolution_convert_fusion.1
  479.5 3.6 fusion.12
  484.1 2.9 convolution_convert_fusion.7
  487.2 2.5 convolution_convert_fusion.9
  491.1 64.7 %reduce-scatter.32.cloned.1.call-done = bf16[128,1024]{1,0:T(8,128)(2,1)} async-done(((bf16[1024,1024]{1,0:T(8,128)(2,1)}), bf16[128,1024]{1,0:T(8,128)(2,1)}) %reduce-scatter.32.cloned.1.call-update) | async-done | bytes 262160 | tf_op jit(solution)/shard_map/reduce_scatter | solution.py:526
  556.4 146.1 %all-reduce.9.cloned.1.call-done = (bf16[8,4,32,768]{3,2,0,1:T(8,128)(2,1)}, bf16[8,4,32,1024]{3,2,0,1:T(8,128)(2,1)}) async-done(((bf16[8,4,32,768]{3,2,0,1:T(8,128)(2,1)}, bf16[8,4,32,1024]{3,2,0,1:T(8,128)(2,1)}), (bf16[8,4,32,768]{3,2,0,1:T(8,128)(2,1)}, bf16[8,4,32,1024]{3,2,0,1:T(8,128)(2,1)})) %all-reduce.9.cloned.1.call-update) | async-done | bytes 3670032
  704.3 7.9 all_to_all.106
  714.8 8.4 all_to_all.107
  724.3 44.5 %reduce-scatter.28.cloned.1.call-done = bf16[64,1024]{1,0:T(8,128)(2,1)} async-done(((bf16[512,1024]{1,0:T(8,128)(2,1)}), bf16[64,1024]{1,0:T(8,128)(2,1)}) %reduce-scatter.28.cloned.1.call-update) | async-done | bytes 131088 | tf_op jit(solution)/shard_map/reduce_scatter | solution.py:526
  770.1 5.7 all-reduce.1
  775.9 20.0 %psum.16 = f32[256]{0:T(256)} all-reduce(f32[256]{0:T(256)S(1)} %dynamic-slice.4), channel_id=1, replica_groups=mesh['blk'=8,'grp'=4] {'blk'}, use_global_device_ids=true, to_apply=%region_30.31 | all-reduce | flops 256 | bytes 2048 | tf_op jit(solution)/shard_map/psum | solution.py:596
  795.9 3.1 convolution_convert_fusion.10
  799.0 3.5 all-to-all-start.7
  802.5 31.5 %reduce-scatter.30.cloned.1.call-done = bf16[32,1024]{1,0:T(8,128)(2,1)} async-done(((bf16[256,1024]{1,0:T(8,128)(2,1)}), bf16[32,1024]{1,0:T(8,128)(2,1)}) %reduce-scatter.30.cloned.1.call-update) | async-done | bytes 65552 | tf_op jit(solution)/shard_map/reduce_scatter | solution.py:526
  833.9 31.8 %all_gather.53 = bf16[256,1024]{1,0:T(8,128)(2,1)S(1)} all-gather(bf16[32,1024]{1,0:T(8,128)(2,1)} %reduce-scatter.30.cloned.1.call-done), channel_id=1, replica_groups=mesh['blk'=8,'grp'=4] {'blk'}, dimensions={0}, use_global_device_ids=true | all-gather | bytes 589824 | tf_op jit(solution)/shard_map/all_gather | solution.py:374
  866.9 38.5 %all-reduce.7.cloned.1.call-done = f32[8,2048]{1,0:T(8,128)} async-done(((f32[8,2048]{1,0:T(8,128)}), f32[8,2048]{1,0:T(8,128)}) %all-reduce.7.cloned.1.call-update) | async-done | bytes 65552 | tf_op jit(solution)/shard_map/psum | solution.py:578
  905.4 6.0 all_gather.51
  913.7 42.9 %all-gather.28.cloned.1.call-done = bf16[1024,1024]{1,0:T(8,128)(2,1)} async-done(((bf16[128,1024]{1,0:T(8,128)(2,1)}), bf16[1024,1024]{1,0:T(8,128)(2,1)}) %all-gather.28.cloned.1.call-update) | async-done | bytes 2097168 | tf_op jit(solution)/shard_map/all_gather | solution.py:374
  956.6 4.1 convert_element_type.224
  967.9 34.0 %all-gather.24.cloned.1.call-done = bf16[256,3072]{1,0:T(8,128)(2,1)} async-done(((bf16[32,3072]{1,0:T(8,128)(2,1)}), bf16[256,3072]{1,0:T(8,128)(2,1)}) %all-gather.24.cloned.1.call-update) | async-done | bytes 1572880 | tf_op jit(solution)/shard_map/all_gather | solution.py:374
  1001.9 3.4 convert_element_type.216
  1005.3 47.4 %all-gather.26.cloned.1.call-done = bf16[256,4096]{1,0:T(8,128)(2,1)} async-done(((bf16[32,4096]{1,0:T(8,128)(2,1)}), bf16[256,4096]{1,0:T(8,128)(2,1)}) %all-gather.26.cloned.1.call-update) | async-done | bytes 2097168 | tf_op jit(solution)/shard_map/all_gather | solution.py:374
  1052.7 4.1 convert_element_type.222
  1056.8 36.5 %all-gather.22.cloned.1.call-done = bf16[512,1024]{1,0:T(8,128)(2,1)} async-done(((bf16[64,1024]{1,0:T(8,128)(2,1)}), bf16[512,1024]{1,0:T(8,128)(2,1)}) %all-gather.22.cloned.1.call-update) | async-done | bytes 1048592 | tf_op jit(solution)/shard_map/all_gather | solution.py:374
  1093.4 2.8 convert_element_type.213
  (248 shorter events, 103.3 us)
Async XLA Ops:
  7.2 282.7 %copy-start = (bf16[1024,1024]{1,0:T(8,128)(2,1)S(1)}, bf16[1024,1024]{1,0:T(8,128)(2,1)}, u32[]{:S(2)}) copy-start(bf16[1024,1024]{1,0:T(8,128)(2,1)} %param.20) | copy-start | bytes 6291460
  7.2 7.5 copy-start.39
  10.5 16.7 %all-to-all-start = ((bf16[128,4,512]{0,2,1:T(8,128)(2,1)}), bf16[128,4,512]{0,2,1:T(8,128)(2,1)S(1)}, u32[]{:S(2)}, u32[]{:S(2)}) async-start(bf16[128,4,512]{0,2,1:T(8,128)(2,1)} %pad_maximum_fusion.2), calls=%async_computation | async-start | bytes 1048576 | tf_op jit(solution)/shard_map/all_to_all | solution.py:424
  14.7 33.6 %reduce-scatter.18.cloned.1.call-start = ((), (), s32[]{:S(2)}) async-start(), calls=%async_computation.20 | async-start | bytes 327680 | tf_op jit(solution)/shard_map/reduce_scatter | solution.py:433
  27.1 49.4 %reduce-scatter.16.cloned.1.call-start = ((), (), s32[]{:S(2)}) async-start(), calls=%async_computation.19 | async-start | bytes 1310720 | tf_op jit(solution)/shard_map/reduce_scatter | solution.py:368
  27.4 3.5 copy-start.16
  27.4 3.2 copy-start.40
  30.5 88.4 %all-gather.14.cloned.1.call-start = ((), (), s32[]{:S(2)}) async-start(), calls=%async_computation.21 | async-start | bytes 1310720 | tf_op jit(solution)/shard_map/all_gather | solution.py:374
  30.9 52.4 %copy-start.36 = (s32[128]{0:T(128)}, s32[128]{0:T(128)S(1)}, u32[]{:S(2)}) copy-start(s32[128]{0:T(128)S(1)} %convert_reduce_fusion.3) | copy-start | bytes 1540
  77.6 5.7 copy-start.27
  78.7 4.5 copy-start.30
  85.9 28.8 %all-to-all-start.1 = ((bf16[256,3,4,256]{0,3,1,2:T(8,128)(2,1)}), bf16[256,3,4,256]{0,3,1,2:T(8,128)(2,1)}, u32[]{:S(2)}, u32[]{:S(2)}) async-start(bf16[256,3,4,256]{0,3,1,2:T(8,128)(2,1)} %copy.153), calls=%async_computation.3 | async-start | bytes 3145728 | tf_op jit(solution)/shard_map/all_to_all | solution.py:409
  114.1 4.8 copy-start.38
  134.5 11.5 %copy-start.21 = (s32[4,1,8]{2,1,0:T(1,128)S(1)}, s32[4,1,8]{2,1,0:T(1,128)}, u32[]{:S(2)}) copy-start(s32[4,1,8]{2,1,0:T(1,128)} %copy-done.20) | copy-start | bytes 388
  140.2 26.2 %all-to-all-start.2 = ((bf16[8,128,384]{1,2,0:T(8,128)(2,1)}), bf16[8,128,384]{1,2,0:T(8,128)(2,1)}, u32[]{:S(2)}, u32[]{:S(2)}) async-start(bf16[8,128,384]{1,2,0:T(8,128)(2,1)} %bitcast.218), calls=%async_computation.4 | async-start | bytes 1572864 | tf_op jit(solution)/shard_map/all_to_all | solution.py:467
  145.7 83.9 %reduce-scatter.20.cloned.1.call-start = ((), (), s32[]{:S(2)}) async-start(), calls=%async_computation.22 | async-start | bytes 1310720 | tf_op jit(solution)/shard_map/reduce_scatter | solution.py:368
  174.4 12.7 %copy-start.7 = (bf16[1024,128]{0,1:T(8,128)(2,1)}, bf16[1024,128]{0,1:T(8,128)(2,1)S(1)}, u32[]{:S(2)}) copy-start(bf16[1024,128]{0,1:T(8,128)(2,1)S(1)} %copy.161) | copy-start | bytes 786436
  182.4 4.7 copy-start.29
  187.1 2.2 copy-start.1
  190.2 16.4 %copy-start.41 = (bf16[256]{0:T(256)(128)(2,1)S(1)}, bf16[256]{0:T(256)(128)(2,1)}, u32[]{:S(2)}) copy-start(bf16[256]{0:T(256)(128)(2,1)} %param.18) | copy-start | bytes 1540
  190.2 39.4 %copy-start.3 = (bf16[128,1024]{1,0:T(8,128)(2,1)S(1)}, bf16[128,1024]{1,0:T(8,128)(2,1)}, u32[]{:S(2)}) copy-start(bf16[128,1024]{1,0:T(8,128)(2,1)} %reduce-scatter.16.cloned.1.call-done) | copy-start | bytes 786436
  206.6 74.8 %all-gather.16.cloned.1.call-start = ((), (), s32[]{:S(2)}) async-start(), calls=%async_computation.23 | async-start | bytes 1310720 | tf_op jit(solution)/shard_map/all_gather | solution.py:374
  211.7 112.9 %copy-start.18 = (f32[4,1,256]{2,1,0:T(1,128)}, f32[4,1,256]{2,1,0:T(1,128)S(1)}, u32[]{:S(2)}) copy-start(f32[4,1,256]{2,1,0:T(1,128)S(1)} %convert_element_type.230) | copy-start | bytes 12292
  230.8 93.9 %copy-start.23 = (f32[128]{0:T(128)}, f32[128]{0:T(128)S(1)}, u32[]{:S(2)}) copy-start(f32[128]{0:T(128)S(1)} %broadcast_multiply_fusion.4) | copy-start | bytes 1540
  232.0 92.7 %copy-start.25 = (f32[128]{0:T(128)}, f32[128]{0:T(128)S(1)}, u32[]{:S(2)}) copy-start(f32[128]{0:T(128)S(1)} %add_rsqrt_fusion) | copy-start | bytes 1540
  237.9 39.5 %all-to-all-start.4 = ((bf16[256,4,1024]{0,2,1:T(8,128)(2,1)}), bf16[256,4,1024]{0,2,1:T(8,128)(2,1)}, u32[]{:S(2)}, u32[]{:S(2)}) async-start(bf16[256,4,1024]{0,2,1:T(8,128)(2,1)} %bitcast.212), calls=%async_computation.7 | async-start | bytes 4194304 | tf_op jit(solution)/shard_map/all_to_all | solution.py:412
  242.4 47.5 %all-gather.30.cloned.1.call-start = ((), (), s32[]{:S(2)}) async-start(), calls=%async_computation.37 | async-start | bytes 1310720 | tf_op jit(solution)/shard_map/all_gather | solution.py:374
  243.0 79.7 %reduce-scatter.24.cloned.1.call-start = ((), (), s32[]{:S(2)}) async-start(), calls=%async_computation.25 | async-start | bytes 1310720 | tf_op jit(solution)/shard_map/reduce_scatter | solution.py:368
  289.9 5.5 copy-start.11
  297.7 46.0 %all-gather.18.cloned.1.call-start = ((), (), s32[]{:S(2)}) async-start(), calls=%async_computation.26 | async-start | bytes 1310720 | tf_op jit(solution)/shard_map/all_gather | solution.py:374
  324.6 25.1 %copy-start.32 = (f32[128]{0:T(128)}, f32[128]{0:T(128)S(1)}, u32[]{:S(2)}) copy-start(f32[128]{0:T(128)S(1)} %broadcast_multiply_fusion.2) | copy-start | bytes 1540
  324.7 25.1 %copy-start.34 = (f32[128]{0:T(128)}, f32[128]{0:T(128)S(1)}, u32[]{:S(2)}) copy-start(f32[128]{0:T(128)S(1)} %broadcast_multiply_fusion.3) | copy-start | bytes 1540
  349.7 14.9 %all-to-all-start.5 = ((bf16[8,128,128]{1,2,0:T(8,128)(2,1)}), bf16[8,128,128]{1,2,0:T(8,128)(2,1)}, u32[]{:S(2)}, u32[]{:S(2)}) async-start(bf16[8,128,128]{1,2,0:T(8,128)(2,1)} %bitcast.242), calls=%async_computation.10 | async-start | bytes 524288 | tf_op jit(solution)/shard_map/all_to_all | solution.py:467
  355.3 81.3 %reduce-scatter.26.cloned.1.call-start = ((), (), s32[]{:S(2)}) async-start(), calls=%async_computation.27 | async-start | bytes 1310720 | tf_op jit(solution)/shard_map/reduce_scatter | solution.py:368
  369.5 4.9 copy-start.13
  375.8 2.2 copy-start.2
  375.8 2.2 copy-start.8
  413.4 51.1 %reduce-scatter.22.cloned.1.call-start = ((), (), s32[]{:S(2)}) async-start(), calls=%async_computation.24 | async-start | bytes 1310720 | tf_op jit(solution)/shard_map/reduce_scatter | solution.py:368
  413.5 23.1 %copy-start.28 = (f32[128]{0:T(128)S(1)}, f32[128]{0:T(128)}, u32[]{:S(2)}) copy-start(f32[128]{0:T(128)} %copy-done.27) | copy-start | bytes 1540
  413.5 23.1 %copy-start.31 = (f32[128]{0:T(128)S(1)}, f32[128]{0:T(128)}, u32[]{:S(2)}) copy-start(f32[128]{0:T(128)} %copy-done.30) | copy-start | bytes 1540
  416.9 47.6 %copy-start.19 = (f32[4,1,256]{2,1,0:T(1,128)S(1)}, f32[4,1,256]{2,1,0:T(1,128)}, u32[]{:S(2)}) copy-start(f32[4,1,256]{2,1,0:T(1,128)} %copy-done.18) | copy-start | bytes 12292
  416.9 47.6 %copy-start.24 = (f32[128]{0:T(128)S(1)}, f32[128]{0:T(128)}, u32[]{:S(2)}) copy-start(f32[128]{0:T(128)} %copy-done.23) | copy-start | bytes 1540
  416.9 47.6 %copy-start.26 = (f32[128]{0:T(128)S(1)}, f32[128]{0:T(128)}, u32[]{:S(2)}) copy-start(f32[128]{0:T(128)} %copy-done.25) | copy-start | bytes 1540
  416.9 47.6 %copy-start.33 = (f32[128]{0:T(128)S(1)}, f32[128]{0:T(128)}, u32[]{:S(2)}) copy-start(f32[128]{0:T(128)} %copy-done.32) | copy-start | bytes 1540
  417.0 47.6 %copy-start.35 = (f32[128]{0:T(128)S(1)}, f32[128]{0:T(128)}, u32[]{:S(2)}) copy-start(f32[128]{0:T(128)} %copy-done.34) | copy-start | bytes 1540
  417.0 67.0 %all-gather.20.cloned.1.call-start = ((), (), s32[]{:S(2)}) async-start(), calls=%async_computation.28 | async-start | bytes 1310720 | tf_op jit(solution)/shard_map/all_gather | solution.py:374
  467.1 88.6 %reduce-scatter.32.cloned.1.call-start = ((), (), s32[]{:S(2)}) async-start(), calls=%async_computation.35 | async-start | bytes 2359296 | tf_op jit(solution)/shard_map/reduce_scatter | solution.py:526
  471.3 231.2 %all-reduce.9.cloned.1.call-start = ((), (), s32[]{:S(2)}) async-start(), calls=%async_computation.38 | async-start | bytes 7340032
  473.9 4.4 copy-start.4
  483.1 4.0 copy-start.6
  483.1 285.7 %reduce-scatter.28.cloned.1.call-start = ((), (), s32[]{:S(2)}) async-start(), calls=%async_computation.29 | async-start | bytes 1179648 | tf_op jit(solution)/shard_map/reduce_scatter | solution.py:526
  487.1 2.7 copy-start.9
  487.1 2.8 copy-start.12
  487.1 2.8 copy-start.37
  487.1 68.7 %copy-start.43 = (u32[32]{0:T(128)S(1)}, u32[32]{0:T(128)}, u32[]{:S(2)}) copy-start(u32[32]{0:T(128)} %constant.149) | copy-start | bytes 388
  487.1 346.8 %reduce-scatter.30.cloned.1.call-start = ((), (), s32[]{:S(2)}) async-start(), calls=%async_computation.33 | async-start | bytes 589824 | tf_op jit(solution)/shard_map/reduce_scatter | solution.py:526
  489.7 415.6 %all-reduce.7.cloned.1.call-start = ((), (), s32[]{:S(2)}) async-start(), calls=%async_computation.31 | async-start | bytes 131072 | tf_op jit(solution)/shard_map/psum | solution.py:578
  491.0 465.6 %all-gather.28.cloned.1.call-start = ((), (), s32[]{:S(2)}) async-start(), calls=%async_computation.36 | async-start | bytes 2359296 | tf_op jit(solution)/shard_map/all_gather | solution.py:374
  555.8 446.1 %all-gather.24.cloned.1.call-start = ((), (), s32[]{:S(2)}) async-start(), calls=%async_computation.32 | async-start | bytes 1769472 | tf_op jit(solution)/shard_map/all_gather | solution.py:374
  704.2 64.6 %copy-start.42 = (u32[32]{0:T(128)S(1)}, u32[32]{0:T(128)}, u32[]{:S(2)}) copy-start(u32[32]{0:T(128)} %constant.153) | copy-start | bytes 388
  704.3 65.8 %copy-start.22 = (f32[1024]{0:T(1024)S(1)}, f32[1024]{0:T(1024)}, u32[]{:S(2)}) copy-start(f32[1024]{0:T(1024)} %get-tuple-element.32) | copy-start | bytes 12292
  713.2 339.6 %all-gather.26.cloned.1.call-start = ((), (), s32[]{:S(2)}) async-start(), calls=%async_computation.34 | async-start | bytes 2359296 | tf_op jit(solution)/shard_map/all_gather | solution.py:374
  724.3 369.1 %all-gather.22.cloned.1.call-start = ((), (), s32[]{:S(2)}) async-start(), calls=%async_computation.30 | async-start | bytes 1179648 | tf_op jit(solution)/shard_map/all_gather | solution.py:374
  799.0 161.7 %all-to-all-start.7 = ((bf16[4,128,1,512]{3,1,2,0:T(8,128)(2,1)}), bf16[4,128,1,512]{3,1,2,0:T(8,128)(2,1)S(1)}, u32[]{:S(2)}, u32[]{:S(2)}) async-start(bf16[4,128,1,512]{3,1,2,0:T(8,128)(2,1)} %bitcast.49), calls=%async_computation.13 | async-start | bytes 1048576 | tf_op jit(solution)/shard_map/all_to_all | solution.py:586
  (7 other events, 7.3 us)
Sparse Core Ops, SparseCore 0:
  27.2 21.0 reduce-scatter.17
  51.5 24.8 reduce-scatter.15
  80.8 19.3 all-gather.13
  206.7 22.9 reduce-scatter.19
  233.9 20.3 all-gather.15
  255.8 22.7 all-gather.29
  297.8 24.8 reduce-scatter.23
  326.9 16.7 all-gather.17
  413.5 22.9 reduce-scatter.25
  439.6 24.8 reduce-scatter.21
  467.2 16.7 all-gather.19
  488.0 67.7 reduce-scatter.31
  560.1 142.4 all-reduce.8
  706.4 62.3 reduce-scatter.27
  773.0 60.9 reduce-scatter.29
  837.8 67.5 all-reduce.6
  907.3 49.2 all-gather.27
  959.2 42.6 all-gather.23
  1004.6 48.0 all-gather.25
  1054.7 38.6 all-gather.21

commit v2 on v1

--- a/solution.py
+++ b/solution.py
@@ -3,6 +3,8 @@
 import jax
 import jax.numpy as jnp
 from jax import lax
+from jax.experimental import pallas as pl
+from jax.experimental.pallas import tpu as pltpu
 from jax.sharding import PartitionSpec as P
 
 HEADS = 16
@@ -13,6 +15,8 @@
 EPSILON = 1e-06
 NEGATIVE = -1e30
 HIGHEST = lax.Precision.HIGHEST
+MESH = pl.DeviceIdType.MESH
+RING = 8
 
 
 def from_behind(block, axis, distance):
@@ -374,6 +378,167 @@
     return lax.all_gather(block, axis, axis=0, tiled=True)
 
 
+def ring_place(rank):
+    odd = lax.rem(rank, 2)
+    return (1 - odd) * (rank // 2) + odd * ((15 - rank) // 2)
+
+
+def ring_rank(place):
+    upper = place // 4
+    return (1 - upper) * (2 * place) + upper * (15 - 2 * place)
+
+
+class Ring:
+    def __init__(self, part, land, done, sems, rank, group_rank):
+        self.part, self.land, self.done = part, land, done
+        self.sems = sems
+        self.place = ring_place(rank)
+        self.group_rank = group_rank
+        self.half = part.shape[1] // 2
+        self.copies = {}
+
+    def block_at(self, offset):
+        return ring_rank(lax.rem(self.place + offset + 2 * RING, RING))
+
+    def rows(self, way):
+        return pl.ds(way * self.half, self.half)
+
+    def send(self, kind, step, way, source, target):
+        to = ring_rank(lax.rem(self.place + (1 if way == 0 else RING - 1), RING))
+        copy = pltpu.make_async_remote_copy(
+            src_ref=source,
+            dst_ref=target,
+            send_sem=self.sems.at[kind, 0, way, step],
+            recv_sem=self.sems.at[kind, 1, way, step],
+            device_id=(to, self.group_rank),
+            device_id_type=MESH,
+        )
+        copy.start()
+        self.copies[kind, step, way] = copy
+
+    def sum_step(self, step, way):
+        sign = -1 if way == 0 else 1
+        block = self.block_at(sign * (step + 1))
+        rows = self.rows(way)
+        if step > 0:
+            self.copies[0, step - 1, way].wait_recv()
+            tile = min(self.half, 32)
+
+            def add(i, carry):
+                at = pl.ds(pl.multiple_of(way * self.half + i * tile, tile), tile)
+                total = self.part[block, at].astype(jnp.float32) + self.land[
+                    step - 1, at
+                ].astype(jnp.float32)
+                self.land[step - 1, at] = total.astype(jnp.bfloat16)
+                return carry
+
+            lax.fori_loop(0, self.half // tile, add, 0)
+        if step < RING - 1:
+            source = self.part.at[block, rows] if step == 0 else self.land.at[step - 1, rows]
+            self.send(0, step, way, source, self.land.at[step, rows])
+
+    def spread_step(self, step, way):
+        sign = -1 if way == 0 else 1
+        block = self.block_at(sign * step)
+        rows = self.rows(way)
+        if step > 0:
+            self.copies[1, step - 1, way].wait_recv()
+        if step < RING - 1:
+            self.send(1, step, way, self.done.at[block, rows], self.done.at[block, rows])
+
+    def finish(self):
+        for copy in self.copies.values():
+            copy.wait_send()
+
+
+def gradient_kernel(
+    down_ref, up_ref, qkv_ref, skip_ref, out_ref,
+    down_done, up_done, qkv_done, skip_done, out_done,
+    down_land, up_land, qkv_land, skip_land, out_land,
+    down_sem, up_sem, qkv_sem, skip_sem, out_sem,
+    turn_sem,
+):
+    rank, group_rank = lax.axis_index("blk"), lax.axis_index("grp")
+    rows = 4
+    place = ring_place(rank)
+    barrier = pltpu.get_barrier_semaphore()
+    for step in (1, RING - 1):
+        pl.semaphore_signal(
+            barrier,
+            inc=1,
+            device_id=(ring_rank(lax.rem(place + step, RING)), group_rank),
+            device_id_type=MESH,
+        )
+    for other in range(1, rows):
+        pl.semaphore_signal(
+            barrier,
+            inc=1,
+            device_id=(rank, lax.rem(group_rank + other, rows)),
+            device_id_type=MESH,
+        )
+    pl.semaphore_wait(barrier, 2 + rows - 1)
+
+    rings = [
+        Ring(down_ref, down_land, down_done, down_sem, rank, group_rank),
+        Ring(up_ref, up_land, up_done, up_sem, rank, group_rank),
+        Ring(qkv_ref, qkv_land, qkv_done, qkv_sem, rank, group_rank),
+        Ring(skip_ref, skip_land, skip_done, skip_sem, rank, group_rank),
+        Ring(out_ref, out_land, out_done, out_sem, rank, group_rank),
+    ]
+    for step in range(RING):
+        for ring in rings:
+            for way in range(2):
+                ring.sum_step(step, way)
+    turned = []
+    for index, ring in enumerate(rings[1:3]):
+        deep = ring.part.shape[1] // rows
+        for other in range(1, rows):
+            target = lax.rem(group_rank + other, rows)
+            copy = pltpu.make_async_remote_copy(
+                src_ref=ring.land.at[RING - 2, pl.ds(pl.multiple_of(target * deep, deep), deep)],
+                dst_ref=ring.done.at[rank, pl.ds(pl.multiple_of(group_rank * deep, deep), deep)],
+                send_sem=turn_sem.at[index, 0, other - 1],
+                recv_sem=turn_sem.at[index, 1, other - 1],
+                device_id=(rank, target),
+                device_id_type=MESH,
+            )
+            copy.start()
+            turned.append(copy)
+        mine = pl.ds(pl.multiple_of(group_rank * deep, deep), deep)
+        ring.done[rank, mine] = ring.land[RING - 2, mine]
+    for ring in (rings[0], rings[3], rings[4]):
+        ring.done[rank] = ring.land[RING - 2]
+    for copy in turned:
+        copy.wait_recv()
+    for step in range(RING):
+        for ring in rings:
+            for way in range(2):
+                ring.spread_step(step, way)
+    for ring in rings:
+        ring.finish()
+    for copy in turned:
+        copy.wait_send()
+
+
+def sum_gradients(down, up, qkv, skip, out):
+    parts = (down, up, qkv, skip, out)
+    vmem = pl.BlockSpec(memory_space=pltpu.VMEM)
+    return pl.pallas_call(
+        gradient_kernel,
+        out_shape=[jax.ShapeDtypeStruct(part.shape, jnp.bfloat16) for part in parts],
+        in_specs=[vmem] * 5,
+        out_specs=[vmem] * 5,
+        scratch_shapes=[
+            pltpu.VMEM((RING - 1,) + part.shape[1:], jnp.bfloat16) for part in parts
+        ]
+        + [pltpu.SemaphoreType.DMA((2, 2, 2, RING - 1))] * 5
+        + [pltpu.SemaphoreType.DMA((2, 2, 3))],
+        compiler_params=pltpu.CompilerParams(
+            collective_id=0, has_side_effects=True, vmem_limit_bytes=56 * 1024 * 1024
+        ),
+    )(*parts)
+
+
 def per_device_shards(
     inputs,
     skipped,
@@ -522,27 +687,20 @@
         grad_ff_in * gain_vector, normal_two, spread_two
     )
 
-    def over_blocks(grad):
-        shard = lax.psum_scatter(
-            grad.astype(jnp.bfloat16), "blk", scatter_dimension=0, tiled=True
-        )
-        return gathered(shard, "blk").astype(jnp.float32)
-
-    def over_blocks_columns(grad, kinds):
-        wide = grad.shape[1] // kinds
-        grad = grad.reshape(rows, blocks, columns_here // blocks, grad.shape[1])
-        grad = jnp.transpose(grad, (1, 0, 2, 3)).astype(jnp.bfloat16)
-        shard = lax.psum_scatter(grad, "blk", scatter_dimension=0, tiled=True)[0]
-        shard = lax.all_to_all(
-            shard.reshape(rows, columns_here // blocks, kinds, 1, wide), "grp", 0, 3, tiled=True
-        )
-        return gathered(shard.reshape(columns_here // blocks, -1), "blk").astype(jnp.float32)
-
-    total_down = over_blocks(grad_down)
-    total_up = over_blocks_columns(grad_up, 1)
+    def blocked(grad):
+        return grad.astype(jnp.bfloat16).reshape(blocks, -1, grad.shape[1])
+
+    def blocked_columns(grad):
+        grad = grad.astype(jnp.bfloat16).reshape(rows, blocks, columns_here // blocks, -1)
+        return jnp.transpose(grad, (1, 0, 2, 3)).reshape(
+            blocks, model_width // blocks, grad.shape[3]
+        )
+
+    part_down = blocked(grad_down)
+    part_up = blocked_columns(grad_up)
 
     grad_two_low = gathered(grad_hidden_two.astype(jnp.bfloat16))
-    total_out = over_blocks(contract_rows(attended_here, grad_two_low))
+    part_out = blocked(contract_rows(attended_here, grad_two_low))
     grad_attended = heads_of_block(
         to_pairs(dot_columns(grad_two_low, w_out).astype(jnp.bfloat16), 1)
     )
@@ -571,7 +729,7 @@
         axis=1,
     ).astype(jnp.bfloat16)
     grad_project = from_pairs(grad_paired, 3)
-    total_qkv = over_blocks_columns(contract_rows(attn_in, grad_project), 3)
+    part_qkv = blocked_columns(contract_rows(attn_in, grad_project))
     grad_attn_in = summed_rows(dot_columns(grad_project, w_qkv_here))
 
     mod_terms = jnp.concatenate([grad_attn_in * normal_one, grad_attn_in], axis=1)
@@ -582,7 +740,7 @@
 
     grad_hidden = grad_hidden_two + norm_back(grad_attn_in * scale_one, normal_one, spread_one)
     grad_hidden_low = gathered(grad_hidden.astype(jnp.bfloat16))
-    total_skip = over_blocks(contract_rows(joined_here, grad_hidden_low))
+    part_skip = blocked(contract_rows(joined_here, grad_hidden_low))
     grad_joined = lax.all_to_all(
         dot_columns(grad_hidden_low, w_skip)
         .astype(jnp.bfloat16)
@@ -595,6 +753,21 @@
     total_gain = lax.psum_scatter(
         lax.psum(grad_gain, "blk"), "grp", scatter_dimension=0, tiled=True
     )
+    total_down, total_up, total_qkv, total_skip, total_out = sum_gradients(
+        part_down, part_up, part_qkv, part_skip, part_out
+    )
+
+    def columns_back(total, kinds):
+        total = total.astype(jnp.float32).reshape(
+            blocks, rows, columns_here // blocks, kinds, total.shape[2] // kinds
+        )
+        return jnp.transpose(total, (0, 2, 3, 1, 4)).reshape(columns_here, -1)
+
+    def rows_back(total):
+        return total.astype(jnp.float32).reshape(-1, total.shape[2])
+
+    total_down, total_skip, total_out = map(rows_back, (total_down, total_skip, total_out))
+    total_up, total_qkv = columns_back(total_up, 1), columns_back(total_qkv, 3)
     return (
         output[None],
         grad_joined[:, :model_width][None],
@@ -626,7 +799,7 @@
     )
     rows, blocks = mesh.shape["grp"], mesh.shape["blk"]
     body = per_device
-    if blocks % rows == 0 and HEADS % blocks == 0:
+    if blocks == RING and rows == 4:
         body = per_device_shards
     return jax.shard_map(
         body,

time: 1110 us -> 780 us (0.70)
  waiting for transfers between devices: 697 us -> 246 us
  Pallas kernels: 0 us -> 159 us
  blocking collectives: 155 us -> 109 us
  local copies, waits for them, and re-layouts: 76.9 us -> 95.1 us
    pallas_call x0 -> x1, Pallas kernels: none -> 159 us  [sum_gradients(): pl.pallas_call(gradient_kernel, out_shape=[jax.ShapeDtypeStruct(part.shap...]
    all_gather x9 -> x5, waiting for transfers between devices: 179 us -> 27.2 us  [gathered(): return lax.all_gather(block, axis, axis=0, tiled=True)]
    unnamed x21 -> x12, waiting for transfers between devices: 147 us -> 0.7 us
    reduce_scatter x3 -> x0, waiting for transfers between devices: 141 us -> none  [over_blocks(): lax.psum_scatter(grad.astype(jnp.bfloat16), 'blk', scatter_dimension=0, t...]
    all_gather x5 -> x4, blocking collectives: 76.1 us -> 44.3 us  [gathered(): return lax.all_gather(block, axis, axis=0, tiled=True)]
    reshape x2 -> x6, local copies, waits for them, and re-layouts: 3.85 us -> 24.2 us  [the longest x4 21.5 us: columns_back(): return jnp.transpose(total, (0, 2, 3, 1, 4)).reshape(columns_here, -1)]
    all_to_all x2 -> x0, blocking collectives: 16.3 us -> none  [over_blocks_columns(): lax.all_to_all(shard.reshape(rows, columns_here // blocks, kinds, 1, wide...]
    convert_element_type x5 -> x0, other arithmetic: 15.5 us -> none  [the longest x3 7.94 us: over_blocks(): return gathered(shard, 'blk').astype(jnp.float32)]
  transfers between devices with their start and end apart: 26 -> 18, of which waited for: 20 -> 12; matrix products, arithmetic and copies ran while one was open for 9% -> 12% of each run, Pallas kernels for 0% -> 0%
where the time goes in v2:
time: 780 us; the launch traced here: 771 us
  waiting for transfers between devices  246 us (32%)
  Pallas kernels  159 us (20%)
  blocking collectives  109 us (14%)
  local copies, waits for them, and re-layouts  95.1 us (12%)
  matrix products  72.7 us (9%)
  other arithmetic  44.3 us (6%)
  starting transfers between devices  29.5 us (4%)
  between operations  15.8 us (2%)
    pallas_call x1, Pallas kernels, sum_gradients(): pl.pallas_call(gradient_kernel, out_shape=[jax.ShapeDtypeStruct(part.shap...  159 us
    reduce_scatter x5, waiting for transfers between devices, summed_rows(): lax.psum_scatter(partial.astype(jnp.bfloat16), axis, scatter_dimension=0,...  112 us
    all_gather x4, blocking collectives, gathered(): return lax.all_gather(block, axis, axis=0, tiled=True)  44.3 us
    all_to_all x2, blocking collectives, from_pairs(): lax.all_to_all(block.reshape(blocks, frame_count, kinds * pair_columns),...  36.5 us
    all_to_all x1, waiting for transfers between devices, per_device_shards(): lax.all_to_all(w_up.reshape(columns_here, rows, -1), 'grp', 1, 0, tiled=T...  34.2 us
    psum x1, waiting for transfers between devices, per_device_shards(): lax.psum(jnp.dot(picker.T, mod_terms, precision=HIGHEST), 'blk')  29.3 us
    all_gather x5, waiting for transfers between devices, gathered(): return lax.all_gather(block, axis, axis=0, tiled=True)  27.2 us
    all_to_all x2, waiting for transfers between devices, to_pairs(): lax.all_to_all(block, 'blk', 0, 0, tiled=True)  25.5 us
  transfers between devices with their start and end apart: 18, of which 12 were waited for; matrix products, arithmetic and copies ran while one was open for 12% of the time, Pallas kernels for 0%

profile of v2, /device:TPU:0, one launch (start us, length us, event | category | flops | bytes accessed | tf_op | source)
XLA Modules:
  0.0 770.9 jit_solution(14040067018174437108)
XLA Ops:
  10.5 4.2 all-to-all-start
  14.7 9.7 %all-gather.1 = s32[4,1,8]{2,1,0:T(1,128)S(1)} all-gather(s32[1,1,8]{2,1,0:T(1,128)S(1)} %bitcast.259), channel_id=1, replica_groups=mesh['blk'=8,'grp'=4] {'grp'}, dimensions={0}, use_global_device_ids=true | all-gather | bytes 160 | tf_op jit(solution)/shard_map/all_gather | solution.py:378
  24.9 2.2 fusion.70
  27.4 3.1 convolution_convert_fusion.8
  30.9 17.4 %reduce-scatter.9.cloned.1.call-done = f32[8,2048]{1,0:T(8,128)} async-done(((f32[32,2048]{1,0:T(8,128)}), f32[8,2048]{1,0:T(8,128)}) %reduce-scatter.9.cloned.1.call-update) | async-done | bytes 65552 | tf_op jit(solution)/shard_map/reduce_scatter | solution.py:598
  49.7 26.7 %reduce-scatter.7.cloned.1.call-done = bf16[128,1024]{1,0:T(8,128)(2,1)} async-done(((bf16[512,1024]{1,0:T(8,128)(2,1)}), bf16[128,1024]{1,0:T(8,128)(2,1)}) %reduce-scatter.7.cloned.1.call-update) | async-done | bytes 262160 | tf_op jit(solution)/shard_map/reduce_scatter | solution.py:372
  80.7 2.6 copy.155
  83.3 2.7 copy.156
  85.9 4.4 all-to-all-start.1
  90.3 23.5 %all-gather.2 = s32[4,1,8]{2,1,0:T(1,128)S(1)} all-gather(s32[1,1,8]{2,1,0:T(1,128)S(1)} %bitcast.261), channel_id=1, replica_groups=mesh['blk'=8,'grp'=4] {'grp'}, dimensions={0}, use_global_device_ids=true | all-gather | bytes 160 | tf_op jit(solution)/shard_map/all_gather | solution.py:378
  114.9 2.6 copy.157
  119.0 2.7 fusion.71
  134.6 2.7 convert_element_type.164
  137.4 3.0 copy.162
  140.3 5.5 all-to-all-start.2
  148.3 18.3 %all-to-all-done.2 = bf16[8,128,384]{1,2,0:T(8,128)(2,1)} async-done(((bf16[8,128,384]{1,2,0:T(8,128)(2,1)}), bf16[8,128,384]{1,2,0:T(8,128)(2,1)}, u32[]{:S(2)}, u32[]{:S(2)}) %all-to-all-start.2) | async-done | bytes 786464 | tf_op jit(solution)/shard_map/all_to_all | solution.py:632
  166.6 2.3 copy.163
  174.6 8.0 %fusion.68 = (f32[2,1024]{1,0:T(2,128)S(1)}, f32[2,1024,1024]{1,2,0:T(8,128)}) fusion(pred[1024,1024]{0,1:T(8,128)(4,1)} %broadcast_compare_fusion, bf16[1024,2,64]{0,2,1:T(8,128)(2,1)} %bitcast.232, bf16[1024,2,64]{0,2,1:T(8,128)(2,1)} %bitcast.217), kind=kOutput, calls=%fused_computation.164 | convolution fusion | flops 276825088 | bytes 9969664 | tf_op jit(solution)/shard_map/sub | solution.py:663
  182.5 4.6 fusion.5
  187.2 2.2 fusion.69
  190.3 12.9 %all_to_all.74 = bf16[8,128,128]{2,1,0:T(8,128)(2,1)S(1)} all-to-all(bf16[8,128,128]{2,1,0:T(8,128)(2,1)} %copy.168), channel_id=1, replica_groups=mesh['blk'=8,'grp'=4] {'blk'}, dimensions={0} | all-to-all | bytes 524288 | tf_op jit(solution)/shard_map/all_to_all | solution.py:637
  204.2 2.5 convolution_convert_fusion.6
  206.7 5.1 all-gather.3
  211.8 18.0 %reduce-scatter.11.cloned.1.call-done = bf16[128,1024]{1,0:T(8,128)(2,1)} async-done(((bf16[512,1024]{1,0:T(8,128)(2,1)}), bf16[128,1024]{1,0:T(8,128)(2,1)}) %reduce-scatter.11.cloned.1.call-update) | async-done | bytes 262160 | tf_op jit(solution)/shard_map/reduce_scatter | solution.py:372
  233.9 4.1 copy.170
  238.0 4.5 all-to-all-start.4
  243.3 34.2 %all-to-all-done.4 = bf16[256,4,1024]{0,2,1:T(8,128)(2,1)} async-done(((bf16[256,4,1024]{0,2,1:T(8,128)(2,1)}), bf16[256,4,1024]{0,2,1:T(8,128)(2,1)}, u32[]{:S(2)}, u32[]{:S(2)}) %all-to-all-start.4) | async-done | bytes 2097184 | tf_op jit(solution)/shard_map/all_to_all | solution.py:577
  277.5 3.9 copy.171
  281.4 8.5 %multiply_convert_fusion.1 = (bf16[512,1024]{1,0:T(8,128)(2,1)}, f32[512,1024]{1,0:T(8,128)}, f32[512,1024]{1,0:T(8,128)}) fusion(bf16[512,1024]{1,0:T(8,128)(2,1)} %all-gather.12.cloned.1.call-done, bf16[1024,1024]{1,0:T(8,128)(2,1)} %bitcast.222), kind=kOutput, calls=%fused_computation.15 | convolution fusion | flops 1107820544 | bytes 8388608 | tf_op jit(solution)/shard_map/dot_general | solution.py:362
  290.0 4.5 add_convert_fusion
  295.5 2.3 convolution_convert_fusion.4
  297.8 25.0 %reduce-scatter.15.cloned.1.call-done = bf16[128,1024]{1,0:T(8,128)(2,1)} async-done(((bf16[512,1024]{1,0:T(8,128)(2,1)}), bf16[128,1024]{1,0:T(8,128)(2,1)}) %reduce-scatter.15.cloned.1.call-update) | async-done | bytes 262160 | tf_op jit(solution)/shard_map/reduce_scatter | solution.py:372
  326.9 16.9 %all-gather.14.cloned.1.call-done = bf16[512,1024]{1,0:T(8,128)(2,1)} async-done(((bf16[128,1024]{1,0:T(8,128)(2,1)}), bf16[512,1024]{1,0:T(8,128)(2,1)}) %all-gather.14.cloned.1.call-update) | async-done | bytes 1048592 | tf_op jit(solution)/shard_map/all_gather | solution.py:378
  343.8 2.5 convolution_convert_fusion.12
  349.8 5.5 all-to-all-start.5
  357.6 7.2 all-to-all-done.5
  369.6 4.9 multiply_convert_fusion
  380.1 23.6 %all_to_all.75 = bf16[8,128,384]{1,2,0:T(8,128)(2,1)} all-to-all(bf16[8,128,384]{1,2,0:T(8,128)(2,1)S(1)} %pad_maximum_fusion.1), channel_id=1, replica_groups=mesh['blk'=8,'grp'=4] {'blk'}, dimensions={0} | all-to-all | bytes 1572864 | tf_op jit(solution)/shard_map/all_to_all | solution.py:637
  403.7 3.0 copy.181
  406.7 3.1 reshape.455
  409.9 3.6 convolution_convert_fusion.3
  413.6 3.5 convolution_convert_fusion.5
  418.4 18.2 %reduce-scatter.17.cloned.1.call-done = bf16[128,1024]{1,0:T(8,128)(2,1)} async-done(((bf16[512,1024]{1,0:T(8,128)(2,1)}), bf16[128,1024]{1,0:T(8,128)(2,1)}) %reduce-scatter.17.cloned.1.call-update) | async-done | bytes 262160 | tf_op jit(solution)/shard_map/reduce_scatter | solution.py:372
  440.5 24.1 %reduce-scatter.13.cloned.1.call-done = bf16[128,1024]{1,0:T(8,128)(2,1)} async-done(((bf16[512,1024]{1,0:T(8,128)(2,1)}), bf16[128,1024]{1,0:T(8,128)(2,1)}) %reduce-scatter.13.cloned.1.call-update) | async-done | bytes 262160 | tf_op jit(solution)/shard_map/reduce_scatter | solution.py:372
  464.7 2.5 fusion.40
  467.2 2.8 convolution_convert_fusion
  472.3 2.6 convolution_convert_fusion.1
  475.0 5.7 all-reduce
  480.8 22.1 %psum.16 = f32[256]{0:T(256)} all-reduce(f32[256]{0:T(256)S(1)} %dynamic-slice.2), channel_id=1, replica_groups=mesh['blk'=8,'grp'=4] {'blk'}, use_global_device_ids=true, to_apply=%region_27.28 | all-reduce | flops 256 | bytes 2048 | tf_op jit(solution)/shard_map/psum | solution.py:754
  504.1 2.5 convolution_convert_fusion.2
  507.9 29.3 %all-reduce.3.cloned.1.call-done = f32[8,2048]{1,0:T(8,128)} async-done(((f32[8,2048]{1,0:T(8,128)}), f32[8,2048]{1,0:T(8,128)}) %all-reduce.3.cloned.1.call-update) | async-done | bytes 65552 | tf_op jit(solution)/shard_map/psum | solution.py:736
  537.2 6.0 all_gather.35
  543.1 2.3 fusion.72
  545.5 10.4 %all-gather.16.cloned.1.call-done = bf16[512,1024]{1,0:T(8,128)(2,1)} async-done(((bf16[128,1024]{1,0:T(8,128)(2,1)}), bf16[512,1024]{1,0:T(8,128)(2,1)}) %all-gather.16.cloned.1.call-update) | async-done | bytes 1048592 | tf_op jit(solution)/shard_map/all_gather | solution.py:378
  555.8 2.9 convolution_convert_fusion.7
  558.8 158.6 %shard_map.195 = (bf16[8,128,1024]{2,1,0:T(8,128)(2,1)}, bf16[8,128,1024]{2,1,0:T(8,128)(2,1)}, bf16[8,128,768]{2,1,0:T(8,128)(2,1)}, bf16[8,64,1024]{2,1,0:T(8,128)(2,1)}, bf16[8,32,1024]{2,1,0:T(8,128)(2,1)}) custom-call(bf16[8,128,1024]{2,1,0:T(8,128)(2,1)} %bitcast.220, bf16[8,128,1024]{2,1,0:T(8,128)(2,1)} %bitcast.202, bf16[8,128,768]{2,1,0:T(8,128)(2,1)} %bitcast.204, ...), custom_call_target="tpu_custom_call" | custom-call | tf_op jit(solution)/shard_map/pallas_call | solution.py:526
  717.4 4.2 convert_bitcast_fusion
  725.4 3.6 all-to-all-start.7
  730.1 4.9 copy.187
  735.1 5.8 copy.201
  740.9 5.6 reshape.491
  746.4 5.9 copy.186
  752.3 5.1 reshape.480
  757.4 4.1 bitcast_convert_fusion
  (221 shorter events, 78.1 us)
Async XLA Ops:
  7.2 282.8 %copy-start = (bf16[1024,1024]{1,0:T(8,128)(2,1)S(1)}, bf16[1024,1024]{1,0:T(8,128)(2,1)}, u32[]{:S(2)}) copy-start(bf16[1024,1024]{1,0:T(8,128)(2,1)} %param.20) | copy-start | bytes 6291460
  7.2 7.5 copy-start.38
  10.5 16.7 %all-to-all-start = ((bf16[128,4,512]{0,2,1:T(8,128)(2,1)}), bf16[128,4,512]{0,2,1:T(8,128)(2,1)S(1)}, u32[]{:S(2)}, u32[]{:S(2)}) async-start(bf16[128,4,512]{0,2,1:T(8,128)(2,1)} %pad_maximum_fusion.2), calls=%async_computation | async-start | bytes 1048576 | tf_op jit(solution)/shard_map/all_to_all | solution.py:589
  14.7 33.6 %reduce-scatter.9.cloned.1.call-start = ((), (), s32[]{:S(2)}) async-start(), calls=%async_computation.15 | async-start | bytes 327680 | tf_op jit(solution)/shard_map/reduce_scatter | solution.py:598
  27.1 49.4 %reduce-scatter.7.cloned.1.call-start = ((), (), s32[]{:S(2)}) async-start(), calls=%async_computation.14 | async-start | bytes 1310720 | tf_op jit(solution)/shard_map/reduce_scatter | solution.py:372
  27.4 3.5 copy-start.15
  27.4 3.2 copy-start.39
  30.5 88.5 %all-gather.10.cloned.1.call-start = ((), (), s32[]{:S(2)}) async-start(), calls=%async_computation.16 | async-start | bytes 1310720 | tf_op jit(solution)/shard_map/all_gather | solution.py:378
  30.9 45.6 %copy-start.35 = (s32[128]{0:T(128)}, s32[128]{0:T(128)S(1)}, u32[]{:S(2)}) copy-start(s32[128]{0:T(128)S(1)} %convert_reduce_fusion.3) | copy-start | bytes 1540
  77.6 5.7 copy-start.26
  78.7 4.5 copy-start.29
  85.9 29.0 %all-to-all-start.1 = ((bf16[256,3,4,256]{0,3,1,2:T(8,128)(2,1)}), bf16[256,3,4,256]{0,3,1,2:T(8,128)(2,1)}, u32[]{:S(2)}, u32[]{:S(2)}) async-start(bf16[256,3,4,256]{0,3,1,2:T(8,128)(2,1)} %copy.156), calls=%async_computation.3 | async-start | bytes 3145728 | tf_op jit(solution)/shard_map/all_to_all | solution.py:574
  113.9 0.6 copy-start.19
  134.6 11.8 %copy-start.20 = (s32[4,1,8]{2,1,0:T(1,128)S(1)}, s32[4,1,8]{2,1,0:T(1,128)}, u32[]{:S(2)}) copy-start(s32[4,1,8]{2,1,0:T(1,128)} %copy-done.19) | copy-start | bytes 388
  140.3 26.2 %all-to-all-start.2 = ((bf16[8,128,384]{1,2,0:T(8,128)(2,1)}), bf16[8,128,384]{1,2,0:T(8,128)(2,1)}, u32[]{:S(2)}, u32[]{:S(2)}) async-start(bf16[8,128,384]{1,2,0:T(8,128)(2,1)} %bitcast.209), calls=%async_computation.4 | async-start | bytes 1572864 | tf_op jit(solution)/shard_map/all_to_all | solution.py:632
  145.9 83.9 %reduce-scatter.11.cloned.1.call-start = ((), (), s32[]{:S(2)}) async-start(), calls=%async_computation.17 | async-start | bytes 1310720 | tf_op jit(solution)/shard_map/reduce_scatter | solution.py:372
  174.5 12.7 %copy-start.6 = (bf16[1024,128]{0,1:T(8,128)(2,1)}, bf16[1024,128]{0,1:T(8,128)(2,1)S(1)}, u32[]{:S(2)}) copy-start(bf16[1024,128]{0,1:T(8,128)(2,1)S(1)} %copy.164) | copy-start | bytes 786436
  182.5 4.7 copy-start.28
  187.2 2.2 copy-start.1
  190.3 16.4 %copy-start.43 = (bf16[256]{0:T(256)(128)(2,1)S(1)}, bf16[256]{0:T(256)(128)(2,1)}, u32[]{:S(2)}) copy-start(bf16[256]{0:T(256)(128)(2,1)} %param.18) | copy-start | bytes 1540
  190.3 39.4 %copy-start.3 = (bf16[128,1024]{1,0:T(8,128)(2,1)S(1)}, bf16[128,1024]{1,0:T(8,128)(2,1)}, u32[]{:S(2)}) copy-start(bf16[128,1024]{1,0:T(8,128)(2,1)} %reduce-scatter.7.cloned.1.call-done) | copy-start | bytes 786436
  203.5 0.7 copy-start.4
  206.7 74.8 %all-gather.12.cloned.1.call-start = ((), (), s32[]{:S(2)}) async-start(), calls=%async_computation.18 | async-start | bytes 1310720 | tf_op jit(solution)/shard_map/all_gather | solution.py:378
  211.8 112.9 %copy-start.17 = (f32[4,1,256]{2,1,0:T(1,128)}, f32[4,1,256]{2,1,0:T(1,128)S(1)}, u32[]{:S(2)}) copy-start(f32[4,1,256]{2,1,0:T(1,128)S(1)} %convert_element_type.203) | copy-start | bytes 12292
  230.9 93.8 %copy-start.22 = (f32[128]{0:T(128)}, f32[128]{0:T(128)S(1)}, u32[]{:S(2)}) copy-start(f32[128]{0:T(128)S(1)} %broadcast_multiply_fusion.4) | copy-start | bytes 1540
  232.1 92.7 %copy-start.24 = (f32[128]{0:T(128)}, f32[128]{0:T(128)S(1)}, u32[]{:S(2)}) copy-start(f32[128]{0:T(128)S(1)} %add_rsqrt_fusion) | copy-start | bytes 1540
  238.0 39.5 %all-to-all-start.4 = ((bf16[256,4,1024]{0,2,1:T(8,128)(2,1)}), bf16[256,4,1024]{0,2,1:T(8,128)(2,1)}, u32[]{:S(2)}, u32[]{:S(2)}) async-start(bf16[256,4,1024]{0,2,1:T(8,128)(2,1)} %bitcast.203), calls=%async_computation.7 | async-start | bytes 4194304 | tf_op jit(solution)/shard_map/all_to_all | solution.py:577
  242.5 47.5 %all-gather.18.cloned.1.call-start = ((), (), s32[]{:S(2)}) async-start(), calls=%async_computation.25 | async-start | bytes 1310720 | tf_op jit(solution)/shard_map/all_gather | solution.py:378
  243.1 79.7 %reduce-scatter.15.cloned.1.call-start = ((), (), s32[]{:S(2)}) async-start(), calls=%async_computation.20 | async-start | bytes 1310720 | tf_op jit(solution)/shard_map/reduce_scatter | solution.py:372
  290.0 5.5 copy-start.9
  294.5 1.0 copy-start.46
  297.7 46.0 %all-gather.14.cloned.1.call-start = ((), (), s32[]{:S(2)}) async-start(), calls=%async_computation.21 | async-start | bytes 1310720 | tf_op jit(solution)/shard_map/all_gather | solution.py:378
  324.7 25.1 %copy-start.31 = (f32[128]{0:T(128)}, f32[128]{0:T(128)S(1)}, u32[]{:S(2)}) copy-start(f32[128]{0:T(128)S(1)} %broadcast_multiply_fusion.2) | copy-start | bytes 1540
  324.8 25.1 %copy-start.33 = (f32[128]{0:T(128)}, f32[128]{0:T(128)S(1)}, u32[]{:S(2)}) copy-start(f32[128]{0:T(128)S(1)} %broadcast_multiply_fusion.3) | copy-start | bytes 1540
  349.8 14.9 %all-to-all-start.5 = ((bf16[8,128,128]{1,2,0:T(8,128)(2,1)}), bf16[8,128,128]{1,2,0:T(8,128)(2,1)}, u32[]{:S(2)}, u32[]{:S(2)}) async-start(bf16[8,128,128]{1,2,0:T(8,128)(2,1)} %bitcast.235), calls=%async_computation.10 | async-start | bytes 524288 | tf_op jit(solution)/shard_map/all_to_all | solution.py:632
  355.4 81.3 %reduce-scatter.17.cloned.1.call-start = ((), (), s32[]{:S(2)}) async-start(), calls=%async_computation.22 | async-start | bytes 1310720 | tf_op jit(solution)/shard_map/reduce_scatter | solution.py:372
  369.6 4.9 copy-start.12
  374.5 1.4 copy-start.8
  375.9 2.2 copy-start.2
  375.9 2.2 copy-start.7
  378.1 1.4 copy-start.13
  413.5 51.1 %reduce-scatter.13.cloned.1.call-start = ((), (), s32[]{:S(2)}) async-start(), calls=%async_computation.19 | async-start | bytes 1310720 | tf_op jit(solution)/shard_map/reduce_scatter | solution.py:372
  413.5 3.6 copy-start.44
  413.6 24.1 %copy-start.27 = (f32[128]{0:T(128)S(1)}, f32[128]{0:T(128)}, u32[]{:S(2)}) copy-start(f32[128]{0:T(128)} %copy-done.26) | copy-start | bytes 1540
  413.6 24.1 %copy-start.30 = (f32[128]{0:T(128)S(1)}, f32[128]{0:T(128)}, u32[]{:S(2)}) copy-start(f32[128]{0:T(128)} %copy-done.29) | copy-start | bytes 1540
  417.0 21.9 %copy-start.36 = (s32[128]{0:T(128)S(1)}, s32[128]{0:T(128)}, u32[]{:S(2)}) copy-start(s32[128]{0:T(128)} %copy-done.35) | copy-start | bytes 1540
  417.0 47.6 %copy-start.18 = (f32[4,1,256]{2,1,0:T(1,128)S(1)}, f32[4,1,256]{2,1,0:T(1,128)}, u32[]{:S(2)}) copy-start(f32[4,1,256]{2,1,0:T(1,128)} %copy-done.17) | copy-start | bytes 12292
  417.0 47.6 %copy-start.23 = (f32[128]{0:T(128)S(1)}, f32[128]{0:T(128)}, u32[]{:S(2)}) copy-start(f32[128]{0:T(128)} %copy-done.22) | copy-start | bytes 1540
  417.0 47.6 %copy-start.25 = (f32[128]{0:T(128)S(1)}, f32[128]{0:T(128)}, u32[]{:S(2)}) copy-start(f32[128]{0:T(128)} %copy-done.24) | copy-start | bytes 1540
  417.0 47.6 %copy-start.32 = (f32[128]{0:T(128)S(1)}, f32[128]{0:T(128)}, u32[]{:S(2)}) copy-start(f32[128]{0:T(128)} %copy-done.31) | copy-start | bytes 1540
  417.1 47.6 %copy-start.34 = (f32[128]{0:T(128)S(1)}, f32[128]{0:T(128)}, u32[]{:S(2)}) copy-start(f32[128]{0:T(128)} %copy-done.33) | copy-start | bytes 1540
  417.1 120.1 %all-reduce.3.cloned.1.call-start = ((), (), s32[]{:S(2)}) async-start(), calls=%async_computation.24 | async-start | bytes 131072 | tf_op jit(solution)/shard_map/psum | solution.py:736
  440.1 115.8 %all-gather.16.cloned.1.call-start = ((), (), s32[]{:S(2)}) async-start(), calls=%async_computation.23 | async-start | bytes 1310720 | tf_op jit(solution)/shard_map/all_gather | solution.py:378
  470.0 1.5 copy-start.41
  470.0 2.3 copy-start.45
  472.3 2.6 copy-start.21
  472.3 30.5 %copy-start.5 = (bf16[4,128,1,2,128]{4,3,1,0,2:T(2,128)(2,1)S(1)}, bf16[4,128,1,2,128]{4,3,1,0,2:T(2,128)(2,1)}, u32[]{:S(2)}) copy-start(bf16[4,128,1,2,128]{4,3,1,0,2:T(2,128)(2,1)} %copy-done.4) | copy-start | bytes 786436
  472.3 30.5 %copy-start.11 = (bf16[512,1024]{1,0:T(8,128)(2,1)S(1)}, bf16[512,1024]{1,0:T(8,128)(2,1)}, u32[]{:S(2)}) copy-start(bf16[512,1024]{1,0:T(8,128)(2,1)} %all-gather.14.cloned.1.call-done) | copy-start | bytes 3145732
  507.9 48.0 %copy-start.16 = (bf16[4,128,1,512]{3,1,0,2:T(8,128)(2,1)S(1)}, bf16[4,128,1,512]{3,1,0,2:T(8,128)(2,1)}, u32[]{:S(2)}) copy-start(bf16[4,128,1,512]{3,1,0,2:T(8,128)(2,1)} %copy-done.15) | copy-start | bytes 1572868
  717.3 4.2 copy-start.10
  721.5 1.6 copy-start.40
  721.5 2.3 copy-start.42
  723.8 5.2 copy-start.14
  725.4 36.1 %all-to-all-start.7 = ((bf16[4,128,1,512]{3,1,2,0:T(8,128)(2,1)}), bf16[4,128,1,512]{3,1,2,0:T(8,128)(2,1)S(1)}, u32[]{:S(2)}, u32[]{:S(2)}) async-start(bf16[4,128,1,512]{3,1,2,0:T(8,128)(2,1)} %bitcast.250), calls=%async_computation.13 | async-start | bytes 1048576 | tf_op jit(solution)/shard_map/all_to_all | solution.py:744
  (1 other events, 0.5 us)
Sparse Core Ops, SparseCore 0:
  27.2 21.0 reduce-scatter.8
  51.5 24.8 reduce-scatter.6
  80.8 19.3 all-gather.9
  206.8 22.9 reduce-scatter.10
  234.0 20.3 all-gather.11
  255.9 22.7 all-gather.17
  297.9 24.8 reduce-scatter.14
  327.0 16.7 all-gather.13
  413.6 22.9 reduce-scatter.16
  439.7 24.8 reduce-scatter.12
  468.6 68.4 all-reduce.2
  539.1 16.6 all-gather.15

commit v3 on v0

--- a/solution.py
+++ b/solution.py
@@ -1,8 +1,12 @@
+import functools
 import math
+import types
 
 import jax
 import jax.numpy as jnp
 from jax import lax
+from jax.experimental import pallas as pl
+from jax.experimental.pallas import tpu as pltpu
 from jax.sharding import PartitionSpec as P
 
 HEADS = 16
@@ -13,6 +17,9 @@
 EPSILON = 1e-06
 NEGATIVE = -1e30
 HIGHEST = lax.Precision.HIGHEST
+MESH = pl.DeviceIdType.MESH
+RING = 8
+ROWS = 4
 
 
 def from_behind(block, axis, distance):
@@ -354,6 +361,1097 @@
     )
 
 
+def dot_plain(left_side, right_side):
+    return jnp.dot(left_side, right_side, preferred_element_type=jnp.float32)
+
+
+def dot_across(left_side, right_side):
+    return lax.dot_general(
+        left_side, right_side, (((1,), (1,)), ((), ())), preferred_element_type=jnp.float32
+    )
+
+
+def ring_place(rank):
+    odd = lax.rem(rank, 2)
+    return (1 - odd) * (rank // 2) + odd * ((15 - rank) // 2)
+
+
+def ring_rank(place):
+    upper = place // 4
+    return (1 - upper) * (2 * place) + upper * (15 - 2 * place)
+
+
+class Ring:
+    def __init__(self, part, land, sems, rank, group_rank):
+        self.part, self.land = part, land
+        self.sems = sems
+        self.rank, self.group_rank = rank, group_rank
+        self.place = ring_place(rank)
+        self.half = part.shape[1] // 2
+        self.copies = {}
+
+    def block_at(self, offset):
+        return ring_rank(lax.rem(self.place + offset + 2 * RING, RING))
+
+    def rows(self, way):
+        return pl.ds(way * self.half, self.half)
+
+    def send(self, kind, step, way, source, target):
+        to = ring_rank(lax.rem(self.place + (1 if way == 0 else RING - 1), RING))
+        copy = pltpu.make_async_remote_copy(
+            src_ref=source,
+            dst_ref=target,
+            send_sem=self.sems.at[kind, 0, way, step],
+            recv_sem=self.sems.at[kind, 1, way, step],
+            device_id=(to, self.group_rank),
+            device_id_type=MESH,
+        )
+        copy.start()
+        self.copies[kind, step, way] = copy
+
+    def sum_step(self, step):
+        if step == 1:
+            for way in range(2):
+                self.copies[0, 0, way].wait_send()
+        for way in range(2):
+            block = self.block_at((-1 if way == 0 else 1) * (step + 1))
+            rows = self.rows(way)
+            if step > 0:
+                self.copies[0, step - 1, way].wait_recv()
+                tile = min(self.half, 32)
+
+                def add(i, carry, way=way, block=block, tile=tile):
+                    at = pl.ds(pl.multiple_of(way * self.half + i * tile, tile), tile)
+                    total = self.part[block, at].astype(jnp.float32) + self.land[
+                        step - 1, at
+                    ].astype(jnp.float32)
+                    self.land[step - 1, at] = total.astype(jnp.bfloat16)
+                    return carry
+
+                lax.fori_loop(0, self.half // tile, add, 0)
+            if step < RING - 1:
+                source = self.part.at[block, rows] if step == 0 else self.land.at[step - 1, rows]
+                self.send(0, step, way, source, self.land.at[step, rows])
+
+    def total(self):
+        return self.land.at[RING - 2]
+
+    def spread_step(self, step):
+        for way in range(2):
+            block = self.block_at((-1 if way == 0 else 1) * step)
+            rows = self.rows(way)
+            if step > 0:
+                self.copies[1, step - 1, way].wait_recv()
+            if step < RING - 1:
+                target = self.part.at[block, rows]
+                self.send(1, step, way, target, target)
+
+    def finish(self):
+        for (kind, step, _), copy in self.copies.items():
+            if kind or step:
+                copy.wait_send()
+
+
+def block_kernel(names, *refs):
+    n = types.SimpleNamespace(**dict(zip(names, refs)))
+    low, full = jnp.bfloat16, jnp.float32
+    rank, group_rank = lax.axis_index("blk"), lax.axis_index("grp")
+    core, chip = lax.rem(group_rank, 2), group_rank // 2
+    sibling = (rank, group_rank + 1 - 2 * core)
+    across = (rank, group_rank + 2 - 4 * chip)
+    frames, width = n.cotangent.shape
+    half = 2 * frames
+    columns = width // ROWS
+    mine, theirs = core * half, (1 - core) * half
+    own_slot = 2 * core + chip
+    pair_row, pair_side = rank // 2, lax.rem(rank, 2)
+    sent = []
+
+    def lines(offset, size):
+        return pl.ds(pl.multiple_of(offset, min(size, 128)), size)
+
+    def slot_of(row):
+        return 2 * lax.rem(row, 2) + row // 2
+
+    def row_of(slot):
+        return 2 * lax.rem(slot, 2) + slot // 2
+
+    def group(other):
+        return lax.rem(group_rank + other, ROWS)
+
+    def block(other):
+        return lax.rem(rank + other, RING)
+
+    def link(source, target, send_sem, recv_sem, device):
+        return pltpu.make_async_remote_copy(
+            src_ref=source,
+            dst_ref=target,
+            send_sem=send_sem,
+            recv_sem=recv_sem,
+            device_id=device,
+            device_id_type=MESH,
+        )
+
+    def push(source, target, sems, index, device):
+        copy = link(source, target, sems.at[(0,) + index], sems.at[(1,) + index], device)
+        copy.start()
+        sent.append(copy)
+        return copy
+
+    def load(source, target, index):
+        copy = pltpu.make_async_copy(source, target, n.load_sem.at[index])
+        copy.start()
+        return copy
+
+    def tiles(count, tile, body):
+        def step(i, carry):
+            body(pl.multiple_of(i * tile, tile))
+            return carry
+
+        lax.fori_loop(0, count // tile, step, 0)
+
+    joined_loads = [
+        load((n.inputs, n.skipped)[t // 2].at[:, pl.ds((t % 2) * 512, 512)], n.joined_own.at[t], t)
+        for t in range(ROWS)
+    ]
+    upstream_load = load(n.cotangent, n.upstream.at[lines(own_slot * frames, frames)], 4)
+    skip_load = load(n.w_skip, n.skip_held, 5)
+    mod_load = load(n.w_mod, n.mod_held, 6)
+    out_load = load(n.w_out, n.out_held, 7)
+    down_load = load(n.w_down, n.down_held, 8)
+    pieces = [(side, kind) for side in range(2) for kind in range(3)]
+
+    def qkv_piece(target, side, kind):
+        return n.w_qkv.at[:, pl.ds(pl.multiple_of(kind * width + target * columns + side * 128, 128), 128)]
+
+    def qkv_place(side, kind):
+        return n.qkv_held.at[lines(group_rank * columns, columns), pl.ds((side * 3 + kind) * 128, 128)]
+
+    qkv_loads = [
+        load(qkv_piece(group_rank, *piece), qkv_place(*piece), 9 + i)
+        for i, piece in enumerate(pieces)
+    ]
+    hidden_units = n.up_held.shape[1]
+
+    def up_piece(target):
+        return n.w_up.at[:, pl.ds(pl.multiple_of(target * hidden_units, 128), hidden_units)]
+
+    up_place = n.up_held.at[lines(group_rank * columns, columns)]
+    up_load = load(up_piece(group_rank), up_place, 15)
+
+    barrier = pltpu.get_barrier_semaphore()
+    for other in range(1, ROWS):
+        pl.semaphore_signal(barrier, inc=1, device_id=(rank, group(other)), device_id_type=MESH)
+    for other in range(1, RING):
+        pl.semaphore_signal(barrier, inc=1, device_id=(block(other), group_rank), device_id_type=MESH)
+    for copy in joined_loads:
+        copy.wait()
+    pl.semaphore_wait(barrier, ROWS + RING - 2)
+
+    joined_place = n.joined.at[lines(own_slot * frames, frames)]
+    joined_sends = [
+        push(n.joined_own.at[group(o)], joined_place, n.joined_sem, (o - 1,), (rank, group(o)))
+        for o in (2, 1, 3)
+    ]
+    small_sends = [
+        push(n.small, n.smalls.at[group_rank], n.small_sem, (o - 1,), (rank, group(o)))
+        for o in (2, 1, 3)
+    ]
+    qkv_sends = [
+        push(
+            qkv_piece(group(o), *piece),
+            qkv_place(*piece),
+            n.qkv_sem,
+            (o - 1, i),
+            (rank, group(o)),
+        )
+        for o in (2, 1, 3)
+        for i, piece in enumerate(pieces)
+    ]
+    n.joined[lines(own_slot * frames, frames)] = n.joined_own[group_rank]
+    n.smalls[group_rank] = n.small[...]
+    for copy in small_sends:
+        copy.wait_recv()
+
+    steps = jnp.concatenate([n.smalls[(0, 2, 1, 3)[s], 0] for s in range(ROWS)], axis=0)
+    steps = jnp.concatenate([steps, steps], axis=1)
+    lane = lax.broadcasted_iota(jnp.int32, steps.shape, 1) + lax.rem(group_rank, 2) * columns
+    rate = jnp.exp(-math.log(10000.0) * lane.astype(full) / (width // 2))
+    angles = 1000.0 * (steps / STEPS) * rate
+    turned = jnp.where(group_rank >= 2, jnp.cos(angles), jnp.sin(angles))
+    n.condition[...] = (turned / (1.0 + jnp.exp(-turned))).astype(low)
+    mod_load.wait()
+
+    def mod_tile(at):
+        where = pl.ds(at, 512)
+        n.mod_part[:, where] = dot_plain(n.condition[...], n.mod_held[:, where])
+
+    tiles(2 * width, 512, mod_tile)
+    mod_first = push(
+        n.mod_part.at[pl.ds(pl.multiple_of(16 * (1 - core), 16), 16)], n.mod_land.at[0], n.mod_sem, (0,), sibling
+    )
+
+    gains = [n.smalls[r, 5 + i][0:1] for r in range(ROWS) for i in range(2)]
+    n.gain[...] = jnp.broadcast_to(jnp.concatenate(gains, axis=1), n.gain.shape)
+
+    def picked(row, first, count):
+        spot = (lax.broadcasted_iota(jnp.int32, (count, 128), 0) + first).astype(full)
+        return (spot >= n.smalls[row, 3][0:1]) & (spot < n.smalls[row, 4][0:1]), spot
+
+    lanes = lax.broadcasted_iota(jnp.int32, (frames, 128), 1)
+    turn_rate = jnp.exp(-math.log(10000.0) * lax.rem(lanes, 32).astype(full) / 32)
+    turn_sign = jnp.where(lax.rem(lanes, 64) < 32, -1.0, 1.0)
+
+    def turn_tables(row, first, cosine, sine, at):
+        chosen, spot = picked(row, first, frames)
+        start = jnp.where(chosen & (lanes < 8), n.smalls[row, 3][0:1], 0.0)
+        position = spot - jnp.sum(start, axis=1, keepdims=True)
+        angle = position * turn_rate
+        cosine[at] = jnp.cos(angle)
+        sine[at] = jnp.sin(angle) * turn_sign
+
+    def swapped(value):
+        ahead = pltpu.roll(value, 96, 1)
+        behind = pltpu.roll(value, 32, 1)
+        return jnp.where(lax.rem(lanes, 64) < 32, ahead, behind)
+
+    def partial_sum(index, left_ref, right_tile):
+        def to_send(at):
+            n.send_one[:, pl.ds(at, 256)] = right_tile(left_ref[lines(theirs, half)], at).astype(low)
+
+        def to_keep(at):
+            n.keep[:, pl.ds(at, 256)] = right_tile(left_ref[lines(mine, half)], at)
+
+        if index > 0:
+            for copy in group_copies[index - 1][0]:
+                copy.wait_send()
+        tiles(width, 256, to_send)
+        first = [
+            push(
+                n.send_one.at[pl.ds(k * frames, frames)],
+                n.land_one.at[index, pl.ds(k * frames, frames)],
+                n.first_sem,
+                (index, k),
+                sibling,
+            )
+            for k in range(2)
+        ]
+        tiles(width, 256, to_keep)
+        return first
+
+    def cross_sum(index, first):
+        if index > 0:
+            for copy in group_copies[index - 1][1]:
+                copy.wait_send()
+        second = []
+        for k in range(2):
+            first[k].wait_recv()
+
+            def add(at, k=k):
+                where = pl.ds(k * frames + at, 32)
+                total = n.keep[where] + n.land_one[index, where].astype(full)
+                n.keep[where] = total
+                n.send_two[where] = total.astype(low)
+
+            tiles(frames, 32, add)
+            second.append(
+                push(
+                    n.send_two.at[pl.ds(k * frames, frames)],
+                    n.land_two.at[index, pl.ds(k * frames, frames)],
+                    n.second_sem,
+                    (index, k),
+                    across,
+                )
+            )
+        group_copies[index] = (first, second)
+        return second
+
+    group_copies = {}
+
+    def mean(value):
+        return jnp.mean(value, axis=-1, keepdims=True)
+
+    def share(buffer, k, sems):
+        where = lines(mine + k * frames, frames)
+        return push(buffer.at[where], buffer.at[where], sems, (k,), sibling)
+
+    skip_load.wait()
+    for copy in joined_sends:
+        copy.wait_recv()
+
+    def skip_tile(left, at):
+        return dot_plain(left, n.skip_held[:, pl.ds(at, 256)])
+
+    first = partial_sum(0, n.joined, skip_tile)
+    mod_first.wait_recv()
+    mod_mine = n.mod_part[pl.ds(pl.multiple_of(16 * core, 16), 16)] + n.mod_land[0]
+    n.mod_send[...] = mod_mine
+    mod_second = push(n.mod_send, n.mod_land.at[1], n.mod_sem, (1,), across)
+    second = cross_sum(0, first)
+    up_sends = [
+        push(up_piece(group(o)), up_place, n.up_sem, (o - 1,), (rank, group(o))) for o in (2, 1, 3)
+    ]
+    upstream_load.wait()
+    own_lines = lines(own_slot * frames, frames)
+    upstream_sends = [
+        push(n.upstream.at[own_lines], n.upstream.at[own_lines], n.upstream_sem, (i,), device)
+        for i, device in enumerate((across, sibling))
+    ]
+    for slot in range(ROWS):
+        turn_tables(
+            (0, 2, 1, 3)[slot],
+            rank * frames,
+            n.cosine,
+            n.sine,
+            pl.ds(slot * frames, frames),
+        )
+    mod_second.wait_recv()
+    mod_total = n.mod_send[...] + n.mod_land[1]
+    for k in range(2):
+        row = 2 * k + core
+        values = mod_total[8 * k : 8 * k + 8]
+        high = values.astype(low).astype(full)
+        stack = jnp.concatenate([high, values - high], axis=0).astype(low)
+        chosen = picked(row, rank * frames, frames)[0]
+        picker = jnp.where(chosen, 1.0, 0.0).astype(low)[:, :16]
+
+        def per_frame(at, stack=stack, picker=picker, k=k):
+            del at
+
+        where = pl.ds(k * frames, frames)
+        n.scale_one[where] = 1.0 + dot_plain(picker, stack[:, :width])
+        n.shift_one[where] = dot_plain(picker, stack[:, width:])
+
+    attn_sends = []
+    for k in range(2):
+        second[k].wait_recv()
+
+        def norm_one(at, k=k):
+            where = pl.ds(k * frames + at, 32)
+            hidden = n.keep[where] + n.land_two[0, where].astype(full)
+            n.hidden[where] = hidden
+            centred = hidden - mean(hidden)
+            spread = lax.rsqrt(mean(centred * centred) + EPSILON)
+            normal = centred * spread
+            n.normal_one[where] = normal
+            n.spread_one[where] = jnp.broadcast_to(spread, (32, 128))
+            n.attn_in[lines(mine + k * frames + at, 32)] = (
+                normal * n.scale_one[where] + n.shift_one[where]
+            ).astype(low)
+
+        tiles(frames, 32, norm_one)
+        attn_sends.append(share(n.attn_in, k, n.attn_sem))
+
+    for copy in qkv_loads:
+        copy.wait()
+    for copy in qkv_sends:
+        copy.wait_recv()
+
+    def to_heads(offset, value_of, target, sems, wide, send_buffer):
+        for k in range(2):
+            slot = offset // frames + k
+            for side in range(2):
+                to = 2 * row_of(slot) + side
+                value = value_of(k, side, slot)
+
+                @pl.when(to != rank)
+                def _():
+                    send_buffer[to] = value
+                    link(
+                        send_buffer.at[to],
+                        target.at[lines(rank * frames, frames)],
+                        sems.at[0, to],
+                        sems.at[1, rank],
+                        (to, group_rank),
+                    ).start()
+
+                @pl.when(to == rank)
+                def _():
+                    target[lines(rank * frames, frames)] = value
+
+    def heads_arrive(target, sems):
+        for other in range(1, RING):
+            source = block(other)
+            where = target.at[lines(source * frames, frames)]
+            link(where, where, sems.at[0, source], sems.at[1, source], (source, group_rank)).wait_recv()
+
+    def project_half(offset):
+        def project_tile(at):
+            n.project[:, pl.ds(at, 256)] = dot_plain(
+                n.attn_in[lines(offset, half)], n.qkv_held[:, pl.ds(at, 256)]
+            )
+
+        tiles(3 * columns, 256, project_tile)
+
+        def value_of(k, side, slot):
+            where = lines(slot * frames, frames)
+            cosine, sine = n.cosine[where], n.sine[where]
+            blocks = []
+            for kind in range(3):
+                value = n.project[pl.ds(k * frames, frames), pl.ds((side * 3 + kind) * 128, 128)]
+                if kind < 2:
+                    value = value * cosine + swapped(value) * sine
+                blocks.append(value.astype(low))
+            return jnp.concatenate(blocks, axis=1)
+
+        to_heads(offset, value_of, n.paired, n.pair_sem, 384, n.pair_send)
+
+    project_half(mine)
+    for copy in attn_sends:
+        copy.wait_recv()
+    project_half(theirs)
+
+    def row_tables(at):
+        turn_tables(pair_row, at, n.row_cosine, n.row_sine, pl.ds(at, frames))
+        chosen = jnp.where(picked(pair_row, at, frames)[0], 1.0, 0.0)
+        n.chosen[pl.ds(at, frames)] = chosen.astype(low)
+
+    tiles(RING * frames, frames, row_tables)
+    heads_arrive(n.paired, n.pair_sem)
+
+    def masked_parts(at):
+        where = pl.ds(at, frames)
+        query, key = n.paired[where, 0:128], n.paired[where, 128:256]
+        chosen = n.chosen[where]
+        first_head = lanes < 64
+        blocked = jnp.where(
+            lax.rem(lanes, 64) < 8, NEGATIVE * (1.0 - chosen.astype(full)), 0.0
+        ).astype(low)
+        scaled = (query.astype(full) * HEAD_DIM ** (-0.5)).astype(low)
+        n.query_head[0, where] = jnp.where(first_head, scaled, chosen)
+        n.query_head[1, where] = jnp.where(first_head, chosen, scaled)
+        n.key_head[0, where] = jnp.where(first_head, key, blocked)
+        n.key_head[1, where] = jnp.where(first_head, blocked, key)
+        n.query_turned[:, where] = jnp.transpose(query.astype(full)).astype(low)
+
+    tiles(RING * frames, frames, masked_parts)
+    all_frames = RING * frames
+    pair_place = (lines(slot_of(pair_row) * frames, frames), lines(pair_side * 128, 128))
+
+    def attend(at):
+        where = pl.ds(at, half)
+        sums = []
+        for head in range(2):
+            scores = dot_across(n.query_head[head, where], n.key_head[head])
+            top = jnp.max(scores, axis=1, keepdims=True)
+            weights = jnp.exp(scores - top)
+            total = jnp.sum(weights, axis=1, keepdims=True)
+            shares = (weights * (1.0 / total)).astype(low)
+            n.shares[head, where] = shares
+            sums.append(dot_plain(shares, n.paired[:, 256:384]))
+        first_head = lax.broadcasted_iota(jnp.int32, (half, 128), 1) < 64
+        value = jnp.where(first_head, sums[0], sums[1])
+        n.attended_pair[where] = value
+        n.attended_send[where] = value.astype(low)
+        for k in range(2):
+            to = at // frames + k
+            place = lines(at + k * frames, frames)
+
+            @pl.when(to != rank)
+            def _():
+                link(
+                    n.attended_send.at[place],
+                    n.attended.at[pair_place],
+                    n.attended_sem.at[0, to],
+                    n.attended_sem.at[1, rank],
+                    (to, group_rank),
+                ).start()
+
+            @pl.when(to == rank)
+            def _():
+                n.attended[pair_place] = n.attended_send[place]
+
+    tiles(all_frames, half, attend)
+
+    def pairs_arrive(buffer, sems, wide):
+        for other in range(1, RING):
+            source = block(other)
+            where = buffer.at[
+                lines(slot_of(source // 2) * frames, frames),
+                pl.ds(pl.multiple_of(lax.rem(source, 2) * wide, 128), wide),
+            ]
+            link(where, where, sems.at[0, source], sems.at[1, source], (source, group_rank)).wait_recv()
+
+    upstream_sends[0].wait_recv()
+    other_lines = lines((2 * core + 1 - chip) * frames, frames)
+    upstream_sends.append(
+        push(n.upstream.at[other_lines], n.upstream.at[other_lines], n.upstream_sem, (2,), sibling)
+    )
+    pairs_arrive(n.attended, n.attended_sem, 128)
+
+    out_load.wait()
+    first = partial_sum(1, n.attended, lambda left, at: dot_plain(left, n.out_held[:, pl.ds(at, 256)]))
+    second = cross_sum(1, first)
+    ff_sends = []
+    for k in range(2):
+        second[k].wait_recv()
+
+        def norm_two(at, k=k):
+            where = pl.ds(k * frames + at, 32)
+            hidden = n.hidden[where] + n.keep[where] + n.land_two[1, where].astype(full)
+            n.hidden[where] = hidden
+            centred = hidden - mean(hidden)
+            spread = lax.rsqrt(mean(centred * centred) + EPSILON)
+            normal = centred * spread
+            n.normal_two[where] = normal
+            n.spread_two[where] = jnp.broadcast_to(spread, (32, 128))
+            n.ff_in[lines(mine + k * frames + at, 32)] = (normal * n.gain[0:1]).astype(low)
+
+        tiles(frames, 32, norm_two)
+        ff_sends.append(share(n.ff_in, k, n.ff_sem))
+
+    up_load.wait()
+    down_load.wait()
+    for copy in up_sends:
+        copy.wait_recv()
+    for copy in upstream_sends[1:]:
+        copy.wait_recv()
+
+    def feed_half(offset):
+        where = lines(offset, half)
+
+        def feed_tile(at):
+            widened = dot_plain(n.ff_in[where], n.up_held[:, pl.ds(at, 256)])
+            grad = dot_across(n.upstream[where], n.down_held[pl.ds(at, 256)])
+            share_of = 0.5 * (1.0 + lax.erf(widened * math.sqrt(0.5)))
+            slope = share_of + widened * jnp.exp(-0.5 * widened * widened) * (
+                1.0 / math.sqrt(2.0 * math.pi)
+            )
+            n.activated[where, pl.ds(at, 256)] = (widened * share_of).astype(low)
+            n.grad_widened[where, pl.ds(at, 256)] = (grad * slope).astype(low)
+
+        tiles(hidden_units, 256, feed_tile)
+
+    feed_half(mine)
+    for copy in ff_sends:
+        copy.wait_recv()
+    feed_half(theirs)
+    first = partial_sum(
+        2, n.grad_widened, lambda left, at: dot_across(left, n.up_held[pl.ds(at, 256)])
+    )
+    second = cross_sum(2, first)
+
+    def down_tile(at):
+        value = contract_rows(n.activated[:, pl.ds(at, 256)], n.upstream[...]).astype(low)
+        n.down_total[at // 128] = value[:128]
+        n.down_total[at // 128 + 1] = value[128:]
+
+    tiles(hidden_units, 256, down_tile)
+
+    def up_tile(at):
+        value = contract_rows(n.ff_in[:, pl.ds(at, columns)], n.grad_widened[...]).astype(low)
+        deep = columns // RING
+        for j in range(RING):
+            n.up_total[j, pl.ds(pl.multiple_of(at // RING, deep), deep)] = value[
+                j * deep : (j + 1) * deep
+            ]
+
+    tiles(width, columns, up_tile)
+
+    gain_sums = jnp.zeros((1, width), full)
+    grad_sends = []
+    for k in range(2):
+        second[k].wait_recv()
+        weight = (1 - jnp.abs(chip - k)).astype(full)
+
+        def back_two(i, sums, k=k, weight=weight):
+            at = pl.multiple_of(i * 32, 32)
+            where = pl.ds(k * frames + at, 32)
+            grad = n.keep[where] + n.land_two[2, where].astype(full)
+            normal = n.normal_two[where]
+            scaled = grad * n.gain[0:1]
+            back = n.spread_two[where][:, 0:1] * (
+                scaled - mean(scaled) - normal * mean(scaled * normal)
+            )
+            total = n.upstream[lines(mine + k * frames + at, 32)].astype(full) + back
+            n.grad_two[where] = total
+            n.grad_two_low[lines(mine + k * frames + at, 32)] = total.astype(low)
+            return sums + weight * jnp.sum(grad * normal, axis=0, keepdims=True)
+
+        gain_sums = lax.fori_loop(0, frames // 32, back_two, gain_sums)
+        grad_sends.append(share(n.grad_two_low, k, n.grad_two_sem))
+    n.mod_sums[8:16] = jnp.zeros((8, 2 * width), full)
+    n.mod_sums[8:9, :width] = gain_sums
+
+    def attended_half(offset):
+        value = dot_across(n.grad_two_low[lines(offset, half)], n.out_held[...]).astype(low)
+
+        def value_of(k, side, slot):
+            return value[k * frames : (k + 1) * frames, side * 128 : side * 128 + 128]
+
+        to_heads(offset, value_of, n.grad_pair, n.grad_pair_sem, 128, n.grad_pair_send)
+
+    attended_half(mine)
+    for copy in grad_sends:
+        copy.wait_recv()
+    attended_half(theirs)
+    value = contract_rows(n.attended[...], n.grad_two_low[...]).astype(low)
+    for j in range(RING):
+        n.out_total[j] = value[j * 32 : (j + 1) * 32]
+
+    first = partial_sum(3, n.activated, lambda left, at: dot_plain(left, n.down_held[:, pl.ds(at, 256)]))
+    output_second = cross_sum(3, first)
+
+    heads_arrive(n.grad_pair, n.grad_pair_sem)
+
+    def turn_upstream(at):
+        where = pl.ds(at, frames)
+        n.grad_turned[:, where] = jnp.transpose(n.grad_pair[where].astype(full)).astype(low)
+
+    tiles(all_frames, frames, turn_upstream)
+    n.key_turned[...] = jnp.zeros(n.key_turned.shape, full)
+    n.value_turned[...] = jnp.zeros(n.value_turned.shape, full)
+
+    def back_turned(value, where):
+        return value * n.row_cosine[where] - swapped(value) * n.row_sine[where]
+
+    def attend_back(at):
+        where = pl.ds(at, half)
+        first_head = lax.broadcasted_iota(jnp.int32, (half, 128), 1) < 64
+        grad = n.grad_pair[where]
+        product = grad.astype(full) * n.attended_pair[where]
+        terms = []
+        for head in range(2):
+            here = first_head if head == 0 else jnp.logical_not(first_head)
+            delta = jnp.sum(jnp.where(here, product, 0.0), axis=1, keepdims=True)
+            grad_head = jnp.where(here, grad, jnp.zeros_like(grad))
+            prob_grad = dot_across(grad_head, n.paired[:, 256:384])
+            shares = n.shares[head, where]
+            score_grad = (shares.astype(full) * (prob_grad - delta)).astype(low)
+            terms.append(dot_plain(score_grad, n.paired[:, 128:256]))
+            rows = pl.ds(head * 64, 64)
+            n.value_turned[rows] += dot_plain(n.grad_turned[rows, where], shares)
+            n.key_turned[rows] += dot_plain(n.query_turned[rows, where], score_grad)
+        query_grad = jnp.where(first_head, terms[0], terms[1]) * HEAD_DIM ** (-0.5)
+        for k in range(2):
+            place = lines(at + k * frames, frames)
+            n.project_send[place, 0:128] = back_turned(
+                query_grad[k * frames : (k + 1) * frames], place
+            ).astype(low)
+
+    tiles(all_frames, half, attend_back)
+    project_place = (lines(slot_of(pair_row) * frames, frames), lines(pair_side * 384, 384))
+
+    def keys_back(at):
+        place = pl.ds(at, frames)
+        key_grad = jnp.transpose(n.key_turned[:, place]) * HEAD_DIM ** (-0.5)
+        n.project_send[place, 128:256] = back_turned(key_grad, place).astype(low)
+        n.project_send[place, 256:384] = jnp.transpose(n.value_turned[:, place]).astype(low)
+        to = at // frames
+
+        @pl.when(to != rank)
+        def _():
+            link(
+                n.project_send.at[place],
+                n.grad_project.at[project_place],
+                n.project_sem.at[0, to],
+                n.project_sem.at[1, rank],
+                (to, group_rank),
+            ).start()
+
+        @pl.when(to == rank)
+        def _():
+            n.grad_project[project_place] = n.project_send[place]
+
+    tiles(all_frames, frames, keys_back)
+
+    for copy in output_second:
+        copy.wait_recv()
+
+    def finish_output(at):
+        where = lines(chip * frames + at, 32)
+        n.output[pl.ds(at, 32)] = (
+            n.hidden[where] + n.keep[where] + n.land_two[3, where].astype(full)
+        ).astype(low)
+
+    tiles(frames, 32, finish_output)
+    pairs_arrive(n.grad_project, n.project_sem, 384)
+
+    first = partial_sum(
+        4, n.grad_project, lambda left, at: dot_across(left, n.qkv_held[pl.ds(at, 256)])
+    )
+    second = cross_sum(4, first)
+
+    def qkv_tile(at):
+        value = contract_rows(n.attn_in[:, pl.ds(at, columns)], n.grad_project[...]).astype(low)
+        deep = columns // RING
+        for j in range(RING):
+            n.qkv_total[j, pl.ds(pl.multiple_of(at // RING, deep), deep)] = value[
+                j * deep : (j + 1) * deep
+            ]
+
+    tiles(width, columns, qkv_tile)
+    hidden_sends = []
+    for k in range(2):
+        second[k].wait_recv()
+
+        def back_one(at, k=k):
+            where = pl.ds(k * frames + at, 32)
+            grad = n.keep[where] + n.land_two[4, where].astype(full)
+            normal = n.normal_one[where]
+            scaled = grad * n.scale_one[where]
+            back = n.spread_one[where][:, 0:1] * (
+                scaled - mean(scaled) - normal * mean(scaled * normal)
+            )
+            n.grad_hidden[lines(mine + k * frames + at, 32)] = (n.grad_two[where] + back).astype(low)
+
+            @pl.when(chip == k)
+            def _():
+                n.mod_terms[pl.ds(at, 32), :width] = grad * normal
+                n.mod_terms[pl.ds(at, 32), width:] = grad
+
+        tiles(frames, 32, back_one)
+        hidden_sends.append(share(n.grad_hidden, k, n.grad_hidden_sem))
+
+    spot = (lax.broadcasted_iota(jnp.int32, (8, frames), 1) + rank * frames).astype(full)
+    chosen = (spot >= n.small[1]) & (spot < n.small[2])
+    picker = jnp.where(chosen, 1.0, 0.0)
+
+    def mod_sum(at):
+        where = pl.ds(at, 512)
+        n.mod_sums[0:8, where] = jnp.dot(picker, n.mod_terms[:, where], precision=HIGHEST)
+
+    tiles(2 * width, 512, mod_sum)
+    for other in range(1, RING):
+        to = block(other)
+        push(
+            n.mod_sums.at[:, pl.ds(pl.multiple_of(to * 256, 256), 256)],
+            n.sums_land.at[rank],
+            n.sums_sem,
+            (other - 1,),
+            (to, group_rank),
+        )
+    sums_copies = sent[-(RING - 1) :]
+    n.sums_land[rank] = n.mod_sums[:, pl.ds(pl.multiple_of(rank * 256, 256), 256)]
+
+    for copy in hidden_sends:
+        copy.wait_recv()
+    back = dot_across(n.grad_hidden[...], n.skip_held[...]).astype(low)
+    n.joined_send[...] = back
+    grad_joined_copies = []
+    for other in (2, 1, 3):
+        to = group(other)
+        grad_joined_copies.append(
+            push(
+                n.joined_send.at[lines(slot_of(to) * frames, frames)],
+                n.grad_joined.at[group_rank],
+                n.grad_joined_sem,
+                (other - 1,),
+                (rank, to),
+            )
+        )
+    n.grad_joined[group_rank] = n.joined_send[own_lines]
+
+    def skip_weight_tile(at):
+        value = contract_rows(n.joined[:, pl.ds(at, 256)], n.grad_hidden[...]).astype(low)
+        for j in range(4):
+            n.skip_total[at // 64 + j] = value[j * 64 : (j + 1) * 64]
+
+    tiles(n.joined.shape[1], 256, skip_weight_tile)
+
+    for copy in sums_copies:
+        copy.wait_recv()
+    n.sums_send[...] = jnp.sum(n.sums_land[...], axis=0)
+    n.mod_grad[rank, group_rank] = n.sums_send[...]
+    group_sums = [
+        push(
+            n.sums_send,
+            n.mod_grad.at[rank, group_rank],
+            n.sums_group_sem,
+            (other - 1,),
+            (rank, group(other)),
+        )
+        for other in (2, 1, 3)
+    ]
+    for copy in group_sums:
+        copy.wait_recv()
+    mod_spread = [
+        push(
+            n.mod_grad.at[rank],
+            n.mod_grad.at[rank],
+            n.sums_block_sem,
+            (other - 1,),
+            (block(other), group_rank),
+        )
+        for other in range(1, RING)
+    ]
+
+    rings = [
+        Ring(n.down_total, n.down_land, n.down_sem, rank, group_rank),
+        Ring(n.up_total, n.up_land, n.up_ring_sem, rank, group_rank),
+        Ring(n.qkv_total, n.qkv_land, n.qkv_ring_sem, rank, group_rank),
+        Ring(n.skip_total, n.skip_land, n.skip_ring_sem, rank, group_rank),
+        Ring(n.out_total, n.out_land, n.out_ring_sem, rank, group_rank),
+    ]
+    for step in range(RING):
+        for ring in rings:
+            ring.sum_step(step)
+    turns = []
+    for index, (ring, place) in enumerate(((rings[1], n.up_turn), (rings[2], n.qkv_turn))):
+        deep = columns // RING
+        for other in (2, 1, 3):
+            turns.append(
+                push(
+                    ring.total().at[lines(group(other) * deep, deep)],
+                    place.at[lines(group_rank * deep, deep)],
+                    n.turn_sem,
+                    (index, other - 1),
+                    (rank, group(other)),
+                )
+            )
+        place[lines(group_rank * deep, deep)] = ring.land[RING - 2, lines(group_rank * deep, deep)]
+    for ring in (rings[0], rings[3], rings[4]):
+        ring.part[rank] = ring.land[RING - 2]
+    for copy in turns:
+        copy.wait_recv()
+    n.up_total[rank] = n.up_turn[...]
+    n.qkv_total[rank] = n.qkv_turn[...]
+    for step in range(RING):
+        for ring in rings:
+            ring.spread_step(step)
+    for ring in rings:
+        ring.finish()
+    for copy in mod_spread + grad_joined_copies:
+        copy.wait_recv()
+    for index, copy in enumerate(sent):
+        if not any(copy is other for pair in list(group_copies.values())[:-1] for kind in pair for other in kind):
+            copy.wait_send()
+    for sems, wide in ((n.pair_sem, 384), (n.attended_sem, 128), (n.grad_pair_sem, 128), (n.project_sem, 384)):
+        buffer = {384: n.project_send, 128: n.attended_send}[wide]
+        for other in range(1, RING):
+            to = block(other)
+            where = buffer.at[lines(to * frames, frames)]
+            link(where, where, sems.at[0, to], sems.at[1, to], (to, group_rank)).wait_send()
+
+
+def block_call(
+    inputs, skipped, w_skip, w_mod, w_qkv, w_out, w_up, w_down, cotangent, small
+):
+    low, full = jnp.bfloat16, jnp.float32
+    frames, width = inputs.shape
+    tokens, half = ROWS * frames, 2 * frames
+    columns = width // ROWS
+    hidden_units = w_down.shape[0]
+    joint = w_skip.shape[0]
+    all_frames = RING * frames
+    deep = width // RING
+
+    held = dict(
+        inputs=inputs,
+        skipped=skipped,
+        w_skip=w_skip,
+        w_mod=w_mod,
+        w_qkv=w_qkv,
+        w_out=w_out,
+        w_up=w_up,
+        w_down=w_down,
+        cotangent=cotangent,
+        small=small,
+    )
+    given = dict(
+        output=((frames, width), low),
+        grad_joined=((ROWS, frames, joint), low),
+        condition=((ROWS * 8, columns), low),
+        mod_grad=((RING, ROWS, 16, 256), full),
+        down_total=((RING, hidden_units // RING, width), low),
+        up_total=((RING, deep, hidden_units), low),
+        qkv_total=((RING, deep, 3 * columns), low),
+        skip_total=((RING, joint // RING, width), low),
+        out_total=((RING, columns // RING, width), low),
+    )
+    buffers = dict(
+        joined_own=((ROWS, frames, joint), low),
+        joined=((tokens, joint), low),
+        upstream=((tokens, width), low),
+        skip_held=(w_skip.shape, low),
+        mod_held=(w_mod.shape, low),
+        out_held=(w_out.shape, low),
+        down_held=(w_down.shape, low),
+        qkv_held=((width, 3 * columns), low),
+        up_held=((width, hidden_units), low),
+        smalls=((ROWS,) + small.shape, full),
+        mod_part=((ROWS * 8, 2 * width), full),
+        mod_land=((2, 16, 2 * width), full),
+        mod_send=((16, 2 * width), full),
+        gain=((8, width), full),
+        cosine=((tokens, 128), full),
+        sine=((tokens, 128), full),
+        row_cosine=((all_frames, 128), full),
+        row_sine=((all_frames, 128), full),
+        chosen=((all_frames, 128), low),
+        send_one=((half, width), low),
+        send_two=((half, width), low),
+        keep=((half, width), full),
+        land_one=((5, half, width), low),
+        land_two=((5, half, width), low),
+        scale_one=((half, width), full),
+        shift_one=((half, width), full),
+        hidden=((half, width), full),
+        normal_one=((half, width), full),
+        spread_one=((half, 128), full),
+        normal_two=((half, width), full),
+        spread_two=((half, 128), full),
+        grad_two=((half, width), full),
+        attn_in=((tokens, width), low),
+        project=((half, 3 * columns), full),
+        pair_send=((RING, frames, 384), low),
+        paired=((all_frames, 384), low),
+        query_head=((2, all_frames, 128), low),
+        key_head=((2, all_frames, 128), low),
+        query_turned=((128, all_frames), low),
+        shares=((2, all_frames, all_frames), low),
+        attended_pair=((all_frames, 128), full),
+        attended_send=((all_frames, 128), low),
+        attended=((tokens, columns), low),
+        ff_in=((tokens, width), low),
+        activated=((tokens, hidden_units), low),
+        grad_widened=((tokens, hidden_units), low),
+        grad_two_low=((tokens, width), low),
+        grad_pair_send=((RING, frames, 128), low),
+        grad_pair=((all_frames, 128), low),
+        grad_turned=((128, all_frames), low),
+        key_turned=((128, all_frames), full),
+        value_turned=((128, all_frames), full),
+        project_send=((all_frames, 384), low),
+        grad_project=((tokens, 3 * columns), low),
+        grad_hidden=((tokens, width), low),
+        mod_terms=((frames, 2 * width), full),
+        mod_sums=((16, 2 * width), full),
+        sums_land=((RING, 16, 256), full),
+        sums_send=((16, 256), full),
+        joined_send=((tokens, joint), low),
+        down_land=((RING - 1, hidden_units // RING, width), low),
+        up_land=((RING - 1, deep, hidden_units), low),
+        qkv_land=((RING - 1, deep, 3 * columns), low),
+        skip_land=((RING - 1, joint // RING, width), low),
+        out_land=((RING - 1, columns // RING, width), low),
+        up_turn=((deep, hidden_units), low),
+        qkv_turn=((deep, 3 * columns), low),
+    )
+    sems = dict(
+        load_sem=(16,),
+        joined_sem=(2, 3),
+        small_sem=(2, 3),
+        qkv_sem=(2, 3, 6),
+        up_sem=(2, 3),
+        mod_sem=(2, 2),
+        first_sem=(2, 5, 2),
+        second_sem=(2, 5, 2),
+        upstream_sem=(2, 3),
+        attn_sem=(2, 2),
+        ff_sem=(2, 2),
+        grad_two_sem=(2, 2),
+        grad_hidden_sem=(2, 2),
+        pair_sem=(2, RING),
+        attended_sem=(2, RING),
+        grad_pair_sem=(2, RING),
+        project_sem=(2, RING),
+        grad_joined_sem=(2, 3),
+        sums_sem=(2, RING - 1),
+        sums_group_sem=(2, 3),
+        sums_block_sem=(2, RING - 1),
+        down_sem=(2, 2, 2, RING - 1),
+        up_ring_sem=(2, 2, 2, RING - 1),
+        qkv_ring_sem=(2, 2, 2, RING - 1),
+        skip_ring_sem=(2, 2, 2, RING - 1),
+        out_ring_sem=(2, 2, 2, RING - 1),
+        turn_sem=(2, 2, 3),
+    )
+    names = [*held, *given, *buffers, *sems]
+    vmem = pl.BlockSpec(memory_space=pltpu.VMEM)
+    anywhere = pl.BlockSpec(memory_space=pl.ANY)
+    return pl.pallas_call(
+        functools.partial(block_kernel, names),
+        out_shape=[jax.ShapeDtypeStruct(*spec) for spec in given.values()],
+        in_specs=[vmem if name == "small" else anywhere for name in held],
+        out_specs=[vmem] * len(given),
+        scratch_shapes=[pltpu.VMEM(*spec) for spec in buffers.values()]
+        + [pltpu.SemaphoreType.DMA(shape) for shape in sems.values()],
+        compiler_params=pltpu.CompilerParams(
+            collective_id=0, has_side_effects=True, vmem_limit_bytes=62 * 1024 * 1024
+        ),
+    )(*held.values())
+
+
+def small_table(lengths_row, steps_row, gain):
+    end = jnp.cumsum(lengths_row).astype(jnp.float32)
+    start = end - lengths_row.astype(jnp.float32)
+    count = end.shape[0]
+
+    def down(values):
+        return jnp.broadcast_to(values[:, None], (count, 128))
+
+    def along(values, empty):
+        rest = jnp.full((64 - 2 * count,), empty, jnp.float32)
+        lane = jnp.concatenate([values, values, rest, values, values, rest])
+        return jnp.broadcast_to(lane[None], (8, 128))
+
+    gain = gain.astype(jnp.float32)
+    return jnp.stack(
+        [
+            down(steps_row.astype(jnp.float32)),
+            down(start),
+            down(end),
+            along(start, 1e9),
+            along(end, 0.0),
+            jnp.broadcast_to(gain[None, :128], (8, 128)),
+            jnp.broadcast_to(gain[None, 128:], (8, 128)),
+        ]
+    )
+
+
+def per_device_block(
+    inputs,
+    skipped,
+    w_skip,
+    w_mod,
+    w_qkv,
+    w_out,
+    ff_gain,
+    w_up,
+    w_down,
+    cotangent,
+    lengths,
+    flow_steps,
+):
+    width = inputs.shape[2]
+    columns = width // ROWS
+    group_rank = lax.axis_index("grp")
+    small = small_table(lengths[0], flow_steps[0], ff_gain)
+    output, grad_joined, condition, mod_grad, down, up, qkv, skip, out = block_call(
+        inputs[0], skipped[0], w_skip, w_mod, w_qkv, w_out, w_up, w_down, cotangent[0], small
+    )
+
+    def rows_back(total):
+        return total.astype(jnp.float32).reshape(-1, total.shape[2])
+
+    up = jnp.transpose(
+        up.astype(jnp.float32).reshape(RING, ROWS, columns // RING, -1), (0, 2, 1, 3)
+    ).reshape(columns, -1)
+    qkv = jnp.transpose(
+        qkv.astype(jnp.float32).reshape(RING, ROWS, columns // RING, 2, 3, columns // 2),
+        (0, 2, 4, 1, 3, 5),
+    ).reshape(columns, -1)
+    joined = grad_joined.astype(jnp.float32)
+    mod = jnp.transpose(mod_grad, (1, 2, 0, 3)).reshape(ROWS, 16, 2 * width)
+    gain = jnp.sum(mod[:, 8, :width], axis=0)
+    gain = lax.dynamic_slice_in_dim(gain, group_rank * columns, columns)
+    slots = jnp.concatenate([mod[r, :8] for r in (0, 2, 1, 3)], axis=0)
+    grad_mod = jnp.dot(condition.astype(jnp.float32).T, slots, precision=HIGHEST)
+    return (
+        output[None],
+        jnp.concatenate([joined[0], joined[1]], axis=1)[None],
+        jnp.concatenate([joined[2], joined[3]], axis=1)[None],
+        rows_back(skip),
+        grad_mod,
+        qkv,
+        rows_back(out),
+        gain,
+        up,
+        rows_back(down),
+    )
+
+
 def solution(mesh):
     placed = (
         P("grp", "blk", None),
@@ -369,8 +1467,11 @@
         P("grp", None),
         P("grp", None),
     )
+    body = per_device
+    if mesh.shape["blk"] == RING and mesh.shape["grp"] == ROWS:
+        body = per_device_block
     return jax.shard_map(
-        per_device,
+        body,
         mesh=mesh,
         in_specs=placed,
         out_specs=(

time: 1480 us -> 375 us (0.25)
  blocking collectives: 659 us -> 0 us
  waiting for transfers between devices: 606 us -> 0 us
  Pallas kernels: 0 us -> 336 us
  matrix products: 102 us -> 3.06 us
  other arithmetic: 38 us -> 10.7 us
  starting transfers between devices: 18.1 us -> 0 us
  between operations: 15.8 us -> 0.76 us
    psum x1 -> x0, blocking collectives: 646 us -> none  [per_device(): lax.psum((shards[0], shards[1], shards[2], shards[3], shards[4], shards[5...]
    pallas_call x0 -> x1, Pallas kernels: none -> 336 us  [block_call(): pl.pallas_call(functools.partial(block_kernel, names), out_shape=[jax.Sha...]
    reduce_scatter x6 -> x0, waiting for transfers between devices: 256 us -> none  [the longest x1 74.4 us: per_device(): lax.psum_scatter(grad_down.astype(jnp.bfloat16), 'grp', scatter_dimension...]
    ppermute x48 -> x0, waiting for transfers between devices: 238 us -> none  [from_behind(): return lax.ppermute(block, axis, route)]
    all_gather x6 -> x0, waiting for transfers between devices: 107 us -> none  [the longest x1 43.4 us: per_device(): lax.all_gather(w_qkv, 'grp', axis=0, tiled=True)]
    dot_general x75 -> x1, matrix products: 102 us -> 3.06 us  [per_device_block(): jnp.dot(condition.astype(jnp.float32).T, slots, precision=HIGHEST)]
    convert_element_type x36 -> x3, other arithmetic: 28.5 us -> 0.78 us  [the longest x1 0.66 us: small_table(): steps_row.astype(jnp.float32)]
    while x40 -> x0, local copies, waits for them, and re-layouts: 23 us -> none
  transfers between devices with their start and end apart: 60 -> 0, of which waited for: 40 -> 0; matrix products, arithmetic and copies ran while one was open for 10% -> 0% of each run, Pallas kernels for 0% -> 0%
where the time goes in v3:
time: 375 us; the launch traced here: 374 us
  Pallas kernels  336 us (90%)
  local copies, waits for them, and re-layouts  23.8 us (6%)
  other arithmetic  10.7 us (3%)
    pallas_call x1, Pallas kernels, block_call(): pl.pallas_call(functools.partial(block_kernel, names), out_shape=[jax.Sha...  336 us
    reshape x3, local copies, waits for them, and re-layouts, per_device_block(): qkv = jnp.transpose(qkv.astype(jnp.float32).reshape(RING, ROWS, columns /...  10.7 us
    unnamed x22, local copies, waits for them, and re-layouts  7.55 us

profile of v3, /device:TPU:0, one launch (start us, length us, event | category | flops | bytes accessed | tf_op | source)
XLA Modules:
  0.0 373.8 jit_solution(4515921544810458219)
XLA Ops:
  0.6 0.8 reduce-window.9
  1.5 0.7 bitcast_subtract_fusion
  2.1 0.7 convert_bitcast_fusion.2
  2.8 0.1 constant_dynamic-update-slice_fusion.6
  2.9 0.1 constant_dynamic-update-slice_fusion.5
  2.9 0.1 constant_dynamic-update-slice_fusion.4
  3.0 0.1 concatenate.15
  3.1 0.1 concatenate.16
  3.2 0.7 fusion.9
  3.9 0.0 copy-start.6
  3.9 0.6 copy-done.6
  4.5 335.5 %shard_map.195 = (bf16[128,1024]{1,0:T(8,128)(2,1)}, bf16[4,128,512]{2,1,0:T(8,128)(2,1)}, bf16[32,256]{1,0:T(8,128)(2,1)}, f32[8,4,16,256]{3,2,1,0:T(8,128)}, b...) custom-call(bf16[128,1024]{1,0:T(8,128)(2,1)} %bitcast.61, ...), custom_call_target="tpu_custom_call" | custom-call | tf_op jit(solution)/shard_map/pallas_call | solution.py:1363
  340.1 0.0 copy-start.4
  340.1 1.1 copy.29
  341.3 3.1 fusion
  344.3 0.0 copy-done.4
  344.3 0.1 convert_element_type.37
  344.5 0.0 copy-start
  344.5 0.1 slice_bitcast_fusion.1
  344.6 1.1 maximum_bitcast_fusion
  345.6 0.6 dynamic_slice.3
  346.3 0.2 copy-done
  346.4 0.5 convert_bitcast_fusion
  346.9 2.7 copy.28
  349.7 0.0 copy-start.1
  349.7 5.8 %copy.30 = f32[32,8,4,1024]{3,1,2,0:T(8,128)} copy(f32[32,8,4,1024]{3,2,1,0:T(4,128)S(1)} %bitcast.55) | data formatting | bytes 8388608
  355.5 0.0 copy-done.1
  355.5 3.2 reshape.116
  358.7 3.8 %copy.27 = f32[8,32,3,4,2,128]{5,4,3,2,1,0:T(2,128)S(1)} copy(f32[8,32,3,4,2,128]{5,2,4,1,3,0:T(4,128)} %bitcast.54) | data formatting | bytes 6291456 | tf_op jit(solution)/shard_map/reshape | solution.py:1434
  362.5 3.7 reshape.106
  366.2 0.0 copy-start.2
  366.2 4.2 %bitcast_convert_fusion = f32[1024,1024]{1,0:T(8,128)} fusion(bf16[8,128,1024]{2,1,0:T(8,128)(2,1)} %get-tuple-element.27), kind=kLoop, calls=%fused_computation.1 | loop fusion | flops 1048576 | bytes 6291456 | tf_op jit(solution)/shard_map/reshape | solution.py:1426
  370.4 0.0 copy-start.3
  370.4 0.0 copy-done.2
  370.4 0.0 copy-start.5
  370.4 1.6 bitcast_convert_fusion.1
  372.0 0.0 copy-done.3
  372.0 1.1 bitcast_convert_fusion.2
  373.1 0.0 copy-done.5
  373.1 0.7 copy.38
  (9 shorter events, 0.1 us)
Async XLA Ops:
  3.9 0.6 copy-start.6
  340.1 4.2 %copy-start.4 = (bf16[4,128,512]{2,1,0:T(8,128)(2,1)S(1)}, bf16[4,128,512]{2,1,0:T(8,128)(2,1)}, u32[]{:S(2)}) copy-start(bf16[4,128,512]{2,1,0:T(8,128)(2,1)} %get-tuple-element.20) | copy-start | bytes 1572868
  344.5 2.0 copy-start
  349.7 5.8 %copy-start.1 = (bf16[8,128,768]{2,1,0:T(8,128)(2,1)S(1)}, bf16[8,128,768]{2,1,0:T(8,128)(2,1)}, u32[]{:S(2)}) copy-start(bf16[8,128,768]{2,1,0:T(8,128)(2,1)} %get-tuple-element.24) | copy-start | bytes 4718596
  366.2 4.2 %copy-start.2 = (bf16[8,64,1024]{2,1,0:T(8,128)(2,1)S(1)}, bf16[8,64,1024]{2,1,0:T(8,128)(2,1)}, u32[]{:S(2)}) copy-start(bf16[8,64,1024]{2,1,0:T(8,128)(2,1)} %get-tuple-element.21) | copy-start | bytes 3145732
  370.4 1.6 copy-start.3
  370.4 2.8 copy-start.5

commit v4 on v3

--- a/solution.py
+++ b/solution.py
@@ -381,14 +381,18 @@
     return (1 - upper) * (2 * place) + upper * (15 - 2 * place)
 
 
+TICKS = (2, 1, 1, 2, 2, 1, 5, 3, 1, 3, 4)
+
+
 class Ring:
-    def __init__(self, part, land, sems, rank, group_rank):
-        self.part, self.land = part, land
-        self.sems = sems
+    def __init__(self, part, land, whole, sems, whole_sems, rank, group_rank, turn=None):
+        self.part, self.land, self.whole = part, land, whole
+        self.sems, self.whole_sems = sems, whole_sems
         self.rank, self.group_rank = rank, group_rank
         self.place = ring_place(rank)
         self.half = part.shape[1] // 2
         self.copies = {}
+        self.puts, self.turns, self.turn = [], [], turn
 
     def block_at(self, offset):
         return ring_rank(lax.rem(self.place + offset + 2 * RING, RING))
@@ -433,10 +437,17 @@
                 source = self.part.at[block, rows] if step == 0 else self.land.at[step - 1, rows]
                 self.send(0, step, way, source, self.land.at[step, rows])
 
-    def total(self):
-        return self.land.at[RING - 2]
+    def put(self, block, step, way):
+        rows = self.rows(way)
+        copy = pltpu.make_async_copy(
+            self.part.at[block, rows], self.whole.at[block, rows], self.whole_sems.at[way, step]
+        )
+        copy.start()
+        self.puts.append(copy)
 
     def spread_step(self, step):
+        if step == 0:
+            self.close_sum()
         for way in range(2):
             block = self.block_at((-1 if way == 0 else 1) * step)
             rows = self.rows(way)
@@ -445,11 +456,49 @@
             if step < RING - 1:
                 target = self.part.at[block, rows]
                 self.send(1, step, way, target, target)
+            self.put(block, step, way)
+
+    def begin(self):
+        self.sum_step(0)
+        self.left = [functools.partial(self.sum_step, step) for step in range(1, RING)]
+        self.left += [functools.partial(self.spread_step, step) for step in range(RING)]
+        if self.turn is not None:
+            self.left.insert(RING - 1, self.turn_out)
+
+    def turn_out(self):
+        place, sems = self.turn
+        deep = self.part.shape[1] // ROWS
+
+        def rows(group):
+            return pl.ds(pl.multiple_of(group * deep, deep), deep)
+
+        for other in (2, 1, 3):
+            to = lax.rem(self.group_rank + other, ROWS)
+            copy = pltpu.make_async_remote_copy(
+                src_ref=self.land.at[RING - 2, rows(to)],
+                dst_ref=place.at[rows(self.group_rank)],
+                send_sem=sems.at[0, other - 1],
+                recv_sem=sems.at[1, other - 1],
+                device_id=(self.rank, to),
+                device_id_type=MESH,
+            )
+            copy.start()
+            self.turns.append(copy)
+        place[rows(self.group_rank)] = self.land[RING - 2, rows(self.group_rank)]
+
+    def close_sum(self):
+        for copy in self.turns:
+            copy.wait_recv()
+        self.part[self.rank] = self.land[RING - 2] if self.turn is None else self.turn[0][...]
 
     def finish(self):
+        for copy in self.turns:
+            copy.wait_send()
         for (kind, step, _), copy in self.copies.items():
             if kind or step:
                 copy.wait_send()
+        for copy in self.puts:
+            copy.wait()
 
 
 def block_kernel(names, *refs):
@@ -668,6 +717,32 @@
 
     group_copies = {}
 
+    down_ring, up_ring, out_ring, qkv_ring, skip_ring = rings = [
+        Ring(part, land, whole, sems, n.whole_sem.at[index], rank, group_rank, turn)
+        for index, (part, land, whole, sems, turn) in enumerate(
+            (
+                (n.down_total, n.down_land, n.down_whole, n.down_sem, None),
+                (n.up_total, n.up_land, n.up_whole, n.up_ring_sem, (n.up_turn, n.turn_sem.at[0])),
+                (n.out_total, n.out_land, n.out_whole, n.out_ring_sem, None),
+                (n.qkv_total, n.qkv_land, n.qkv_whole, n.qkv_ring_sem, (n.qkv_turn, n.turn_sem.at[1])),
+                (n.skip_total, n.skip_land, n.skip_whole, n.skip_ring_sem, None),
+            )
+        )
+    ]
+    running = []
+
+    def begin(ring):
+        ring.begin()
+        running.append(ring)
+
+    def ticks(count):
+        for _ in range(count):
+            if running:
+                ring = running.pop(0)
+                ring.left.pop(0)()
+                if ring.left:
+                    running.append(ring)
+
     def mean(value):
         return jnp.mean(value, axis=-1, keepdims=True)
 
@@ -688,15 +763,7 @@
     n.mod_send[...] = mod_mine
     mod_second = push(n.mod_send, n.mod_land.at[1], n.mod_sem, (1,), across)
     second = cross_sum(0, first)
-    up_sends = [
-        push(up_piece(group(o)), up_place, n.up_sem, (o - 1,), (rank, group(o))) for o in (2, 1, 3)
-    ]
-    upstream_load.wait()
     own_lines = lines(own_slot * frames, frames)
-    upstream_sends = [
-        push(n.upstream.at[own_lines], n.upstream.at[own_lines], n.upstream_sem, (i,), device)
-        for i, device in enumerate((across, sibling))
-    ]
     for slot in range(ROWS):
         turn_tables(
             (0, 2, 1, 3)[slot],
@@ -714,10 +781,6 @@
         stack = jnp.concatenate([high, values - high], axis=0).astype(low)
         chosen = picked(row, rank * frames, frames)[0]
         picker = jnp.where(chosen, 1.0, 0.0).astype(low)[:, :16]
-
-        def per_frame(at, stack=stack, picker=picker, k=k):
-            del at
-
         where = pl.ds(k * frames, frames)
         n.scale_one[where] = 1.0 + dot_plain(picker, stack[:, :width])
         n.shift_one[where] = dot_plain(picker, stack[:, width:])
@@ -741,6 +804,15 @@
 
         tiles(frames, 32, norm_one)
         attn_sends.append(share(n.attn_in, k, n.attn_sem))
+
+    up_sends = [
+        push(up_piece(group(o)), up_place, n.up_sem, (o - 1,), (rank, group(o))) for o in (2, 1, 3)
+    ]
+    upstream_load.wait()
+    upstream_sends = [
+        push(n.upstream.at[own_lines], n.upstream.at[own_lines], n.upstream_sem, (i,), device)
+        for i, device in enumerate((across, sibling))
+    ]
 
     for copy in qkv_loads:
         copy.wait()
@@ -937,6 +1009,7 @@
         n.down_total[at // 128 + 1] = value[128:]
 
     tiles(hidden_units, 256, down_tile)
+    begin(down_ring)
 
     def up_tile(at):
         value = contract_rows(n.ff_in[:, pl.ds(at, columns)], n.grad_widened[...]).astype(low)
@@ -947,6 +1020,8 @@
             ]
 
     tiles(width, columns, up_tile)
+    begin(up_ring)
+    ticks(TICKS[0])
 
     gain_sums = jnp.zeros((1, width), full)
     grad_sends = []
@@ -970,6 +1045,7 @@
 
         gain_sums = lax.fori_loop(0, frames // 32, back_two, gain_sums)
         grad_sends.append(share(n.grad_two_low, k, n.grad_two_sem))
+    ticks(TICKS[1])
     n.mod_sums[8:16] = jnp.zeros((8, 2 * width), full)
     n.mod_sums[8:9, :width] = gain_sums
 
@@ -988,9 +1064,12 @@
     value = contract_rows(n.attended[...], n.grad_two_low[...]).astype(low)
     for j in range(RING):
         n.out_total[j] = value[j * 32 : (j + 1) * 32]
+    begin(out_ring)
+    ticks(TICKS[2])
 
     first = partial_sum(3, n.activated, lambda left, at: dot_plain(left, n.down_held[:, pl.ds(at, 256)]))
     output_second = cross_sum(3, first)
+    ticks(TICKS[3])
 
     heads_arrive(n.grad_pair, n.grad_pair_sem)
 
@@ -1006,6 +1085,7 @@
         return value * n.row_cosine[where] - swapped(value) * n.row_sine[where]
 
     def attend_back(at):
+        at = pl.multiple_of(at, half)
         where = pl.ds(at, half)
         first_head = lax.broadcasted_iota(jnp.int32, (half, 128), 1) < 64
         grad = n.grad_pair[where]
@@ -1029,7 +1109,9 @@
                 query_grad[k * frames : (k + 1) * frames], place
             ).astype(low)
 
-    tiles(all_frames, half, attend_back)
+    for part in range(2):
+        tiles(all_frames // 2, half, lambda at, part=part: attend_back(at + part * all_frames // 2))
+        ticks(TICKS[4 + part])
     project_place = (lines(slot_of(pair_row) * frames, frames), lines(pair_side * 384, 384))
 
     def keys_back(at):
@@ -1065,6 +1147,7 @@
         ).astype(low)
 
     tiles(frames, 32, finish_output)
+    ticks(TICKS[6])
     pairs_arrive(n.grad_project, n.project_sem, 384)
 
     first = partial_sum(
@@ -1081,6 +1164,8 @@
             ]
 
     tiles(width, columns, qkv_tile)
+    begin(qkv_ring)
+    ticks(TICKS[7])
     hidden_sends = []
     for k in range(2):
         second[k].wait_recv()
@@ -1102,6 +1187,7 @@
 
         tiles(frames, 32, back_one)
         hidden_sends.append(share(n.grad_hidden, k, n.grad_hidden_sem))
+    ticks(TICKS[8])
 
     spot = (lax.broadcasted_iota(jnp.int32, (8, frames), 1) + rank * frames).astype(full)
     chosen = (spot >= n.small[1]) & (spot < n.small[2])
@@ -1148,6 +1234,8 @@
             n.skip_total[at // 64 + j] = value[j * 64 : (j + 1) * 64]
 
     tiles(n.joined.shape[1], 256, skip_weight_tile)
+    begin(skip_ring)
+    ticks(TICKS[9])
 
     for copy in sums_copies:
         copy.wait_recv()
@@ -1163,6 +1251,7 @@
         )
         for other in (2, 1, 3)
     ]
+    ticks(TICKS[10])
     for copy in group_sums:
         copy.wait_recv()
     mod_spread = [
@@ -1176,43 +1265,15 @@
         for other in range(1, RING)
     ]
 
-    rings = [
-        Ring(n.down_total, n.down_land, n.down_sem, rank, group_rank),
-        Ring(n.up_total, n.up_land, n.up_ring_sem, rank, group_rank),
-        Ring(n.qkv_total, n.qkv_land, n.qkv_ring_sem, rank, group_rank),
-        Ring(n.skip_total, n.skip_land, n.skip_ring_sem, rank, group_rank),
-        Ring(n.out_total, n.out_land, n.out_ring_sem, rank, group_rank),
-    ]
-    for step in range(RING):
-        for ring in rings:
-            ring.sum_step(step)
-    turns = []
-    for index, (ring, place) in enumerate(((rings[1], n.up_turn), (rings[2], n.qkv_turn))):
-        deep = columns // RING
-        for other in (2, 1, 3):
-            turns.append(
-                push(
-                    ring.total().at[lines(group(other) * deep, deep)],
-                    place.at[lines(group_rank * deep, deep)],
-                    n.turn_sem,
-                    (index, other - 1),
-                    (rank, group(other)),
-                )
-            )
-        place[lines(group_rank * deep, deep)] = ring.land[RING - 2, lines(group_rank * deep, deep)]
-    for ring in (rings[0], rings[3], rings[4]):
-        ring.part[rank] = ring.land[RING - 2]
-    for copy in turns:
-        copy.wait_recv()
-    n.up_total[rank] = n.up_turn[...]
-    n.qkv_total[rank] = n.qkv_turn[...]
-    for step in range(RING):
-        for ring in rings:
-            ring.spread_step(step)
+    ticks(5 * (2 * RING + 1))
     for ring in rings:
         ring.finish()
     for copy in mod_spread + grad_joined_copies:
         copy.wait_recv()
+    gain_grad = n.mod_grad[group_rank, 0, 8:9]
+    for row in range(1, ROWS):
+        gain_grad = gain_grad + n.mod_grad[group_rank, row, 8:9]
+    n.gain_grad[...] = jnp.broadcast_to(gain_grad, n.gain_grad.shape)
     for index, copy in enumerate(sent):
         if not any(copy is other for pair in list(group_copies.values())[:-1] for kind in pair for other in kind):
             copy.wait_send()
@@ -1253,11 +1314,12 @@
         grad_joined=((ROWS, frames, joint), low),
         condition=((ROWS * 8, columns), low),
         mod_grad=((RING, ROWS, 16, 256), full),
-        down_total=((RING, hidden_units // RING, width), low),
-        up_total=((RING, deep, hidden_units), low),
-        qkv_total=((RING, deep, 3 * columns), low),
-        skip_total=((RING, joint // RING, width), low),
-        out_total=((RING, columns // RING, width), low),
+        gain_grad=((8, columns), full),
+        down_whole=((RING, hidden_units // RING, width), low),
+        up_whole=((RING, deep, hidden_units), low),
+        qkv_whole=((RING, deep, 3 * columns), low),
+        skip_whole=((RING, joint // RING, width), low),
+        out_whole=((RING, columns // RING, width), low),
     )
     buffers = dict(
         joined_own=((ROWS, frames, joint), low),
@@ -1320,6 +1382,11 @@
         sums_land=((RING, 16, 256), full),
         sums_send=((16, 256), full),
         joined_send=((tokens, joint), low),
+        down_total=((RING, hidden_units // RING, width), low),
+        up_total=((RING, deep, hidden_units), low),
+        qkv_total=((RING, deep, 3 * columns), low),
+        skip_total=((RING, joint // RING, width), low),
+        out_total=((RING, columns // RING, width), low),
         down_land=((RING - 1, hidden_units // RING, width), low),
         up_land=((RING - 1, deep, hidden_units), low),
         qkv_land=((RING - 1, deep, 3 * columns), low),
@@ -1356,6 +1423,7 @@
         skip_ring_sem=(2, 2, 2, RING - 1),
         out_ring_sem=(2, 2, 2, RING - 1),
         turn_sem=(2, 2, 3),
+        whole_sem=(5, 2, RING),
     )
     names = [*held, *given, *buffers, *sems]
     vmem = pl.BlockSpec(memory_space=pltpu.VMEM)
@@ -1364,13 +1432,107 @@
         functools.partial(block_kernel, names),
         out_shape=[jax.ShapeDtypeStruct(*spec) for spec in given.values()],
         in_specs=[vmem if name == "small" else anywhere for name in held],
-        out_specs=[vmem] * len(given),
+        out_specs=[anywhere if name.endswith("_whole") else vmem for name in given],
         scratch_shapes=[pltpu.VMEM(*spec) for spec in buffers.values()]
         + [pltpu.SemaphoreType.DMA(shape) for shape in sems.values()],
         compiler_params=pltpu.CompilerParams(
             collective_id=0, has_side_effects=True, vmem_limit_bytes=62 * 1024 * 1024
         ),
     )(*held.values())
+
+
+def finish_kernel(
+    joined_ref,
+    condition_ref,
+    mod_ref,
+    gain_ref,
+    down_ref,
+    up_ref,
+    qkv_ref,
+    skip_ref,
+    out_ref,
+    grad_inputs,
+    grad_skipped,
+    grad_skip,
+    grad_mod,
+    grad_qkv,
+    grad_out,
+    grad_gain,
+    grad_up,
+    grad_down,
+):
+    full = jnp.float32
+    wide = joined_ref.shape[2]
+    for r in range(ROWS):
+        target = (grad_inputs, grad_skipped)[r // 2]
+        target[:, pl.ds((r % 2) * wide, wide)] = joined_ref[r].astype(full)
+    grad_down[...] = down_ref[0].astype(full)
+    grad_skip[...] = skip_ref[0].astype(full)
+    grad_out[...] = out_ref[0].astype(full)
+    grad_gain[...] = gain_ref[0:1]
+    deep, wide = up_ref.shape[1] // ROWS, up_ref.shape[2]
+    for r in range(ROWS):
+        rows = pl.ds(r * deep, deep)
+        grad_up[:, pl.ds(r * wide, wide)] = up_ref[0, rows].astype(full)
+        for side in range(2):
+            for kind in range(3):
+                source = qkv_ref[0, rows, pl.ds((side * 3 + kind) * 128, 128)]
+                at = kind * (ROWS * 256) + r * 256 + side * 128
+                grad_qkv[:, pl.ds(at, 128)] = source.astype(full)
+    sums = jnp.concatenate([mod_ref[0, r, 0:8] for r in (0, 2, 1, 3)], axis=0)
+    high = sums.astype(jnp.bfloat16)
+    rest = (sums - high.astype(full)).astype(jnp.bfloat16)
+    grad_mod[...] = contract_rows(condition_ref[...], high) + contract_rows(
+        condition_ref[...], rest
+    )
+
+
+def finish_call(joined, condition, mod, gain, down, up, qkv, skip, out):
+    full = jnp.float32
+    frames, wide = joined.shape[1:]
+    columns = condition.shape[1]
+
+    def first(shape):
+        return pl.BlockSpec((1,) + shape[1:], lambda i: (i,) + (0,) * (len(shape) - 1))
+
+    def rows(count, width):
+        return jax.ShapeDtypeStruct((count, width), full), pl.BlockSpec(
+            (count // RING, width), lambda i: (i, 0)
+        )
+
+    deep = up.shape[1] // ROWS
+    results = [
+        rows(frames, 2 * wide),
+        rows(frames, 2 * wide),
+        rows(RING * skip.shape[1], skip.shape[2]),
+        (
+            jax.ShapeDtypeStruct((columns, RING * mod.shape[3]), full),
+            pl.BlockSpec((columns, mod.shape[3]), lambda i: (0, i)),
+        ),
+        rows(RING * deep, ROWS * qkv.shape[2]),
+        rows(RING * out.shape[1], out.shape[2]),
+        (jax.ShapeDtypeStruct((1, columns), full), pl.BlockSpec((1, columns), lambda i: (0, 0))),
+        rows(RING * deep, ROWS * up.shape[2]),
+        rows(RING * down.shape[1], down.shape[2]),
+    ]
+    return pl.pallas_call(
+        finish_kernel,
+        grid=(RING,),
+        out_shape=[shape for shape, _ in results],
+        in_specs=[
+            pl.BlockSpec((ROWS, frames // RING, wide), lambda i: (0, i, 0)),
+            pl.BlockSpec(condition.shape, lambda i: (0, 0)),
+            first(mod.shape),
+            pl.BlockSpec(gain.shape, lambda i: (0, 0)),
+            first(down.shape),
+            first(up.shape),
+            first(qkv.shape),
+            first(skip.shape),
+            first(out.shape),
+        ],
+        out_specs=[spec for _, spec in results],
+        compiler_params=pltpu.CompilerParams(vmem_limit_bytes=62 * 1024 * 1024),
+    )(joined, condition, mod, gain, down, up, qkv, skip, out)
 
 
 def small_table(lengths_row, steps_row, gain):
@@ -1418,37 +1580,21 @@
     columns = width // ROWS
     group_rank = lax.axis_index("grp")
     small = small_table(lengths[0], flow_steps[0], ff_gain)
-    output, grad_joined, condition, mod_grad, down, up, qkv, skip, out = block_call(
+    output, *rest = block_call(
         inputs[0], skipped[0], w_skip, w_mod, w_qkv, w_out, w_up, w_down, cotangent[0], small
     )
-
-    def rows_back(total):
-        return total.astype(jnp.float32).reshape(-1, total.shape[2])
-
-    up = jnp.transpose(
-        up.astype(jnp.float32).reshape(RING, ROWS, columns // RING, -1), (0, 2, 1, 3)
-    ).reshape(columns, -1)
-    qkv = jnp.transpose(
-        qkv.astype(jnp.float32).reshape(RING, ROWS, columns // RING, 2, 3, columns // 2),
-        (0, 2, 4, 1, 3, 5),
-    ).reshape(columns, -1)
-    joined = grad_joined.astype(jnp.float32)
-    mod = jnp.transpose(mod_grad, (1, 2, 0, 3)).reshape(ROWS, 16, 2 * width)
-    gain = jnp.sum(mod[:, 8, :width], axis=0)
-    gain = lax.dynamic_slice_in_dim(gain, group_rank * columns, columns)
-    slots = jnp.concatenate([mod[r, :8] for r in (0, 2, 1, 3)], axis=0)
-    grad_mod = jnp.dot(condition.astype(jnp.float32).T, slots, precision=HIGHEST)
+    grad_inputs, grad_skipped, skip, mod, qkv, out, gain, up, down = finish_call(*rest)
     return (
         output[None],
-        jnp.concatenate([joined[0], joined[1]], axis=1)[None],
-        jnp.concatenate([joined[2], joined[3]], axis=1)[None],
-        rows_back(skip),
-        grad_mod,
+        grad_inputs[None],
+        grad_skipped[None],
+        skip,
+        mod,
         qkv,
-        rows_back(out),
-        gain,
+        out,
+        gain[0],
         up,
-        rows_back(down),
+        down,
     )
 
 

time: 375 us -> 311 us (0.83)
  Pallas kernels: 336 us -> 305 us
  local copies, waits for them, and re-layouts: 23.8 us -> 2.43 us
  other arithmetic: 10.7 us -> 2.15 us
    pallas_call x1, Pallas kernels: 336 us -> 294 us  [block_call(): pl.pallas_call(functools.partial(block_kernel, names), out_shape=[jax.Sha...]
    reshape x5 -> x0, local copies, waits for them, and re-layouts: 14.6 us -> none  [the longest x3 10.7 us: per_device_block(): qkv = jnp.transpose(qkv.astype(jnp.float32).reshape(RING, ROWS, columns /...]
    pallas_call x0 -> x1, Pallas kernels: none -> 10.8 us  [finish_call(): pl.pallas_call(finish_kernel, grid=(RING,), out_shape=[shape for shape, _...]
    reshape x4 -> x0, other arithmetic: 7.38 us -> none  [the longest x3 6.91 us: rows_back(): return total.astype(jnp.float32).reshape(-1, total.shape[2])]
    unnamed x22 -> x11, local copies, waits for them, and re-layouts: 7.55 us -> 1.52 us
where the time goes in v4:
time: 311 us; the launch traced here: 310 us
  Pallas kernels  305 us (98%)
    pallas_call x1, Pallas kernels, block_call(): pl.pallas_call(functools.partial(block_kernel, names), out_shape=[jax.Sha...  294 us
    pallas_call x1, Pallas kernels, finish_call(): pl.pallas_call(finish_kernel, grid=(RING,), out_shape=[shape for shape, _...  10.8 us

profile of v4, /device:TPU:0, one launch (start us, length us, event | category | flops | bytes accessed | tf_op | source)
XLA Modules:
  0.0 310.1 jit_solution(8556295895235708199)
XLA Ops:
  0.6 0.8 reduce-window.9
  1.5 0.7 bitcast_subtract_fusion
  2.1 0.7 convert_bitcast_fusion.1
  2.8 0.1 concatenate.6
  2.9 0.1 concatenate.7
  3.0 0.7 fusion
  3.7 0.1 constant_dynamic-update-slice_fusion.6
  3.8 0.1 constant_dynamic-update-slice_fusion.5
  3.8 0.1 constant_dynamic-update-slice_fusion.4
  3.9 0.0 copy-start.1
  3.9 0.6 copy-done.1
  4.5 294.0 %shard_map.195 = (bf16[128,1024]{1,0:T(8,128)(2,1)}, bf16[4,128,512]{2,1,0:T(8,128)(2,1)}, bf16[32,256]{1,0:T(8,128)(2,1)}, f32[8,4,16,256]{3,2,1,0:T(8,128)}, f...) custom-call(bf16[128,1024]{1,0:T(8,128)(2,1)} %bitcast.16, ...), custom_call_target="tpu_custom_call" | custom-call | tf_op jit(solution)/shard_map/pallas_call | solution.py:1431
  298.6 0.0 copy-start
  298.6 10.8 %shard_map.196 = (f32[128,1024]{1,0:T(8,128)}, f32[128,1024]{1,0:T(8,128)}, f32[512,1024]{1,0:T(8,128)}, f32[256,2048]{1,0:T(8,128)}, f32[256,3072]{1,0:T(8,128)...) custom-call(bf16[4,128,512]{2,1,0:T(8,128)(2,1)} %get-tuple-element.30.joined_ref, ...), custom_call_target="tpu_custom_call" | custom-call | tf_op jit(solution)/shard_map/pallas_call | solution.py:1518
  309.3 0.0 copy-done
  309.4 0.7 copy.29
  (7 shorter events, 0.0 us)
Async XLA Ops:
  3.9 0.6 copy-start.1
  298.6 10.8 %copy-start = (bf16[128,1024]{1,0:T(8,128)(2,1)S(1)}, bf16[128,1024]{1,0:T(8,128)(2,1)}, u32[]{:S(2)}) copy-start(bf16[128,1024]{1,0:T(8,128)(2,1)} %get-tuple-element.29) | copy-start | bytes 786436

commit v5 on v4

--- a/solution.py
+++ b/solution.py
@@ -381,7 +381,7 @@
     return (1 - upper) * (2 * place) + upper * (15 - 2 * place)
 
 
-TICKS = (2, 1, 1, 2, 2, 1, 5, 3, 1, 3, 4)
+TICKS = (1, 1, 0, 1, 0, 1, 0, 1, 1, 0, 1, 0, 1, 2, 1, 1, 1, 1, 0, 2, 1, 1, 2)
 
 
 class Ring:
@@ -566,18 +566,21 @@
     upstream_load = load(n.cotangent, n.upstream.at[lines(own_slot * frames, frames)], 4)
     skip_load = load(n.w_skip, n.skip_held, 5)
     mod_load = load(n.w_mod, n.mod_held, 6)
-    out_load = load(n.w_out, n.out_held, 7)
+    out_place = n.out_held.at[lines(group_rank * columns, columns)]
+    out_load = load(n.w_out, out_place, 7)
     down_load = load(n.w_down, n.down_held, 8)
     pieces = [(side, kind) for side in range(2) for kind in range(3)]
 
-    def qkv_piece(target, side, kind):
-        return n.w_qkv.at[:, pl.ds(pl.multiple_of(kind * width + target * columns + side * 128, 128), 128)]
-
-    def qkv_place(side, kind):
-        return n.qkv_held.at[lines(group_rank * columns, columns), pl.ds((side * 3 + kind) * 128, 128)]
+    def qkv_piece(target, side, kind, first, count):
+        at = pl.multiple_of(kind * width + target * columns + side * 128, 128)
+        return n.w_qkv.at[lines(first, count), pl.ds(at, 128)]
+
+    def qkv_place(side, kind, first, count):
+        rows = lines(group_rank * columns + first, count)
+        return n.qkv_held.at[rows, pl.ds((side * 3 + kind) * 128, 128)]
 
     qkv_loads = [
-        load(qkv_piece(group_rank, *piece), qkv_place(*piece), 9 + i)
+        load(qkv_piece(group_rank, *piece, 0, columns), qkv_place(*piece, 0, columns), 9 + i)
         for i, piece in enumerate(pieces)
     ]
     hidden_units = n.up_held.shape[1]
@@ -587,12 +590,36 @@
 
     up_place = n.up_held.at[lines(group_rank * columns, columns)]
     up_load = load(up_piece(group_rank), up_place, 15)
+
+    def small_tables():
+        down = lax.broadcasted_iota(jnp.int32, (8, 128), 0)
+        across_lanes = lax.rem(lax.broadcasted_iota(jnp.int32, (8, 128), 1), 64)
+        zero = jnp.zeros((8, 128), full)
+        step_tile, start_tile, end_tile = zero, zero, zero
+        start_lane, end_lane = zero + 1e9, zero
+        start = jnp.int32(0)
+        for u in range(8):
+            end = start + n.lengths[0, u]
+            here = down == u
+            lane_here = (across_lanes == u) | (across_lanes == u + 8)
+            step_tile = jnp.where(here, n.flow_steps[0, u].astype(full), step_tile)
+            start_tile = jnp.where(here, start.astype(full), start_tile)
+            end_tile = jnp.where(here, end.astype(full), end_tile)
+            start_lane = jnp.where(lane_here, start.astype(full), start_lane)
+            end_lane = jnp.where(lane_here, end.astype(full), end_lane)
+            start = end
+        tables = (step_tile, start_tile, end_tile, start_lane, end_lane)
+        for i, tile in enumerate(tables):
+            n.small[i] = tile
+        n.small[5] = n.own_gain[:, 0:128]
+        n.small[6] = n.own_gain[:, 128:256]
 
     barrier = pltpu.get_barrier_semaphore()
     for other in range(1, ROWS):
         pl.semaphore_signal(barrier, inc=1, device_id=(rank, group(other)), device_id_type=MESH)
     for other in range(1, RING):
         pl.semaphore_signal(barrier, inc=1, device_id=(block(other), group_rank), device_id_type=MESH)
+    small_tables()
     for copy in joined_loads:
         copy.wait()
     pl.semaphore_wait(barrier, ROWS + RING - 2)
@@ -605,17 +632,6 @@
     small_sends = [
         push(n.small, n.smalls.at[group_rank], n.small_sem, (o - 1,), (rank, group(o)))
         for o in (2, 1, 3)
-    ]
-    qkv_sends = [
-        push(
-            qkv_piece(group(o), *piece),
-            qkv_place(*piece),
-            n.qkv_sem,
-            (o - 1, i),
-            (rank, group(o)),
-        )
-        for o in (2, 1, 3)
-        for i, piece in enumerate(pieces)
     ]
     n.joined[lines(own_slot * frames, frames)] = n.joined_own[group_rank]
     n.smalls[group_rank] = n.small[...]
@@ -754,14 +770,48 @@
     for copy in joined_sends:
         copy.wait_recv()
 
+    side_y, side_z = lax.rem(rank, 2), lax.rem(rank // 2, 2)
+    to_y, to_z = 1 - 2 * side_y, 2 - 4 * side_z
+    beside = (rank + to_y, group_rank)
+    around = (beside, (rank + to_z, group_rank), (rank + to_y + to_z, group_rank))
+    part_rows = columns // 2
+    few_rows = columns // 4
+    first_row = (2 * side_z + side_y) * few_rows
+    over_x = (group_rank + 2 - 4 * chip, 2 * (1 - chip) + 1 - core)
+    qkv_sends = [
+        [
+            push(
+                qkv_piece(to, *piece, first_row, few_rows),
+                qkv_place(*piece, first_row, few_rows),
+                n.qkv_sem,
+                (i, j),
+                (rank, to),
+            )
+            for j, piece in enumerate(pieces)
+        ]
+        for i, to in enumerate(over_x)
+    ]
+    qkv_sends.append(
+        [
+            push(
+                qkv_piece(sibling[1], *piece, 0, columns),
+                qkv_place(*piece, 0, columns),
+                n.qkv_sem,
+                (2, j),
+                sibling,
+            )
+            for j, piece in enumerate(pieces)
+        ]
+    )
+
     def skip_tile(left, at):
         return dot_plain(left, n.skip_held[:, pl.ds(at, 256)])
 
     first = partial_sum(0, n.joined, skip_tile)
     mod_first.wait_recv()
     mod_mine = n.mod_part[pl.ds(pl.multiple_of(16 * core, 16), 16)] + n.mod_land[0]
-    n.mod_send[...] = mod_mine
-    mod_second = push(n.mod_send, n.mod_land.at[1], n.mod_sem, (1,), across)
+    n.mod_send[...] = mod_mine.astype(low)
+    mod_second = push(n.mod_send, n.mod_cross, n.mod_sem, (1,), across)
     second = cross_sum(0, first)
     own_lines = lines(own_slot * frames, frames)
     for slot in range(ROWS):
@@ -773,7 +823,7 @@
             pl.ds(slot * frames, frames),
         )
     mod_second.wait_recv()
-    mod_total = n.mod_send[...] + n.mod_land[1]
+    mod_total = n.mod_send[...].astype(full) + n.mod_cross[...].astype(full)
     for k in range(2):
         row = 2 * k + core
         values = mod_total[8 * k : 8 * k + 8]
@@ -785,6 +835,13 @@
         n.scale_one[where] = 1.0 + dot_plain(picker, stack[:, :width])
         n.shift_one[where] = dot_plain(picker, stack[:, width:])
 
+    qkv_passed = []
+    for i, source in enumerate(over_x):
+        for copy in qkv_sends[i]:
+            copy.wait_recv()
+        where = n.qkv_held.at[lines(source * columns + first_row, few_rows)]
+        for j, to in enumerate(around):
+            qkv_passed.append(push(where, where, n.qkv_pass_sem, (i, j), to))
     attn_sends = []
     for k in range(2):
         second[k].wait_recv()
@@ -805,9 +862,32 @@
         tiles(frames, 32, norm_one)
         attn_sends.append(share(n.attn_in, k, n.attn_sem))
 
+    def part_of(reference, first):
+        return reference.at[lines(first + side_y * part_rows, part_rows)]
+
     up_sends = [
-        push(up_piece(group(o)), up_place, n.up_sem, (o - 1,), (rank, group(o))) for o in (2, 1, 3)
+        push(
+            part_of(up_piece(to), 0),
+            part_of(n.up_held, group_rank * columns),
+            n.up_sem,
+            (i,),
+            (rank, to),
+        )
+        for i, to in enumerate(over_x)
     ]
+    up_sends.append(push(up_piece(sibling[1]), up_place, n.up_sem, (2,), sibling))
+    out_sends = [
+        push(n.w_out, out_place, n.out_sem, (i,), device) for i, device in enumerate((across, sibling))
+    ]
+
+    def pass_on(buffer, copies, sems):
+        passed = []
+        for i, source in enumerate(over_x):
+            copies[i].wait_recv()
+            where = part_of(buffer, source * columns)
+            passed.append(push(where, where, sems, (i,), beside))
+        return passed
+
     upstream_load.wait()
     upstream_sends = [
         push(n.upstream.at[own_lines], n.upstream.at[own_lines], n.upstream_sem, (i,), device)
@@ -816,22 +896,22 @@
 
     for copy in qkv_loads:
         copy.wait()
-    for copy in qkv_sends:
+    for copy in qkv_sends[2] + qkv_passed:
         copy.wait_recv()
 
-    def to_heads(offset, value_of, target, sems, wide, send_buffer):
+    def to_heads(offset, value_of, target, sems, send_buffer, columns_of):
         for k in range(2):
             slot = offset // frames + k
             for side in range(2):
                 to = 2 * row_of(slot) + side
-                value = value_of(k, side, slot)
+                if value_of is not None:
+                    send_buffer[to] = value_of(k, side, slot)
 
                 @pl.when(to != rank)
                 def _():
-                    send_buffer[to] = value
                     link(
-                        send_buffer.at[to],
-                        target.at[lines(rank * frames, frames)],
+                        send_buffer.at[to, :, columns_of],
+                        target.at[lines(rank * frames, frames), columns_of],
                         sems.at[0, to],
                         sems.at[1, rank],
                         (to, group_rank),
@@ -839,12 +919,12 @@
 
                 @pl.when(to == rank)
                 def _():
-                    target[lines(rank * frames, frames)] = value
-
-    def heads_arrive(target, sems):
+                    target[lines(rank * frames, frames), columns_of] = send_buffer[to, :, columns_of]
+
+    def heads_arrive(target, sems, columns_of):
         for other in range(1, RING):
             source = block(other)
-            where = target.at[lines(source * frames, frames)]
+            where = target.at[lines(source * frames, frames), columns_of]
             link(where, where, sems.at[0, source], sems.at[1, source], (source, group_rank)).wait_recv()
 
     def project_half(offset):
@@ -866,12 +946,14 @@
                 blocks.append(value.astype(low))
             return jnp.concatenate(blocks, axis=1)
 
-        to_heads(offset, value_of, n.paired, n.pair_sem, 384, n.pair_send)
+        to_heads(offset, value_of, n.paired, n.pair_sem, n.pair_send, pl.ds(0, 256))
 
     project_half(mine)
     for copy in attn_sends:
         copy.wait_recv()
     project_half(theirs)
+    for offset in (mine, theirs):
+        to_heads(offset, None, n.paired, n.value_sem, n.pair_send, pl.ds(256, 128))
 
     def row_tables(at):
         turn_tables(pair_row, at, n.row_cosine, n.row_sine, pl.ds(at, frames))
@@ -879,7 +961,11 @@
         n.chosen[pl.ds(at, frames)] = chosen.astype(low)
 
     tiles(RING * frames, frames, row_tables)
-    heads_arrive(n.paired, n.pair_sem)
+    heads_arrive(n.paired, n.pair_sem, pl.ds(0, 256))
+    up_passed = pass_on(n.up_held, up_sends, n.up_pass_sem)
+    out_sends[0].wait_recv()
+    where = n.out_held.at[lines(across[1] * columns, columns)]
+    out_sends.append(push(where, where, n.out_sem, (2,), sibling))
 
     def masked_parts(at):
         where = pl.ds(at, frames)
@@ -900,17 +986,21 @@
     all_frames = RING * frames
     pair_place = (lines(slot_of(pair_row) * frames, frames), lines(pair_side * 128, 128))
 
-    def attend(at):
+    def score(at):
         where = pl.ds(at, half)
-        sums = []
         for head in range(2):
             scores = dot_across(n.query_head[head, where], n.key_head[head])
             top = jnp.max(scores, axis=1, keepdims=True)
             weights = jnp.exp(scores - top)
             total = jnp.sum(weights, axis=1, keepdims=True)
-            shares = (weights * (1.0 / total)).astype(low)
-            n.shares[head, where] = shares
-            sums.append(dot_plain(shares, n.paired[:, 256:384]))
+            n.shares[head, where] = (weights * (1.0 / total)).astype(low)
+
+    tiles(all_frames, half, score)
+    heads_arrive(n.paired, n.value_sem, pl.ds(256, 128))
+
+    def attend(at):
+        where = pl.ds(at, half)
+        sums = [dot_plain(n.shares[head, where], n.paired[:, 256:384]) for head in range(2)]
         first_head = lax.broadcasted_iota(jnp.int32, (half, 128), 1) < 64
         value = jnp.where(first_head, sums[0], sums[1])
         n.attended_pair[where] = value
@@ -935,12 +1025,12 @@
 
     tiles(all_frames, half, attend)
 
-    def pairs_arrive(buffer, sems, wide):
+    def pairs_arrive(buffer, sems, pitch, first, wide):
         for other in range(1, RING):
             source = block(other)
             where = buffer.at[
                 lines(slot_of(source // 2) * frames, frames),
-                pl.ds(pl.multiple_of(lax.rem(source, 2) * wide, 128), wide),
+                pl.ds(pl.multiple_of(lax.rem(source, 2) * pitch + first, 128), wide),
             ]
             link(where, where, sems.at[0, source], sems.at[1, source], (source, group_rank)).wait_recv()
 
@@ -949,18 +1039,36 @@
     upstream_sends.append(
         push(n.upstream.at[other_lines], n.upstream.at[other_lines], n.upstream_sem, (2,), sibling)
     )
-    pairs_arrive(n.attended, n.attended_sem, 128)
-
+    pairs_arrive(n.attended, n.attended_sem, 128, 0, 128)
+
+    own_columns = pl.ds(pl.multiple_of(group_rank * columns, columns), columns)
+    attended_sends = [
+        push(
+            n.attended.at[lines(first, half)],
+            n.attended_all.at[:, own_columns],
+            n.attended_all_sem,
+            (i,),
+            (rank, to),
+        )
+        for i, (first, to) in enumerate(
+            ((mine, over_x[0]), (theirs, over_x[1]), (theirs, sibling[1]))
+        )
+    ]
+    n.attended_all[:, own_columns] = n.attended[lines(mine, half)]
     out_load.wait()
-    first = partial_sum(1, n.attended, lambda left, at: dot_plain(left, n.out_held[:, pl.ds(at, 256)]))
-    second = cross_sum(1, first)
+    for copy in out_sends[1:] + attended_sends:
+        copy.wait_recv()
+
+    def out_tile(at):
+        n.keep[:, pl.ds(at, 256)] = dot_plain(n.attended_all[...], n.out_held[:, pl.ds(at, 256)])
+
+    tiles(width, 256, out_tile)
     ff_sends = []
     for k in range(2):
-        second[k].wait_recv()
 
         def norm_two(at, k=k):
             where = pl.ds(k * frames + at, 32)
-            hidden = n.hidden[where] + n.keep[where] + n.land_two[1, where].astype(full)
+            hidden = n.hidden[where] + n.keep[where]
             n.hidden[where] = hidden
             centred = hidden - mean(hidden)
             spread = lax.rsqrt(mean(centred * centred) + EPSILON)
@@ -974,7 +1082,7 @@
 
     up_load.wait()
     down_load.wait()
-    for copy in up_sends:
+    for copy in up_sends[2:] + up_passed:
         copy.wait_recv()
     for copy in upstream_sends[1:]:
         copy.wait_recv()
@@ -999,9 +1107,9 @@
         copy.wait_recv()
     feed_half(theirs)
     first = partial_sum(
-        2, n.grad_widened, lambda left, at: dot_across(left, n.up_held[pl.ds(at, 256)])
-    )
-    second = cross_sum(2, first)
+        1, n.grad_widened, lambda left, at: dot_across(left, n.up_held[pl.ds(at, 256)])
+    )
+    second = cross_sum(1, first)
 
     def down_tile(at):
         value = contract_rows(n.activated[:, pl.ds(at, 256)], n.upstream[...]).astype(low)
@@ -1032,7 +1140,7 @@
         def back_two(i, sums, k=k, weight=weight):
             at = pl.multiple_of(i * 32, 32)
             where = pl.ds(k * frames + at, 32)
-            grad = n.keep[where] + n.land_two[2, where].astype(full)
+            grad = n.keep[where] + n.land_two[1, where].astype(full)
             normal = n.normal_two[where]
             scaled = grad * n.gain[0:1]
             back = n.spread_two[where][:, 0:1] * (
@@ -1045,33 +1153,40 @@
 
         gain_sums = lax.fori_loop(0, frames // 32, back_two, gain_sums)
         grad_sends.append(share(n.grad_two_low, k, n.grad_two_sem))
-    ticks(TICKS[1])
+        ticks(TICKS[1 + k])
     n.mod_sums[8:16] = jnp.zeros((8, 2 * width), full)
     n.mod_sums[8:9, :width] = gain_sums
 
     def attended_half(offset):
-        value = dot_across(n.grad_two_low[lines(offset, half)], n.out_held[...]).astype(low)
+        value = dot_across(
+            n.grad_two_low[lines(offset, half)], n.out_held[lines(group_rank * columns, columns)]
+        ).astype(low)
 
         def value_of(k, side, slot):
             return value[k * frames : (k + 1) * frames, side * 128 : side * 128 + 128]
 
-        to_heads(offset, value_of, n.grad_pair, n.grad_pair_sem, 128, n.grad_pair_send)
+        to_heads(
+            offset, value_of, n.grad_pair, n.grad_pair_sem, n.grad_pair_send, pl.ds(0, 128)
+        )
 
     attended_half(mine)
+    ticks(TICKS[3])
     for copy in grad_sends:
         copy.wait_recv()
     attended_half(theirs)
+    ticks(TICKS[4])
     value = contract_rows(n.attended[...], n.grad_two_low[...]).astype(low)
     for j in range(RING):
         n.out_total[j] = value[j * 32 : (j + 1) * 32]
     begin(out_ring)
-    ticks(TICKS[2])
-
-    first = partial_sum(3, n.activated, lambda left, at: dot_plain(left, n.down_held[:, pl.ds(at, 256)]))
-    output_second = cross_sum(3, first)
-    ticks(TICKS[3])
-
-    heads_arrive(n.grad_pair, n.grad_pair_sem)
+    ticks(TICKS[5])
+
+    first = partial_sum(2, n.activated, lambda left, at: dot_plain(left, n.down_held[:, pl.ds(at, 256)]))
+    ticks(TICKS[6])
+    output_second = cross_sum(2, first)
+    ticks(TICKS[7])
+
+    heads_arrive(n.grad_pair, n.grad_pair_sem, pl.ds(0, 128))
 
     def turn_upstream(at):
         where = pl.ds(at, frames)
@@ -1084,8 +1199,22 @@
     def back_turned(value, where):
         return value * n.row_cosine[where] - swapped(value) * n.row_sine[where]
 
+    project_slot = lines(slot_of(pair_row) * frames, frames)
+
+    def project_back(to, place, first, wide, sems):
+        source = n.project_send.at[place, pl.ds(first, wide)]
+        at = pl.ds(pl.multiple_of(pair_side * 384 + first, 128), wide)
+
+        @pl.when(to != rank)
+        def _():
+            target = n.grad_project.at[project_slot, at]
+            link(source, target, sems.at[0, to], sems.at[1, rank], (to, group_rank)).start()
+
+        @pl.when(to == rank)
+        def _():
+            n.grad_project[project_slot, at] = source[...]
+
     def attend_back(at):
-        at = pl.multiple_of(at, half)
         where = pl.ds(at, half)
         first_head = lax.broadcasted_iota(jnp.int32, (half, 128), 1) < 64
         grad = n.grad_pair[where]
@@ -1108,34 +1237,21 @@
             n.project_send[place, 0:128] = back_turned(
                 query_grad[k * frames : (k + 1) * frames], place
             ).astype(low)
-
-    for part in range(2):
-        tiles(all_frames // 2, half, lambda at, part=part: attend_back(at + part * all_frames // 2))
-        ticks(TICKS[4 + part])
-    project_place = (lines(slot_of(pair_row) * frames, frames), lines(pair_side * 384, 384))
-
+            project_back(at // frames + k, place, 0, 128, n.query_sem)
+
+    for part in range(4):
+        attend_back(part * half)
+        ticks(TICKS[8 + part])
     def keys_back(at):
         place = pl.ds(at, frames)
         key_grad = jnp.transpose(n.key_turned[:, place]) * HEAD_DIM ** (-0.5)
         n.project_send[place, 128:256] = back_turned(key_grad, place).astype(low)
         n.project_send[place, 256:384] = jnp.transpose(n.value_turned[:, place]).astype(low)
-        to = at // frames
-
-        @pl.when(to != rank)
-        def _():
-            link(
-                n.project_send.at[place],
-                n.grad_project.at[project_place],
-                n.project_sem.at[0, to],
-                n.project_sem.at[1, rank],
-                (to, group_rank),
-            ).start()
-
-        @pl.when(to == rank)
-        def _():
-            n.grad_project[project_place] = n.project_send[place]
+        project_back(at // frames, place, 128, 256, n.project_sem)
 
     tiles(all_frames, frames, keys_back)
+
+    ticks(TICKS[12])
 
     for copy in output_second:
         copy.wait_recv()
@@ -1143,17 +1259,20 @@
     def finish_output(at):
         where = lines(chip * frames + at, 32)
         n.output[pl.ds(at, 32)] = (
-            n.hidden[where] + n.keep[where] + n.land_two[3, where].astype(full)
+            n.hidden[where] + n.keep[where] + n.land_two[2, where].astype(full)
         ).astype(low)
 
     tiles(frames, 32, finish_output)
-    ticks(TICKS[6])
-    pairs_arrive(n.grad_project, n.project_sem, 384)
+    ticks(TICKS[13])
+    pairs_arrive(n.grad_project, n.query_sem, 384, 0, 128)
+    pairs_arrive(n.grad_project, n.project_sem, 384, 128, 256)
 
     first = partial_sum(
-        4, n.grad_project, lambda left, at: dot_across(left, n.qkv_held[pl.ds(at, 256)])
-    )
-    second = cross_sum(4, first)
+        3, n.grad_project, lambda left, at: dot_across(left, n.qkv_held[pl.ds(at, 256)])
+    )
+    ticks(TICKS[14])
+    second = cross_sum(3, first)
+    ticks(TICKS[15])
 
     def qkv_tile(at):
         value = contract_rows(n.attn_in[:, pl.ds(at, columns)], n.grad_project[...]).astype(low)
@@ -1165,14 +1284,14 @@
 
     tiles(width, columns, qkv_tile)
     begin(qkv_ring)
-    ticks(TICKS[7])
+    ticks(TICKS[16])
     hidden_sends = []
     for k in range(2):
         second[k].wait_recv()
 
         def back_one(at, k=k):
             where = pl.ds(k * frames + at, 32)
-            grad = n.keep[where] + n.land_two[4, where].astype(full)
+            grad = n.keep[where] + n.land_two[3, where].astype(full)
             normal = n.normal_one[where]
             scaled = grad * n.scale_one[where]
             back = n.spread_one[where][:, 0:1] * (
@@ -1182,22 +1301,35 @@
 
             @pl.when(chip == k)
             def _():
-                n.mod_terms[pl.ds(at, 32), :width] = grad * normal
-                n.mod_terms[pl.ds(at, 32), width:] = grad
+                n.shift_one[pl.ds(at, 32)] = grad * normal
+                n.shift_one[pl.ds(frames + at, 32)] = grad
 
         tiles(frames, 32, back_one)
         hidden_sends.append(share(n.grad_hidden, k, n.grad_hidden_sem))
-    ticks(TICKS[8])
-
+        ticks(TICKS[17 + k])
+
+    for copy in hidden_sends:
+        copy.wait_recv()
+
+    def skip_weight_tile(at):
+        value = contract_rows(n.joined[:, pl.ds(at, 256)], n.grad_hidden[...]).astype(low)
+        for j in range(4):
+            n.skip_total[at // 64 + j] = value[j * 64 : (j + 1) * 64]
+
+    tiles(n.joined.shape[1], 256, skip_weight_tile)
+    begin(skip_ring)
+    ticks(TICKS[19])
     spot = (lax.broadcasted_iota(jnp.int32, (8, frames), 1) + rank * frames).astype(full)
     chosen = (spot >= n.small[1]) & (spot < n.small[2])
     picker = jnp.where(chosen, 1.0, 0.0)
 
     def mod_sum(at):
-        where = pl.ds(at, 512)
-        n.mod_sums[0:8, where] = jnp.dot(picker, n.mod_terms[:, where], precision=HIGHEST)
-
-    tiles(2 * width, 512, mod_sum)
+        for part in range(2):
+            n.mod_sums[0:8, pl.ds(part * width + at, 512)] = jnp.dot(
+                picker, n.shift_one[pl.ds(part * frames, frames), pl.ds(at, 512)], precision=HIGHEST
+            )
+
+    tiles(width, 512, mod_sum)
     for other in range(1, RING):
         to = block(other)
         push(
@@ -1209,9 +1341,7 @@
         )
     sums_copies = sent[-(RING - 1) :]
     n.sums_land[rank] = n.mod_sums[:, pl.ds(pl.multiple_of(rank * 256, 256), 256)]
-
-    for copy in hidden_sends:
-        copy.wait_recv()
+    ticks(TICKS[20])
     back = dot_across(n.grad_hidden[...], n.skip_held[...]).astype(low)
     n.joined_send[...] = back
     grad_joined_copies = []
@@ -1227,19 +1357,10 @@
             )
         )
     n.grad_joined[group_rank] = n.joined_send[own_lines]
-
-    def skip_weight_tile(at):
-        value = contract_rows(n.joined[:, pl.ds(at, 256)], n.grad_hidden[...]).astype(low)
-        for j in range(4):
-            n.skip_total[at // 64 + j] = value[j * 64 : (j + 1) * 64]
-
-    tiles(n.joined.shape[1], 256, skip_weight_tile)
-    begin(skip_ring)
-    ticks(TICKS[9])
-
+    ticks(TICKS[21])
     for copy in sums_copies:
         copy.wait_recv()
-    n.sums_send[...] = jnp.sum(n.sums_land[...], axis=0)
+    n.sums_send[...] = jnp.sum(n.sums_land[...], axis=0).astype(low)
     n.mod_grad[rank, group_rank] = n.sums_send[...]
     group_sums = [
         push(
@@ -1251,7 +1372,7 @@
         )
         for other in (2, 1, 3)
     ]
-    ticks(TICKS[10])
+    ticks(TICKS[22])
     for copy in group_sums:
         copy.wait_recv()
     mod_spread = [
@@ -1270,23 +1391,40 @@
         ring.finish()
     for copy in mod_spread + grad_joined_copies:
         copy.wait_recv()
-    gain_grad = n.mod_grad[group_rank, 0, 8:9]
+    gain_grad = n.mod_grad[group_rank, 0].astype(full)
     for row in range(1, ROWS):
-        gain_grad = gain_grad + n.mod_grad[group_rank, row, 8:9]
-    n.gain_grad[...] = jnp.broadcast_to(gain_grad, n.gain_grad.shape)
+        gain_grad = gain_grad + n.mod_grad[group_rank, row].astype(full)
+    n.gain_grad[...] = gain_grad[8:16]
     for index, copy in enumerate(sent):
         if not any(copy is other for pair in list(group_copies.values())[:-1] for kind in pair for other in kind):
             copy.wait_send()
-    for sems, wide in ((n.pair_sem, 384), (n.attended_sem, 128), (n.grad_pair_sem, 128), (n.project_sem, 384)):
-        buffer = {384: n.project_send, 128: n.attended_send}[wide]
+    for sems, wide in (
+        (n.pair_sem, 256),
+        (n.value_sem, 128),
+        (n.attended_sem, 128),
+        (n.grad_pair_sem, 128),
+        (n.query_sem, 128),
+        (n.project_sem, 256),
+    ):
         for other in range(1, RING):
             to = block(other)
-            where = buffer.at[lines(to * frames, frames)]
+            where = n.project_send.at[lines(to * frames, frames), pl.ds(0, wide)]
             link(where, where, sems.at[0, to], sems.at[1, to], (to, group_rank)).wait_send()
 
 
 def block_call(
-    inputs, skipped, w_skip, w_mod, w_qkv, w_out, w_up, w_down, cotangent, small
+    inputs,
+    skipped,
+    w_skip,
+    w_mod,
+    w_qkv,
+    w_out,
+    w_up,
+    w_down,
+    cotangent,
+    own_gain,
+    lengths,
+    flow_steps,
 ):
     low, full = jnp.bfloat16, jnp.float32
     frames, width = inputs.shape
@@ -1307,13 +1445,15 @@
         w_up=w_up,
         w_down=w_down,
         cotangent=cotangent,
-        small=small,
+        own_gain=own_gain,
+        lengths=lengths,
+        flow_steps=flow_steps,
     )
     given = dict(
         output=((frames, width), low),
         grad_joined=((ROWS, frames, joint), low),
         condition=((ROWS * 8, columns), low),
-        mod_grad=((RING, ROWS, 16, 256), full),
+        mod_grad=((RING, ROWS, 16, 256), low),
         gain_grad=((8, columns), full),
         down_whole=((RING, hidden_units // RING, width), low),
         up_whole=((RING, deep, hidden_units), low),
@@ -1327,14 +1467,17 @@
         upstream=((tokens, width), low),
         skip_held=(w_skip.shape, low),
         mod_held=(w_mod.shape, low),
-        out_held=(w_out.shape, low),
+        out_held=((width, width), low),
+        attended_all=((half, width), low),
         down_held=(w_down.shape, low),
         qkv_held=((width, 3 * columns), low),
         up_held=((width, hidden_units), low),
-        smalls=((ROWS,) + small.shape, full),
+        small=((7, 8, 128), full),
+        smalls=((ROWS, 7, 8, 128), full),
         mod_part=((ROWS * 8, 2 * width), full),
-        mod_land=((2, 16, 2 * width), full),
-        mod_send=((16, 2 * width), full),
+        mod_land=((1, 16, 2 * width), full),
+        mod_send=((16, 2 * width), low),
+        mod_cross=((16, 2 * width), low),
         gain=((8, width), full),
         cosine=((tokens, 128), full),
         sine=((tokens, 128), full),
@@ -1344,8 +1487,8 @@
         send_one=((half, width), low),
         send_two=((half, width), low),
         keep=((half, width), full),
-        land_one=((5, half, width), low),
-        land_two=((5, half, width), low),
+        land_one=((4, half, width), low),
+        land_two=((4, half, width), low),
         scale_one=((half, width), full),
         shift_one=((half, width), full),
         hidden=((half, width), full),
@@ -1377,10 +1520,9 @@
         project_send=((all_frames, 384), low),
         grad_project=((tokens, 3 * columns), low),
         grad_hidden=((tokens, width), low),
-        mod_terms=((frames, 2 * width), full),
         mod_sums=((16, 2 * width), full),
         sums_land=((RING, 16, 256), full),
-        sums_send=((16, 256), full),
+        sums_send=((16, 256), low),
         joined_send=((tokens, joint), low),
         down_total=((RING, hidden_units // RING, width), low),
         up_total=((RING, deep, hidden_units), low),
@@ -1400,10 +1542,14 @@
         joined_sem=(2, 3),
         small_sem=(2, 3),
         qkv_sem=(2, 3, 6),
+        qkv_pass_sem=(2, 2, 3),
         up_sem=(2, 3),
+        up_pass_sem=(2, 2),
+        out_sem=(2, 3),
+        attended_all_sem=(2, 3),
         mod_sem=(2, 2),
-        first_sem=(2, 5, 2),
-        second_sem=(2, 5, 2),
+        first_sem=(2, 4, 2),
+        second_sem=(2, 4, 2),
         upstream_sem=(2, 3),
         attn_sem=(2, 2),
         ff_sem=(2, 2),
@@ -1412,7 +1558,9 @@
         pair_sem=(2, RING),
         attended_sem=(2, RING),
         grad_pair_sem=(2, RING),
+        query_sem=(2, RING),
         project_sem=(2, RING),
+        value_sem=(2, RING),
         grad_joined_sem=(2, 3),
         sums_sem=(2, RING - 1),
         sums_group_sem=(2, 3),
@@ -1431,12 +1579,12 @@
     return pl.pallas_call(
         functools.partial(block_kernel, names),
         out_shape=[jax.ShapeDtypeStruct(*spec) for spec in given.values()],
-        in_specs=[vmem if name == "small" else anywhere for name in held],
+        in_specs=[anywhere] * 9 + [vmem] + [pl.BlockSpec(memory_space=pltpu.SMEM)] * 2,
         out_specs=[anywhere if name.endswith("_whole") else vmem for name in given],
         scratch_shapes=[pltpu.VMEM(*spec) for spec in buffers.values()]
         + [pltpu.SemaphoreType.DMA(shape) for shape in sems.values()],
         compiler_params=pltpu.CompilerParams(
-            collective_id=0, has_side_effects=True, vmem_limit_bytes=62 * 1024 * 1024
+            collective_id=0, has_side_effects=True, vmem_limit_bytes=63 * 1024 * 1024
         ),
     )(*held.values())
 
@@ -1479,11 +1627,9 @@
                 source = qkv_ref[0, rows, pl.ds((side * 3 + kind) * 128, 128)]
                 at = kind * (ROWS * 256) + r * 256 + side * 128
                 grad_qkv[:, pl.ds(at, 128)] = source.astype(full)
-    sums = jnp.concatenate([mod_ref[0, r, 0:8] for r in (0, 2, 1, 3)], axis=0)
-    high = sums.astype(jnp.bfloat16)
-    rest = (sums - high.astype(full)).astype(jnp.bfloat16)
-    grad_mod[...] = contract_rows(condition_ref[...], high) + contract_rows(
-        condition_ref[...], rest
+    sums = [mod_ref[0, r].astype(full)[0:8] for r in (0, 2, 1, 3)]
+    grad_mod[...] = contract_rows(
+        condition_ref[...], jnp.concatenate(sums, axis=0).astype(jnp.bfloat16)
     )
 
 
@@ -1535,33 +1681,6 @@
     )(joined, condition, mod, gain, down, up, qkv, skip, out)
 
 
-def small_table(lengths_row, steps_row, gain):
-    end = jnp.cumsum(lengths_row).astype(jnp.float32)
-    start = end - lengths_row.astype(jnp.float32)
-    count = end.shape[0]
-
-    def down(values):
-        return jnp.broadcast_to(values[:, None], (count, 128))
-
-    def along(values, empty):
-        rest = jnp.full((64 - 2 * count,), empty, jnp.float32)
-        lane = jnp.concatenate([values, values, rest, values, values, rest])
-        return jnp.broadcast_to(lane[None], (8, 128))
-
-    gain = gain.astype(jnp.float32)
-    return jnp.stack(
-        [
-            down(steps_row.astype(jnp.float32)),
-            down(start),
-            down(end),
-            along(start, 1e9),
-            along(end, 0.0),
-            jnp.broadcast_to(gain[None, :128], (8, 128)),
-            jnp.broadcast_to(gain[None, 128:], (8, 128)),
-        ]
-    )
-
-
 def per_device_block(
     inputs,
     skipped,
@@ -1576,12 +1695,20 @@
     lengths,
     flow_steps,
 ):
-    width = inputs.shape[2]
-    columns = width // ROWS
-    group_rank = lax.axis_index("grp")
-    small = small_table(lengths[0], flow_steps[0], ff_gain)
+    gain = jnp.broadcast_to(ff_gain.astype(jnp.float32)[None], (8, ff_gain.shape[0]))
     output, *rest = block_call(
-        inputs[0], skipped[0], w_skip, w_mod, w_qkv, w_out, w_up, w_down, cotangent[0], small
+        inputs[0],
+        skipped[0],
+        w_skip,
+        w_mod,
+        w_qkv,
+        w_out,
+        w_up,
+        w_down,
+        cotangent[0],
+        gain,
+        lengths,
+        flow_steps,
     )
     grad_inputs, grad_skipped, skip, mod, qkv, out, gain, up, down = finish_call(*rest)
     return (

time: 311 us -> 285 us (0.916)
  Pallas kernels: 305 us -> 282 us
    pallas_call x1, Pallas kernels: 294 us -> 272 us  [block_call(): pl.pallas_call(functools.partial(block_kernel, names), out_shape=[jax.Sha...]
where the time goes in v5:
time: 285 us
  Pallas kernels  282 us (99%)
    pallas_call x1, Pallas kernels, block_call(): pl.pallas_call(functools.partial(block_kernel, names), out_shape=[jax.Sha...  272 us
    pallas_call x1, Pallas kernels, finish_call(): pl.pallas_call(finish_kernel, grid=(RING,), out_shape=[shape for shape, _...  10.2 us

profile of v5, /device:TPU:0, one launch (start us, length us, event | category | flops | bytes accessed | tf_op | source)
XLA Modules:
  0.0 284.8 jit_solution(14217623412898178088)
XLA Ops:
  0.6 1.3 broadcast_in_dim.15.refs_9_
  1.9 271.9 %shard_map.195 = (bf16[128,1024]{1,0:T(8,128)(2,1)}, bf16[4,128,512]{2,1,0:T(8,128)(2,1)}, bf16[32,256]{1,0:T(8,128)(2,1)}, bf16[8,4,16,256]{3,2,1,0:T(8,128)(2,...) custom-call(bf16[128,1024]{1,0:T(8,128)(2,1)} %bitcast.7, ...), custom_call_target="tpu_custom_call" | custom-call | tf_op jit(solution)/shard_map/pallas_call | solution.py:1579
  273.8 0.0 copy-start
  273.8 10.2 %shard_map.196 = (f32[128,1024]{1,0:T(8,128)}, f32[128,1024]{1,0:T(8,128)}, f32[512,1024]{1,0:T(8,128)}, f32[256,2048]{1,0:T(8,128)}, f32[256,3072]{1,0:T(8,128)...) custom-call(bf16[4,128,512]{2,1,0:T(8,128)(2,1)} %get-tuple-element.30.joined_ref, ...), custom_call_target="tpu_custom_call" | custom-call | tf_op jit(solution)/shard_map/pallas_call | solution.py:1664
  284.1 0.0 copy-done
  284.1 0.7 copy.23
Async XLA Ops:
  273.8 10.2 %copy-start = (bf16[128,1024]{1,0:T(8,128)(2,1)S(1)}, bf16[128,1024]{1,0:T(8,128)(2,1)}, u32[]{:S(2)}) copy-start(bf16[128,1024]{1,0:T(8,128)(2,1)} %get-tuple-element.29) | copy-start | bytes 786436

commit v6 on v5

--- a/solution.py
+++ b/solution.py
@@ -381,7 +381,11 @@
     return (1 - upper) * (2 * place) + upper * (15 - 2 * place)
 
 
-TICKS = (1, 1, 0, 1, 0, 1, 0, 1, 1, 0, 1, 0, 1, 2, 1, 1, 1, 1, 0, 2, 1, 1, 2)
+TICKS = (2, 0, 0, 0, 0, 2, 0, 0, 0, 0, 2, 0, 0, 2, 0, 2, 4, 0, 0, 6, 3, 2, 2)
+
+TILE = 128
+UNROLLED = 4
+RING_TILE = 32
 
 
 class Ring:
@@ -422,7 +426,7 @@
             rows = self.rows(way)
             if step > 0:
                 self.copies[0, step - 1, way].wait_recv()
-                tile = min(self.half, 32)
+                tile = min(self.half, RING_TILE)
 
                 def add(i, carry, way=way, block=block, tile=tile):
                     at = pl.ds(pl.multiple_of(way * self.half + i * tile, tile), tile)
@@ -553,6 +557,11 @@
         return copy
 
     def tiles(count, tile, body):
+        if count // tile <= UNROLLED:
+            for i in range(count // tile):
+                body(i * tile)
+            return
+
         def step(i, carry):
             body(pl.multiple_of(i * tile, tile))
             return carry
@@ -713,12 +722,12 @@
             first[k].wait_recv()
 
             def add(at, k=k):
-                where = pl.ds(k * frames + at, 32)
+                where = pl.ds(k * frames + at, TILE)
                 total = n.keep[where] + n.land_one[index, where].astype(full)
                 n.keep[where] = total
                 n.send_two[where] = total.astype(low)
 
-            tiles(frames, 32, add)
+            tiles(frames, TILE, add)
             second.append(
                 push(
                     n.send_two.at[pl.ds(k * frames, frames)],
@@ -847,19 +856,19 @@
         second[k].wait_recv()
 
         def norm_one(at, k=k):
-            where = pl.ds(k * frames + at, 32)
+            where = pl.ds(k * frames + at, TILE)
             hidden = n.keep[where] + n.land_two[0, where].astype(full)
             n.hidden[where] = hidden
             centred = hidden - mean(hidden)
             spread = lax.rsqrt(mean(centred * centred) + EPSILON)
             normal = centred * spread
             n.normal_one[where] = normal
-            n.spread_one[where] = jnp.broadcast_to(spread, (32, 128))
-            n.attn_in[lines(mine + k * frames + at, 32)] = (
+            n.spread_one[where] = jnp.broadcast_to(spread, (TILE, 128))
+            n.attn_in[lines(mine + k * frames + at, TILE)] = (
                 normal * n.scale_one[where] + n.shift_one[where]
             ).astype(low)
 
-        tiles(frames, 32, norm_one)
+        tiles(frames, TILE, norm_one)
         attn_sends.append(share(n.attn_in, k, n.attn_sem))
 
     def part_of(reference, first):
@@ -921,11 +930,16 @@
                 def _():
                     target[lines(rank * frames, frames), columns_of] = send_buffer[to, :, columns_of]
 
-    def heads_arrive(target, sems, columns_of):
-        for other in range(1, RING):
+    def heads_arrive(target, sems, columns_of, then=None):
+        for other in range(RING):
             source = block(other)
-            where = target.at[lines(source * frames, frames), columns_of]
-            link(where, where, sems.at[0, source], sems.at[1, source], (source, group_rank)).wait_recv()
+            if other:
+                where = target.at[lines(source * frames, frames), columns_of]
+                link(
+                    where, where, sems.at[0, source], sems.at[1, source], (source, group_rank)
+                ).wait_recv()
+            if then is not None:
+                then(pl.multiple_of(source * frames, frames))
 
     def project_half(offset):
         def project_tile(at):
@@ -961,12 +975,6 @@
         n.chosen[pl.ds(at, frames)] = chosen.astype(low)
 
     tiles(RING * frames, frames, row_tables)
-    heads_arrive(n.paired, n.pair_sem, pl.ds(0, 256))
-    up_passed = pass_on(n.up_held, up_sends, n.up_pass_sem)
-    out_sends[0].wait_recv()
-    where = n.out_held.at[lines(across[1] * columns, columns)]
-    out_sends.append(push(where, where, n.out_sem, (2,), sibling))
-
     def masked_parts(at):
         where = pl.ds(at, frames)
         query, key = n.paired[where, 0:128], n.paired[where, 128:256]
@@ -980,9 +988,12 @@
         n.query_head[1, where] = jnp.where(first_head, chosen, scaled)
         n.key_head[0, where] = jnp.where(first_head, key, blocked)
         n.key_head[1, where] = jnp.where(first_head, blocked, key)
-        n.query_turned[:, where] = jnp.transpose(query.astype(full)).astype(low)
-
-    tiles(RING * frames, frames, masked_parts)
+
+    heads_arrive(n.paired, n.pair_sem, pl.ds(0, 256), masked_parts)
+    up_passed = pass_on(n.up_held, up_sends, n.up_pass_sem)
+    out_sends[0].wait_recv()
+    where = n.out_held.at[lines(across[1] * columns, columns)]
+    out_sends.append(push(where, where, n.out_sem, (2,), sibling))
     all_frames = RING * frames
     pair_place = (lines(slot_of(pair_row) * frames, frames), lines(pair_side * 128, 128))
 
@@ -1067,17 +1078,17 @@
     for k in range(2):
 
         def norm_two(at, k=k):
-            where = pl.ds(k * frames + at, 32)
+            where = pl.ds(k * frames + at, TILE)
             hidden = n.hidden[where] + n.keep[where]
             n.hidden[where] = hidden
             centred = hidden - mean(hidden)
             spread = lax.rsqrt(mean(centred * centred) + EPSILON)
             normal = centred * spread
             n.normal_two[where] = normal
-            n.spread_two[where] = jnp.broadcast_to(spread, (32, 128))
-            n.ff_in[lines(mine + k * frames + at, 32)] = (normal * n.gain[0:1]).astype(low)
-
-        tiles(frames, 32, norm_two)
+            n.spread_two[where] = jnp.broadcast_to(spread, (TILE, 128))
+            n.ff_in[lines(mine + k * frames + at, TILE)] = (normal * n.gain[0:1]).astype(low)
+
+        tiles(frames, TILE, norm_two)
         ff_sends.append(share(n.ff_in, k, n.ff_sem))
 
     up_load.wait()
@@ -1138,20 +1149,20 @@
         weight = (1 - jnp.abs(chip - k)).astype(full)
 
         def back_two(i, sums, k=k, weight=weight):
-            at = pl.multiple_of(i * 32, 32)
-            where = pl.ds(k * frames + at, 32)
+            at = pl.multiple_of(i * TILE, TILE)
+            where = pl.ds(k * frames + at, TILE)
             grad = n.keep[where] + n.land_two[1, where].astype(full)
             normal = n.normal_two[where]
             scaled = grad * n.gain[0:1]
             back = n.spread_two[where][:, 0:1] * (
                 scaled - mean(scaled) - normal * mean(scaled * normal)
             )
-            total = n.upstream[lines(mine + k * frames + at, 32)].astype(full) + back
+            total = n.upstream[lines(mine + k * frames + at, TILE)].astype(full) + back
             n.grad_two[where] = total
-            n.grad_two_low[lines(mine + k * frames + at, 32)] = total.astype(low)
+            n.grad_two_low[lines(mine + k * frames + at, TILE)] = total.astype(low)
             return sums + weight * jnp.sum(grad * normal, axis=0, keepdims=True)
 
-        gain_sums = lax.fori_loop(0, frames // 32, back_two, gain_sums)
+        gain_sums = lax.fori_loop(0, frames // TILE, back_two, gain_sums)
         grad_sends.append(share(n.grad_two_low, k, n.grad_two_sem))
         ticks(TICKS[1 + k])
     n.mod_sums[8:16] = jnp.zeros((8, 2 * width), full)
@@ -1178,7 +1189,6 @@
     value = contract_rows(n.attended[...], n.grad_two_low[...]).astype(low)
     for j in range(RING):
         n.out_total[j] = value[j * 32 : (j + 1) * 32]
-    begin(out_ring)
     ticks(TICKS[5])
 
     first = partial_sum(2, n.activated, lambda left, at: dot_plain(left, n.down_held[:, pl.ds(at, 256)]))
@@ -1186,13 +1196,17 @@
     output_second = cross_sum(2, first)
     ticks(TICKS[7])
 
-    heads_arrive(n.grad_pair, n.grad_pair_sem, pl.ds(0, 128))
+    def turn_queries(at):
+        where = pl.ds(at, frames)
+        n.query_turned[:, where] = jnp.transpose(n.paired[where, 0:128].astype(full)).astype(low)
+
+    tiles(RING * frames, frames, turn_queries)
 
     def turn_upstream(at):
         where = pl.ds(at, frames)
         n.grad_turned[:, where] = jnp.transpose(n.grad_pair[where].astype(full)).astype(low)
 
-    tiles(all_frames, frames, turn_upstream)
+    heads_arrive(n.grad_pair, n.grad_pair_sem, pl.ds(0, 128), turn_upstream)
     n.key_turned[...] = jnp.zeros(n.key_turned.shape, full)
     n.value_turned[...] = jnp.zeros(n.value_turned.shape, full)
 
@@ -1257,12 +1271,12 @@
         copy.wait_recv()
 
     def finish_output(at):
-        where = lines(chip * frames + at, 32)
-        n.output[pl.ds(at, 32)] = (
+        where = lines(chip * frames + at, TILE)
+        n.output[pl.ds(at, TILE)] = (
             n.hidden[where] + n.keep[where] + n.land_two[2, where].astype(full)
         ).astype(low)
 
-    tiles(frames, 32, finish_output)
+    tiles(frames, TILE, finish_output)
     ticks(TICKS[13])
     pairs_arrive(n.grad_project, n.query_sem, 384, 0, 128)
     pairs_arrive(n.grad_project, n.project_sem, 384, 128, 256)
@@ -1290,21 +1304,21 @@
         second[k].wait_recv()
 
         def back_one(at, k=k):
-            where = pl.ds(k * frames + at, 32)
+            where = pl.ds(k * frames + at, TILE)
             grad = n.keep[where] + n.land_two[3, where].astype(full)
             normal = n.normal_one[where]
             scaled = grad * n.scale_one[where]
             back = n.spread_one[where][:, 0:1] * (
                 scaled - mean(scaled) - normal * mean(scaled * normal)
             )
-            n.grad_hidden[lines(mine + k * frames + at, 32)] = (n.grad_two[where] + back).astype(low)
+            n.grad_hidden[lines(mine + k * frames + at, TILE)] = (n.grad_two[where] + back).astype(low)
 
             @pl.when(chip == k)
             def _():
-                n.shift_one[pl.ds(at, 32)] = grad * normal
-                n.shift_one[pl.ds(frames + at, 32)] = grad
-
-        tiles(frames, 32, back_one)
+                n.shift_one[pl.ds(at, TILE)] = grad * normal
+                n.shift_one[pl.ds(frames + at, TILE)] = grad
+
+        tiles(frames, TILE, back_one)
         hidden_sends.append(share(n.grad_hidden, k, n.grad_hidden_sem))
         ticks(TICKS[17 + k])
 
@@ -1318,6 +1332,7 @@
 
     tiles(n.joined.shape[1], 256, skip_weight_tile)
     begin(skip_ring)
+    begin(out_ring)
     ticks(TICKS[19])
     spot = (lax.broadcasted_iota(jnp.int32, (8, frames), 1) + rank * frames).astype(full)
     chosen = (spot >= n.small[1]) & (spot < n.small[2])
@@ -1584,7 +1599,9 @@
         scratch_shapes=[pltpu.VMEM(*spec) for spec in buffers.values()]
         + [pltpu.SemaphoreType.DMA(shape) for shape in sems.values()],
         compiler_params=pltpu.CompilerParams(
-            collective_id=0, has_side_effects=True, vmem_limit_bytes=63 * 1024 * 1024
+            collective_id=0,
+            has_side_effects=True,
+            vmem_limit_bytes=63 * 1024 * 1024,
         ),
     )(*held.values())
 

time: 285 us -> 274 us (0.961)
  Pallas kernels: 282 us -> 271 us
    pallas_call x1, Pallas kernels: 272 us -> 260 us  [block_call(): pl.pallas_call(functools.partial(block_kernel, names), out_shape=[jax.Sha...]
where the time goes in v6:
time: 274 us; the launch traced here: 273 us
  Pallas kernels  271 us (99%)
    pallas_call x1, Pallas kernels, block_call(): pl.pallas_call(functools.partial(block_kernel, names), out_shape=[jax.Sha...  260 us
    pallas_call x1, Pallas kernels, finish_call(): pl.pallas_call(finish_kernel, grid=(RING,), out_shape=[shape for shape, _...  10.2 us

profile of v6, /device:TPU:0, one launch (start us, length us, event | category | flops | bytes accessed | tf_op | source)
XLA Modules:
  0.0 273.3 jit_solution(11887099878960348464)
XLA Ops:
  0.6 1.3 broadcast_in_dim.15.refs_9_
  1.9 260.5 %shard_map.195 = (bf16[128,1024]{1,0:T(8,128)(2,1)}, bf16[4,128,512]{2,1,0:T(8,128)(2,1)}, bf16[32,256]{1,0:T(8,128)(2,1)}, bf16[8,4,16,256]{3,2,1,0:T(8,128)(2,...) custom-call(bf16[128,1024]{1,0:T(8,128)(2,1)} %bitcast.7, ...), custom_call_target="tpu_custom_call" | custom-call | tf_op jit(solution)/shard_map/pallas_call | solution.py:1594
  262.4 0.0 copy-start
  262.4 10.2 %shard_map.196 = (f32[128,1024]{1,0:T(8,128)}, f32[128,1024]{1,0:T(8,128)}, f32[512,1024]{1,0:T(8,128)}, f32[256,2048]{1,0:T(8,128)}, f32[256,3072]{1,0:T(8,128)...) custom-call(bf16[4,128,512]{2,1,0:T(8,128)(2,1)} %get-tuple-element.30.joined_ref, ...), custom_call_target="tpu_custom_call" | custom-call | tf_op jit(solution)/shard_map/pallas_call | solution.py:1681
  272.6 0.0 copy-done
  272.6 0.7 copy.23
Async XLA Ops:
  262.4 10.2 %copy-start = (bf16[128,1024]{1,0:T(8,128)(2,1)S(1)}, bf16[128,1024]{1,0:T(8,128)(2,1)}, u32[]{:S(2)}) copy-start(bf16[128,1024]{1,0:T(8,128)(2,1)} %get-tuple-element.29) | copy-start | bytes 786436

commit v7 on v6

--- a/solution.py
+++ b/solution.py
@@ -381,22 +381,23 @@
     return (1 - upper) * (2 * place) + upper * (15 - 2 * place)
 
 
-TICKS = (2, 0, 0, 0, 0, 2, 0, 0, 0, 0, 2, 0, 0, 2, 0, 2, 4, 0, 0, 6, 3, 2, 2)
+TICKS = (2, 0, 0, 0, 0, 2, 0, 0, 0, 0, 2, 0, 0, 2, 0, 2, 3, 0, 0, 6, 3, 2, 2)
 
 TILE = 128
 UNROLLED = 4
+MAIN_MIB = 55
+LAST_MIB = 24
 RING_TILE = 32
 
 
 class Ring:
-    def __init__(self, part, land, whole, sems, whole_sems, rank, group_rank, turn=None):
-        self.part, self.land, self.whole = part, land, whole
-        self.sems, self.whole_sems = sems, whole_sems
+    def __init__(self, part, land, sems, rank, group_rank, turn=None):
+        self.part, self.land, self.sems = part, land, sems
         self.rank, self.group_rank = rank, group_rank
         self.place = ring_place(rank)
         self.half = part.shape[1] // 2
         self.copies = {}
-        self.puts, self.turns, self.turn = [], [], turn
+        self.turns, self.turn = [], turn
 
     def block_at(self, offset):
         return ring_rank(lax.rem(self.place + offset + 2 * RING, RING))
@@ -440,14 +441,6 @@
             if step < RING - 1:
                 source = self.part.at[block, rows] if step == 0 else self.land.at[step - 1, rows]
                 self.send(0, step, way, source, self.land.at[step, rows])
-
-    def put(self, block, step, way):
-        rows = self.rows(way)
-        copy = pltpu.make_async_copy(
-            self.part.at[block, rows], self.whole.at[block, rows], self.whole_sems.at[way, step]
-        )
-        copy.start()
-        self.puts.append(copy)
 
     def spread_step(self, step):
         if step == 0:
@@ -460,7 +453,6 @@
             if step < RING - 1:
                 target = self.part.at[block, rows]
                 self.send(1, step, way, target, target)
-            self.put(block, step, way)
 
     def begin(self):
         self.sum_step(0)
@@ -501,8 +493,6 @@
         for (kind, step, _), copy in self.copies.items():
             if kind or step:
                 copy.wait_send()
-        for copy in self.puts:
-            copy.wait()
 
 
 def block_kernel(names, *refs):
@@ -620,8 +610,9 @@
         tables = (step_tile, start_tile, end_tile, start_lane, end_lane)
         for i, tile in enumerate(tables):
             n.small[i] = tile
-        n.small[5] = n.own_gain[:, 0:128]
-        n.small[6] = n.own_gain[:, 128:256]
+        gain = jnp.broadcast_to(n.own_gain[...].astype(full).reshape(1, columns), (8, columns))
+        n.small[5] = gain[:, 0:128]
+        n.small[6] = gain[:, 128:256]
 
     barrier = pltpu.get_barrier_semaphore()
     for other in range(1, ROWS):
@@ -743,15 +734,13 @@
     group_copies = {}
 
     down_ring, up_ring, out_ring, qkv_ring, skip_ring = rings = [
-        Ring(part, land, whole, sems, n.whole_sem.at[index], rank, group_rank, turn)
-        for index, (part, land, whole, sems, turn) in enumerate(
-            (
-                (n.down_total, n.down_land, n.down_whole, n.down_sem, None),
-                (n.up_total, n.up_land, n.up_whole, n.up_ring_sem, (n.up_turn, n.turn_sem.at[0])),
-                (n.out_total, n.out_land, n.out_whole, n.out_ring_sem, None),
-                (n.qkv_total, n.qkv_land, n.qkv_whole, n.qkv_ring_sem, (n.qkv_turn, n.turn_sem.at[1])),
-                (n.skip_total, n.skip_land, n.skip_whole, n.skip_ring_sem, None),
-            )
+        Ring(part, land, sems, rank, group_rank, turn)
+        for part, land, sems, turn in (
+            (n.down_total, n.down_land, n.down_sem, None),
+            (n.up_total, n.up_land, n.up_ring_sem, (n.up_turn, n.turn_sem.at[0])),
+            (n.out_total, n.out_land, n.out_ring_sem, None),
+            (n.qkv_total, n.qkv_land, n.qkv_ring_sem, (n.qkv_turn, n.turn_sem.at[1])),
+            (n.skip_total, n.skip_land, n.skip_ring_sem, None),
         )
     ]
     running = []
@@ -1470,11 +1459,11 @@
         condition=((ROWS * 8, columns), low),
         mod_grad=((RING, ROWS, 16, 256), low),
         gain_grad=((8, columns), full),
-        down_whole=((RING, hidden_units // RING, width), low),
-        up_whole=((RING, deep, hidden_units), low),
-        qkv_whole=((RING, deep, 3 * columns), low),
-        skip_whole=((RING, joint // RING, width), low),
-        out_whole=((RING, columns // RING, width), low),
+        down_total=((RING, hidden_units // RING, width), low),
+        up_total=((RING, deep, hidden_units), low),
+        qkv_total=((RING, deep, 3 * columns), low),
+        skip_total=((RING, joint // RING, width), low),
+        out_total=((RING, columns // RING, width), low),
     )
     buffers = dict(
         joined_own=((ROWS, frames, joint), low),
@@ -1539,11 +1528,6 @@
         sums_land=((RING, 16, 256), full),
         sums_send=((16, 256), low),
         joined_send=((tokens, joint), low),
-        down_total=((RING, hidden_units // RING, width), low),
-        up_total=((RING, deep, hidden_units), low),
-        qkv_total=((RING, deep, 3 * columns), low),
-        skip_total=((RING, joint // RING, width), low),
-        out_total=((RING, columns // RING, width), low),
         down_land=((RING - 1, hidden_units // RING, width), low),
         up_land=((RING - 1, deep, hidden_units), low),
         qkv_land=((RING - 1, deep, 3 * columns), low),
@@ -1586,116 +1570,136 @@
         skip_ring_sem=(2, 2, 2, RING - 1),
         out_ring_sem=(2, 2, 2, RING - 1),
         turn_sem=(2, 2, 3),
-        whole_sem=(5, 2, RING),
     )
     names = [*held, *given, *buffers, *sems]
     vmem = pl.BlockSpec(memory_space=pltpu.VMEM)
     anywhere = pl.BlockSpec(memory_space=pl.ANY)
     return pl.pallas_call(
         functools.partial(block_kernel, names),
-        out_shape=[jax.ShapeDtypeStruct(*spec) for spec in given.values()],
+        out_shape=[pltpu.VMEM(*spec) for spec in given.values()],
         in_specs=[anywhere] * 9 + [vmem] + [pl.BlockSpec(memory_space=pltpu.SMEM)] * 2,
-        out_specs=[anywhere if name.endswith("_whole") else vmem for name in given],
+        out_specs=[vmem] * len(given),
         scratch_shapes=[pltpu.VMEM(*spec) for spec in buffers.values()]
         + [pltpu.SemaphoreType.DMA(shape) for shape in sems.values()],
         compiler_params=pltpu.CompilerParams(
             collective_id=0,
             has_side_effects=True,
-            vmem_limit_bytes=63 * 1024 * 1024,
+            vmem_limit_bytes=MAIN_MIB * 1024 * 1024,
         ),
     )(*held.values())
 
 
-def finish_kernel(
-    joined_ref,
-    condition_ref,
-    mod_ref,
-    gain_ref,
-    down_ref,
-    up_ref,
-    qkv_ref,
-    skip_ref,
-    out_ref,
-    grad_inputs,
-    grad_skipped,
-    grad_skip,
-    grad_mod,
-    grad_qkv,
-    grad_out,
-    grad_gain,
-    grad_up,
-    grad_down,
-):
+def finish_kernel(names, *refs):
+    n = types.SimpleNamespace(**dict(zip(names, refs)))
     full = jnp.float32
-    wide = joined_ref.shape[2]
+    pieces = 4
+    chunks = RING // pieces
+
+    def start(source, target, sem):
+        copy = pltpu.make_async_copy(source, target, sem)
+        copy.start()
+        return copy
+
+    def widen_rows(source, target, p):
+        deep, wide = source.shape[1:]
+        target[pl.ds(p * chunks * deep, chunks * deep)] = (
+            source[pl.ds(p * chunks, chunks)].astype(full).reshape(chunks * deep, wide)
+        )
+
+    def widen_columns(source, target, p):
+        deep, wide = source.shape[1] // ROWS, source.shape[2]
+        kinds = wide // 256 if wide % 1024 else 1
+        step = 128 if kinds > 1 else wide
+        for j in range(chunks):
+            to = pl.ds((p * chunks + j) * deep, deep)
+            for r in range(ROWS):
+                value = source[p * chunks + j, pl.ds(r * deep, deep)].astype(full)
+                for i in range(wide // step):
+                    side, kind = i // kinds, i % kinds
+                    at = kind * (ROWS * wide // kinds) + r * (wide // kinds) + side * step
+                    target[to, pl.ds(at, step)] = value[:, i * step : (i + 1) * step]
+
+    work = (
+        (n.down, n.down_out, n.grad_down, widen_rows),
+        (n.up, n.up_out, n.grad_up, widen_columns),
+        (n.qkv, n.qkv_out, n.grad_qkv, widen_columns),
+        (n.skip, n.skip_out, n.grad_skip, widen_rows),
+        (n.out, n.out_out, n.grad_out, widen_rows),
+    )
+    sent = [start(n.output, n.output_back, n.small_sem.at[3])]
+    for p in range(pieces):
+        for i, (held, wide, target, widen) in enumerate(work):
+            widen(held, wide, p)
+            deep = target.shape[0] // pieces
+            rows = pl.ds(p * deep, deep)
+            sent.append(start(wide.at[rows], target.at[rows], n.out_sem.at[i, p]))
+    for i in range(RING):
+        sums = [n.mod[i, r].astype(full)[0:8] for r in (0, 2, 1, 3)]
+        n.mod_out[:, pl.ds(i * 256, 256)] = contract_rows(
+            n.condition[...], jnp.concatenate(sums, axis=0).astype(jnp.bfloat16)
+        )
+    sent.append(start(n.mod_out, n.grad_mod, n.small_sem.at[4]))
+    wide = n.joined.shape[2]
     for r in range(ROWS):
-        target = (grad_inputs, grad_skipped)[r // 2]
-        target[:, pl.ds((r % 2) * wide, wide)] = joined_ref[r].astype(full)
-    grad_down[...] = down_ref[0].astype(full)
-    grad_skip[...] = skip_ref[0].astype(full)
-    grad_out[...] = out_ref[0].astype(full)
-    grad_gain[...] = gain_ref[0:1]
-    deep, wide = up_ref.shape[1] // ROWS, up_ref.shape[2]
-    for r in range(ROWS):
-        rows = pl.ds(r * deep, deep)
-        grad_up[:, pl.ds(r * wide, wide)] = up_ref[0, rows].astype(full)
-        for side in range(2):
-            for kind in range(3):
-                source = qkv_ref[0, rows, pl.ds((side * 3 + kind) * 128, 128)]
-                at = kind * (ROWS * 256) + r * 256 + side * 128
-                grad_qkv[:, pl.ds(at, 128)] = source.astype(full)
-    sums = [mod_ref[0, r].astype(full)[0:8] for r in (0, 2, 1, 3)]
-    grad_mod[...] = contract_rows(
-        condition_ref[...], jnp.concatenate(sums, axis=0).astype(jnp.bfloat16)
-    )
-
-
-def finish_call(joined, condition, mod, gain, down, up, qkv, skip, out):
-    full = jnp.float32
+        n.joined_out[r // 2, :, pl.ds((r % 2) * wide, wide)] = n.joined[r].astype(full)
+    sent.append(start(n.joined_out.at[0], n.grad_inputs, n.small_sem.at[5]))
+    sent.append(start(n.joined_out.at[1], n.grad_skipped, n.small_sem.at[6]))
+    n.grad_gain[...] = n.gain[0:1]
+    for copy in sent:
+        copy.wait()
+
+
+def finish_call(output, joined, condition, mod, gain, down, up, qkv, skip, out):
+    low, full = jnp.bfloat16, jnp.float32
     frames, wide = joined.shape[1:]
     columns = condition.shape[1]
-
-    def first(shape):
-        return pl.BlockSpec((1,) + shape[1:], lambda i: (i,) + (0,) * (len(shape) - 1))
-
-    def rows(count, width):
-        return jax.ShapeDtypeStruct((count, width), full), pl.BlockSpec(
-            (count // RING, width), lambda i: (i, 0)
-        )
-
     deep = up.shape[1] // ROWS
-    results = [
-        rows(frames, 2 * wide),
-        rows(frames, 2 * wide),
-        rows(RING * skip.shape[1], skip.shape[2]),
-        (
-            jax.ShapeDtypeStruct((columns, RING * mod.shape[3]), full),
-            pl.BlockSpec((columns, mod.shape[3]), lambda i: (0, i)),
-        ),
-        rows(RING * deep, ROWS * qkv.shape[2]),
-        rows(RING * out.shape[1], out.shape[2]),
-        (jax.ShapeDtypeStruct((1, columns), full), pl.BlockSpec((1, columns), lambda i: (0, 0))),
-        rows(RING * deep, ROWS * up.shape[2]),
-        rows(RING * down.shape[1], down.shape[2]),
-    ]
+    held = dict(
+        output=output,
+        joined=joined,
+        condition=condition,
+        mod=mod,
+        gain=gain,
+        down=down,
+        up=up,
+        qkv=qkv,
+        skip=skip,
+        out=out,
+    )
+    given = dict(
+        output_back=(output.shape, low),
+        grad_inputs=((frames, 2 * wide), full),
+        grad_skipped=((frames, 2 * wide), full),
+        grad_skip=((RING * skip.shape[1], skip.shape[2]), full),
+        grad_mod=((columns, RING * mod.shape[3]), full),
+        grad_qkv=((RING * deep, ROWS * qkv.shape[2]), full),
+        grad_out=((RING * out.shape[1], out.shape[2]), full),
+        grad_gain=((1, columns), full),
+        grad_up=((RING * deep, ROWS * up.shape[2]), full),
+        grad_down=((RING * down.shape[1], down.shape[2]), full),
+    )
+    buffers = dict(
+        joined_out=((2, frames, 2 * wide), full),
+        mod_out=given["grad_mod"],
+        down_out=given["grad_down"],
+        up_out=given["grad_up"],
+        qkv_out=given["grad_qkv"],
+        skip_out=given["grad_skip"],
+        out_out=given["grad_out"],
+    )
+    sems = dict(out_sem=(5, 4), small_sem=(7,))
+    names = [*held, *given, *buffers, *sems]
+    vmem = pl.BlockSpec(memory_space=pltpu.VMEM)
+    anywhere = pl.BlockSpec(memory_space=pl.ANY)
     return pl.pallas_call(
-        finish_kernel,
-        grid=(RING,),
-        out_shape=[shape for shape, _ in results],
-        in_specs=[
-            pl.BlockSpec((ROWS, frames // RING, wide), lambda i: (0, i, 0)),
-            pl.BlockSpec(condition.shape, lambda i: (0, 0)),
-            first(mod.shape),
-            pl.BlockSpec(gain.shape, lambda i: (0, 0)),
-            first(down.shape),
-            first(up.shape),
-            first(qkv.shape),
-            first(skip.shape),
-            first(out.shape),
-        ],
-        out_specs=[spec for _, spec in results],
-        compiler_params=pltpu.CompilerParams(vmem_limit_bytes=62 * 1024 * 1024),
-    )(joined, condition, mod, gain, down, up, qkv, skip, out)
+        functools.partial(finish_kernel, names),
+        out_shape=[jax.ShapeDtypeStruct(*spec) for spec in given.values()],
+        in_specs=[vmem] * len(held),
+        out_specs=[vmem if name == "grad_gain" else anywhere for name in given],
+        scratch_shapes=[pltpu.VMEM(*spec) for spec in buffers.values()]
+        + [pltpu.SemaphoreType.DMA(shape) for shape in sems.values()],
+        compiler_params=pltpu.CompilerParams(vmem_limit_bytes=LAST_MIB * 1024 * 1024),
+    )(*held.values())
 
 
 def per_device_block(
@@ -1712,8 +1716,7 @@
     lengths,
     flow_steps,
 ):
-    gain = jnp.broadcast_to(ff_gain.astype(jnp.float32)[None], (8, ff_gain.shape[0]))
-    output, *rest = block_call(
+    finished = block_call(
         inputs[0],
         skipped[0],
         w_skip,
@@ -1723,11 +1726,11 @@
         w_up,
         w_down,
         cotangent[0],
-        gain,
+        ff_gain,
         lengths,
         flow_steps,
     )
-    grad_inputs, grad_skipped, skip, mod, qkv, out, gain, up, down = finish_call(*rest)
+    output, grad_inputs, grad_skipped, skip, mod, qkv, out, gain, up, down = finish_call(*finished)
     return (
         output[None],
         grad_inputs[None],

time: 274 us -> 267 us (0.974)
  Pallas kernels: 271 us -> 266 us
    pallas_call x2, Pallas kernels: 271 us -> 266 us  [the longest x1 258 us: block_call(): pl.pallas_call(functools.partial(block_kernel, names), out_shape=[pltpu.V...]
where the time goes in v7:
time: 267 us
  Pallas kernels  266 us (100%)
    pallas_call x1, Pallas kernels, block_call(): pl.pallas_call(functools.partial(block_kernel, names), out_shape=[pltpu.V...  258 us
    pallas_call x1, Pallas kernels, finish_call(): pl.pallas_call(functools.partial(finish_kernel, names), out_shape=[jax.Sh...  7.48 us

profile of v7, /device:TPU:0, one launch (start us, length us, event | category | flops | bytes accessed | tf_op | source)
XLA Modules:
  0.0 266.5 jit_solution(16946108946092915966)
XLA Ops:
  0.6 258.2 %shard_map.195 = (bf16[128,1024]{1,0:T(8,128)(2,1)S(1)}, bf16[4,128,512]{2,1,0:T(8,128)(2,1)S(1)}, bf16[32,256]{1,0:T(8,128)(2,1)S(1)}, bf16[8,4,16,256]{3,2,1,0...) custom-call(bf16[128,1024]{1,0:T(8,128)(2,1)} %bitcast.7, ...), custom_call_target="tpu_custom_call" | custom-call | tf_op jit(solution)/shard_map/pallas_call | solution.py:1577
  258.9 7.5 %shard_map.196 = (bf16[128,1024]{1,0:T(8,128)(2,1)}, f32[128,1024]{1,0:T(8,128)}, f32[128,1024]{1,0:T(8,128)}, f32[512,1024]{1,0:T(8,128)}, f32[256,2048]{1,0:T(...) custom-call(bf16[128,1024]{1,0:T(8,128)(2,1)S(1)} %get-tuple-element, ...), custom_call_target="tpu_custom_call" | custom-call | tf_op jit(solution)/shard_map/pallas_call | solution.py:1694

commit v8 on v7

--- a/solution.py
+++ b/solution.py
@@ -381,7 +381,7 @@
     return (1 - upper) * (2 * place) + upper * (15 - 2 * place)
 
 
-TICKS = (2, 0, 0, 0, 0, 2, 0, 0, 0, 0, 2, 0, 0, 2, 0, 2, 3, 0, 0, 6, 3, 2, 2)
+TICKS = (2, 0, 0, 0, 0, 2, 0, 0, 0, 0, 2, 0, 0, 2, 0, 2, 3, 0, 0, 10, 5, 5, 5)
 
 TILE = 128
 UNROLLED = 4
@@ -625,9 +625,10 @@
     pl.semaphore_wait(barrier, ROWS + RING - 2)
 
     joined_place = n.joined.at[lines(own_slot * frames, frames)]
+    over_x = (group_rank + 2 - 4 * chip, 2 * (1 - chip) + 1 - core)
     joined_sends = [
-        push(n.joined_own.at[group(o)], joined_place, n.joined_sem, (o - 1,), (rank, group(o)))
-        for o in (2, 1, 3)
+        push(n.joined_own.at[to], joined_place, n.joined_sem, (i,), (rank, to))
+        for i, to in enumerate((*over_x, sibling[1]))
     ]
     small_sends = [
         push(n.small, n.smalls.at[group_rank], n.small_sem, (o - 1,), (rank, group(o)))
@@ -635,6 +636,22 @@
     ]
     n.joined[lines(own_slot * frames, frames)] = n.joined_own[group_rank]
     n.smalls[group_rank] = n.small[...]
+    def skip_rows(k):
+        own_rows, their_rows = lines(mine + k * frames, frames), lines(theirs + k * frames, frames)
+        rows = lines(k * frames, frames)
+        n.send_one[rows] = dot_plain(n.joined[their_rows], n.skip_held[...]).astype(low)
+        copy = push(n.send_one.at[rows], n.land_one.at[0, rows], n.first_sem, (0, k), sibling)
+        kept = dot_plain(n.joined[own_rows], n.skip_held[...])
+        copy.wait_recv()
+        kept = kept + n.land_one[0, rows].astype(full)
+        n.keep[rows] = kept
+        n.send_two[rows] = kept.astype(low)
+        return copy, push(n.send_two.at[rows], n.land_two.at[0, rows], n.second_sem, (0, k), across)
+
+    skip_load.wait()
+    joined_sends[2].wait_recv()
+    skip_sums = [skip_rows(chip)]
+
     for copy in small_sends:
         copy.wait_recv()
 
@@ -760,13 +777,9 @@
     def mean(value):
         return jnp.mean(value, axis=-1, keepdims=True)
 
-    def share(buffer, k, sems):
+    def share(buffer, k, sems, step=None):
         where = lines(mine + k * frames, frames)
-        return push(buffer.at[where], buffer.at[where], sems, (k,), sibling)
-
-    skip_load.wait()
-    for copy in joined_sends:
-        copy.wait_recv()
+        return push(buffer.at[where], buffer.at[where], sems, (k if step is None else step,), sibling)
 
     side_y, side_z = lax.rem(rank, 2), lax.rem(rank // 2, 2)
     to_y, to_z = 1 - 2 * side_y, 2 - 4 * side_z
@@ -775,7 +788,6 @@
     part_rows = columns // 2
     few_rows = columns // 4
     first_row = (2 * side_z + side_y) * few_rows
-    over_x = (group_rank + 2 - 4 * chip, 2 * (1 - chip) + 1 - core)
     qkv_sends = [
         [
             push(
@@ -802,15 +814,14 @@
         ]
     )
 
-    def skip_tile(left, at):
-        return dot_plain(left, n.skip_held[:, pl.ds(at, 256)])
-
-    first = partial_sum(0, n.joined, skip_tile)
     mod_first.wait_recv()
     mod_mine = n.mod_part[pl.ds(pl.multiple_of(16 * core, 16), 16)] + n.mod_land[0]
     n.mod_send[...] = mod_mine.astype(low)
     mod_second = push(n.mod_send, n.mod_cross, n.mod_sem, (1,), across)
-    second = cross_sum(0, first)
+    for copy in joined_sends[:2]:
+        copy.wait_recv()
+    skip_sums.append(skip_rows(1 - chip))
+    group_copies[0] = tuple(zip(*skip_sums))
     own_lines = lines(own_slot * frames, frames)
     for slot in range(ROWS):
         turn_tables(
@@ -841,11 +852,19 @@
         for j, to in enumerate(around):
             qkv_passed.append(push(where, where, n.qkv_pass_sem, (i, j), to))
     attn_sends = []
-    for k in range(2):
-        second[k].wait_recv()
+    for step in range(2):
+        k = chip if step else 1 - chip
+        skip_rows_here = lines(k * frames, frames)
+        link(
+            n.send_two.at[skip_rows_here],
+            n.land_two.at[0, skip_rows_here],
+            n.second_sem.at[0, 0, k],
+            n.second_sem.at[1, 0, k],
+            across,
+        ).wait_recv()
 
         def norm_one(at, k=k):
-            where = pl.ds(k * frames + at, TILE)
+            where = lines(k * frames + at, TILE)
             hidden = n.keep[where] + n.land_two[0, where].astype(full)
             n.hidden[where] = hidden
             centred = hidden - mean(hidden)
@@ -858,7 +877,7 @@
             ).astype(low)
 
         tiles(frames, TILE, norm_one)
-        attn_sends.append(share(n.attn_in, k, n.attn_sem))
+        attn_sends.append(share(n.attn_in, k, n.attn_sem, step))
 
     def part_of(reference, first):
         return reference.at[lines(first + side_y * part_rows, part_rows)]

time: 267 us -> 264 us (0.989)
  Pallas kernels: 266 us -> 263 us
    pallas_call x1, Pallas kernels: 258 us -> 255 us  [block_call(): pl.pallas_call(functools.partial(block_kernel, names), out_shape=[pltpu.V...]
where the time goes in v8:
time: 264 us; the launch traced here: 263 us
  Pallas kernels  263 us (100%)
    pallas_call x1, Pallas kernels, block_call(): pl.pallas_call(functools.partial(block_kernel, names), out_shape=[pltpu.V...  255 us
    pallas_call x1, Pallas kernels, finish_call(): pl.pallas_call(functools.partial(finish_kernel, names), out_shape=[jax.Sh...  7.47 us

profile of v8, /device:TPU:0, one launch (start us, length us, event | category | flops | bytes accessed | tf_op | source)
XLA Modules:
  0.0 263.5 jit_solution(5137712501157207931)
XLA Ops:
  0.6 255.2 %shard_map.195 = (bf16[128,1024]{1,0:T(8,128)(2,1)S(1)}, bf16[4,128,512]{2,1,0:T(8,128)(2,1)S(1)}, bf16[32,256]{1,0:T(8,128)(2,1)S(1)}, bf16[8,4,16,256]{3,2,1,0...) custom-call(bf16[128,1024]{1,0:T(8,128)(2,1)} %bitcast.7, ...), custom_call_target="tpu_custom_call" | custom-call | tf_op jit(solution)/shard_map/pallas_call | solution.py:1596
  255.8 7.5 %shard_map.196 = (bf16[128,1024]{1,0:T(8,128)(2,1)}, f32[128,1024]{1,0:T(8,128)}, f32[128,1024]{1,0:T(8,128)}, f32[512,1024]{1,0:T(8,128)}, f32[256,2048]{1,0:T(...) custom-call(bf16[128,1024]{1,0:T(8,128)(2,1)S(1)} %get-tuple-element, ...), custom_call_target="tpu_custom_call" | custom-call | tf_op jit(solution)/shard_map/pallas_call | solution.py:1713

commit v9 on v8

--- a/solution.py
+++ b/solution.py
@@ -381,7 +381,7 @@
     return (1 - upper) * (2 * place) + upper * (15 - 2 * place)
 
 
-TICKS = (2, 0, 0, 0, 0, 2, 0, 0, 0, 0, 2, 0, 0, 2, 0, 2, 3, 0, 0, 10, 5, 5, 5)
+TICKS = (2, 0, 0, 0, 0, 2, 3, 0, 0, 0, 2, 0, 0, 2, 3, 2, 3, 0, 0, 8, 5, 5, 5)
 
 TILE = 128
 UNROLLED = 4
@@ -1199,9 +1199,6 @@
         n.out_total[j] = value[j * 32 : (j + 1) * 32]
     ticks(TICKS[5])
 
-    first = partial_sum(2, n.activated, lambda left, at: dot_plain(left, n.down_held[:, pl.ds(at, 256)]))
-    ticks(TICKS[6])
-    output_second = cross_sum(2, first)
     ticks(TICKS[7])
 
     def turn_queries(at):
@@ -1275,25 +1272,14 @@
 
     ticks(TICKS[12])
 
-    for copy in output_second:
-        copy.wait_recv()
-
-    def finish_output(at):
-        where = lines(chip * frames + at, TILE)
-        n.output[pl.ds(at, TILE)] = (
-            n.hidden[where] + n.keep[where] + n.land_two[2, where].astype(full)
-        ).astype(low)
-
-    tiles(frames, TILE, finish_output)
     ticks(TICKS[13])
     pairs_arrive(n.grad_project, n.query_sem, 384, 0, 128)
     pairs_arrive(n.grad_project, n.project_sem, 384, 128, 256)
 
     first = partial_sum(
-        3, n.grad_project, lambda left, at: dot_across(left, n.qkv_held[pl.ds(at, 256)])
-    )
-    ticks(TICKS[14])
-    second = cross_sum(3, first)
+        2, n.grad_project, lambda left, at: dot_across(left, n.qkv_held[pl.ds(at, 256)])
+    )
+    second = cross_sum(2, first)
     ticks(TICKS[15])
 
     def qkv_tile(at):
@@ -1313,7 +1299,7 @@
 
         def back_one(at, k=k):
             where = pl.ds(k * frames + at, TILE)
-            grad = n.keep[where] + n.land_two[3, where].astype(full)
+            grad = n.keep[where] + n.land_two[2, where].astype(full)
             normal = n.normal_one[where]
             scaled = grad * n.scale_one[where]
             back = n.spread_one[where][:, 0:1] * (
@@ -1342,6 +1328,13 @@
     begin(skip_ring)
     begin(out_ring)
     ticks(TICKS[19])
+
+    first = partial_sum(
+        3, n.activated, lambda left, at: dot_plain(left, n.down_held[:, pl.ds(at, 256)])
+    )
+    ticks(TICKS[6])
+    output_second = cross_sum(3, first)
+    ticks(TICKS[14])
     spot = (lax.broadcasted_iota(jnp.int32, (8, frames), 1) + rank * frames).astype(full)
     chosen = (spot >= n.small[1]) & (spot < n.small[2])
     picker = jnp.where(chosen, 1.0, 0.0)
@@ -1409,6 +1402,16 @@
         for other in range(1, RING)
     ]
 
+    for copy in output_second:
+        copy.wait_recv()
+
+    def finish_output(at):
+        where = lines(chip * frames + at, TILE)
+        n.output[pl.ds(at, TILE)] = (
+            n.hidden[where] + n.keep[where] + n.land_two[3, where].astype(full)
+        ).astype(low)
+
+    tiles(frames, TILE, finish_output)
     ticks(5 * (2 * RING + 1))
     for ring in rings:
         ring.finish()

time: 264 us -> 264 us (level)
  no operation moved by 1% of the time
where the time goes in v9:
time: 264 us
  Pallas kernels  263 us (100%)
    pallas_call x1, Pallas kernels, block_call(): pl.pallas_call(functools.partial(block_kernel, names), out_shape=[pltpu.V...  255 us
    pallas_call x1, Pallas kernels, finish_call(): pl.pallas_call(functools.partial(finish_kernel, names), out_shape=[jax.Sh...  7.48 us

profile of v9, /device:TPU:0, one launch (start us, length us, event | category | flops | bytes accessed | tf_op | source)
XLA Modules:
  0.0 263.5 jit_solution(11421661151656047054)
XLA Ops:
  0.6 255.2 %shard_map.195 = (bf16[128,1024]{1,0:T(8,128)(2,1)S(1)}, bf16[4,128,512]{2,1,0:T(8,128)(2,1)S(1)}, bf16[32,256]{1,0:T(8,128)(2,1)S(1)}, bf16[8,4,16,256]{3,2,1,0...) custom-call(bf16[128,1024]{1,0:T(8,128)(2,1)} %bitcast.7, ...), custom_call_target="tpu_custom_call" | custom-call | tf_op jit(solution)/shard_map/pallas_call | solution.py:1599
  255.9 7.5 %shard_map.196 = (bf16[128,1024]{1,0:T(8,128)(2,1)}, f32[128,1024]{1,0:T(8,128)}, f32[128,1024]{1,0:T(8,128)}, f32[512,1024]{1,0:T(8,128)}, f32[256,2048]{1,0:T(...) custom-call(bf16[128,1024]{1,0:T(8,128)(2,1)S(1)} %get-tuple-element, ...), custom_call_target="tpu_custom_call" | custom-call | tf_op jit(solution)/shard_map/pallas_call | solution.py:1716
